TPU v7x, 128 devices: a whole 4x4x4 slice. The times are simulated.
128 devices in a mesh: gx: 16 (over x_lo, y, core), gy: 8 (over x_hi, z).
Axes of the slice: x: 4 (x_hi: 2, x_lo: 2; x = x_hi * 2 + x_lo), y: 4, z: 4, core: 2. Of those that a mesh axis runs over, the one named last changes fastest.
Arguments:
- e_field: float32 [3, 3, 4096, 4096], P(None, None, 'gx', 'gy'), may hold values from -6 to 6
- h_field: float32 [3, 3, 4096, 4096], P(None, None, 'gx', 'gy'), may hold values from -6 to 6
- material: int32 [3, 4096, 4096], P(None, 'gx', 'gy'), may hold values from 0 to 7
- eps_table: float32 [8], replicated, may hold values from 1 to 12
- src_pos: int32 [4096, 3], replicated, may hold values from 0 to 4095, as said below
- src_amp: float32 [4096], replicated, may hold values from -40 to 40
- freqs: float32 [2], replicated, may hold values from 0.3 to 2.8
Outputs:
- e_out: float32 [3, 3, 4096, 4096], P(None, None, 'gx', 'gy')
- h_out: float32 [3, 3, 4096, 4096], P(None, None, 'gx', 'gy')
- far_field: float32 [1024, 8, 2, 1024], P('gx', None, None, 'gy')
Inputs may be any that keep to these rules, and one draw needn't show every extreme that they name: `src_pos`: each row is a cell (layer, row, column) of the slab; several sources may share a cell.
All inputs are finite; a program needn't handle non-finite values.
Results may differ from a plain program's by a relative error of at most 0.0054.
Values may be sent and summed in bfloat16 or wider, within the bound.
No kernel may reach another device: no remote copies, remote signals or barrier semaphores. Data moves between devices by JAX's collectives and lax.ppermute only.
A program may use at most 192 MiB of HBM per device.

v0:
```python
import math

import jax
import jax.numpy as jnp
from jax import lax
from jax.sharding import PartitionSpec as P

LZ = 3
FACE = 1
STEPS = 2
NF = 2
NA = 1024
NMAT = 8


courant = 0.5
source_rate = 0.7
zoom_factor = 4


def shifted(block, axis, distance):
    devices = range(lax.axis_size(axis))
    route = [(i - distance, i) for i in devices if i - distance in devices]
    return lax.ppermute(block, axis, route)


def chirp(freq_index, cell_index, period):
    remainder = jnp.remainder(freq_index * cell_index, period)
    phase_angle = remainder.astype(jnp.float32) * (2.0 * math.pi / period)
    return (jnp.cos(phase_angle), -jnp.sin(phase_angle))


def forward(field, dimension, boundary):
    inner = lax.slice_in_dim(field, 1, field.shape[dimension], axis=dimension)
    return jnp.concatenate([inner, jnp.expand_dims(boundary, dimension)], dimension)


def backward(field, dimension, boundary):
    inner = lax.slice_in_dim(field, 0, field.shape[dimension] - 1, axis=dimension)
    return jnp.concatenate([jnp.expand_dims(boundary, dimension), inner], dimension)


def curl_forward(electric, row_rim, col_rim):
    field_x, field_y, field_z = (electric[0], electric[1], electric[2])
    zero_layer = jnp.zeros(field_x.shape[1:], jnp.float32)
    curl_x = forward(field_z, 2, col_rim[1]) - field_z - (forward(field_y, 0, zero_layer) - field_y)
    curl_y = forward(field_x, 0, zero_layer) - field_x - (forward(field_z, 1, row_rim[1]) - field_z)
    curl_z = forward(field_y, 1, row_rim[0]) - field_y - (forward(field_x, 2, col_rim[0]) - field_x)
    return jnp.stack([curl_x, curl_y, curl_z])


def curl_backward(magnetic, row_rim, col_rim):
    field_x, field_y, field_z = (magnetic[0], magnetic[1], magnetic[2])
    zero_layer = jnp.zeros(field_x.shape[1:], jnp.float32)
    curl_x = (
        field_z - backward(field_z, 2, col_rim[1]) - (field_y - backward(field_y, 0, zero_layer))
    )
    curl_y = (
        field_x - backward(field_x, 0, zero_layer) - (field_z - backward(field_z, 1, row_rim[1]))
    )
    curl_z = (
        field_y - backward(field_y, 1, row_rim[0]) - (field_x - backward(field_x, 2, col_rim[0]))
    )
    return jnp.stack([curl_x, curl_y, curl_z])


def complex_pair(product_re_re, product_re_im, product_im_re, product_im_im):
    return (product_re_re - product_im_im, product_re_im + product_im_re)


def on_device(e_field, h_field, material, eps_table, src_pos, src_amp, freqs):
    row_count = e_field.shape[2]
    col_count = e_field.shape[3]
    grid_rows = row_count * lax.axis_size("gx")
    grid_cols = col_count * lax.axis_size("gy")
    row_start = lax.axis_index("gx") * row_count
    col_start = lax.axis_index("gy") * col_count
    u_local = NA // lax.axis_size("gx")
    permittivity = jnp.zeros(material.shape, jnp.float32)
    for material_id in range(NMAT):
        permittivity = permittivity + jnp.where(
            material == material_id, eps_table[material_id], 0.0
        )
    update_scale = courant / permittivity
    local_row = src_pos[:, 1] - row_start
    local_col = src_pos[:, 2] - col_start
    inside = (local_row >= 0) & (local_row < row_count) & (local_col >= 0) & (local_col < col_count)
    kept_amp = jnp.where(inside, src_amp, 0.0)
    safe_row = jnp.clip(local_row, 0, row_count - 1)
    safe_col = jnp.clip(local_col, 0, col_count - 1)
    source_grid = (
        jnp.zeros((LZ, row_count, col_count), jnp.float32)
        .at[src_pos[:, 0], safe_row, safe_col]
        .add(kept_amp)
    )
    electric, magnetic = (e_field, h_field)
    real_sum = jnp.zeros((NF, 4, row_count, col_count), jnp.float32)
    imag_sum = jnp.zeros((NF, 4, row_count, col_count), jnp.float32)
    for step_index in range(STEPS):
        moment = float(step_index + 1)
        row_e = shifted(electric[1:3, :, 0, :], "gx", -1)
        col_e = shifted(electric[0::2, :, :, 0], "gy", -1)
        magnetic = magnetic - courant * curl_forward(electric, row_e, col_e)
        row_h = shifted(magnetic[1:3, :, row_count - 1, :], "gx", 1)
        col_h = shifted(magnetic[0::2, :, :, col_count - 1], "gy", 1)
        electric = electric + update_scale * curl_backward(magnetic, row_h, col_h)
        electric = electric.at[2].add(math.sin(source_rate * moment) * source_grid)
        face_now = jnp.stack(
            [-magnetic[1, FACE], magnetic[0, FACE], electric[1, FACE], -electric[0, FACE]]
        )
        real_sum = real_sum + face_now[None] * jnp.cos(freqs * moment)[:, None, None, None]
        imag_sum = imag_sum + face_now[None] * jnp.sin(freqs * moment)[:, None, None, None]
    item_count = NF * 4
    currents = jnp.stack(
        [
            real_sum.reshape(item_count, row_count, col_count),
            imag_sum.reshape(item_count, row_count, col_count),
        ],
        1,
    ).astype(jnp.bfloat16)
    angle_index = jnp.arange(NA, dtype=jnp.int32)
    y_cells = col_start + jnp.arange(col_count, dtype=jnp.int32)
    y_real, y_imag = chirp(
        y_cells[:, None], (angle_index + NA // 4)[None, :], zoom_factor * grid_cols
    )
    y_table = jnp.concatenate([y_real, y_imag], 1).astype(jnp.bfloat16)
    x_cells = row_start + jnp.arange(row_count, dtype=jnp.int32)

    def one_block(block_index):
        u_index = block_index * u_local + jnp.arange(u_local, dtype=jnp.int32)
        x_real, x_imag = chirp(
            (u_index - NA // 2)[:, None], x_cells[None, :], zoom_factor * grid_rows
        )
        x_table = jnp.stack([x_real, x_imag]).astype(jnp.bfloat16)
        product = jnp.einsum(
            "aur,ibrc->uiabc", x_table, currents, preferred_element_type=jnp.float32
        )
        part_re, part_im = complex_pair(
            product[:, :, 0, 0], product[:, :, 0, 1], product[:, :, 1, 0], product[:, :, 1, 1]
        )
        return jnp.stack([part_re, part_im], 2)

    blocks = lax.map(
        one_block, jnp.arange(lax.axis_size("gx") * u_local // u_local, dtype=jnp.int32)
    )
    summed = lax.psum_scatter(
        blocks.reshape((lax.axis_size("gx") * u_local,) + blocks.shape[2:]),
        "gx",
        scatter_dimension=0,
        tiled=True,
    )
    sectioned = summed.astype(jnp.bfloat16)
    second = jnp.einsum("uibc,cw->uibw", sectioned, y_table, preferred_element_type=jnp.float32)
    far_re, far_im = complex_pair(
        second[:, :, 0, :NA], second[:, :, 0, NA:], second[:, :, 1, :NA], second[:, :, 1, NA:]
    )
    partial_far = jnp.stack([far_re, far_im], 2)
    inv_norm = 1.0 / math.sqrt(grid_rows * grid_cols)
    far_field = lax.psum_scatter(partial_far, "gy", scatter_dimension=3, tiled=True) * inv_norm
    return (electric, magnetic, far_field)


def solution(mesh):
    placed = (
        P(None, None, "gx", "gy"),
        P(None, None, "gx", "gy"),
        P(None, "gx", "gy"),
        P(),
        P(),
        P(),
        P(),
    )
    return jax.shard_map(
        on_device,
        mesh=mesh,
        in_specs=placed,
        out_specs=(P(None, None, "gx", "gy"), P(None, None, "gx", "gy"), P("gx", None, None, "gy")),
        check_vma=False,
    )
```

profile of v0, /device:TPU:0, one launch (start us, length us, event | category | flops | bytes accessed | tf_op | source)
XLA Modules:
  0.0 587.6 jit_solution(14347437408852494837)
XLA Ops:
  14.4 3.1 slice_bitcast_fusion.28
  21.7 22.3 %scatter_custom_fusion = f32[393216]{0:T(1024)S(1)} fusion(s32[4096]{0:T(1024)S(1)} %broadcast_select_fusion, f32[4096]{0:T(1024)S(1)} %broadcast_select_fusion.1, f32[]{:T(128)} %constant.146.clone.1), kind=kCustom, calls=%fused_computation.129 | custom fusion | flops 4096 | bytes 1572868
  45.9 6.4 %add_divide_fusion = f32[3,256,512]{2,1,0:T(8,128)S(1)} fusion(s32[3,256,512]{2,1,0:T(8,128)S(1)} %copy-done.29, f32[]{:T(128)} %bitcast.7, f32[]{:T(128)} %bitcast.6, f32[]{:T(128)} %bitcast.5, f32[]{:T(128)} %bitcast.4, f32[]{:T(128)} %bitcast.3, f32[]{:T(128)} %bitcast.2, f32[]{:T(128)} %bitcast.1, f32[]{:T(128)} %bitcast), kind=kLoop, calls=%fused_computation.109 | loop fusion | flops 9437184 | bytes 3145760 | tf_op jit(solution)/shard_map/div | solution.py:84
  52.4 3.1 reshape.426
  60.2 4.4 slice_bitcast_fusion.12
  76.8 4.5 collective-permute-start.2
  85.2 3.8 collective-permute-start.3
  91.0 3.9 slice_bitcast_fusion.9
  112.8 3.1 slice_bitcast_fusion.5
  120.5 3.8 fusion.41
  125.6 2.8 fusion.38
  136.1 4.5 collective-permute-start.6
  144.4 3.9 collective-permute-start.7
  150.3 3.5 slice_bitcast_fusion.4
  167.1 124.0 %while.15 = (s32[]{:T(128)}, f32[16,64,8,2,512]{4,2,3,1,0:T(8,128)}, s32[16]{0:T(128)S(1)}, bf16[8,2,256,512]{3,2,1,0:T(8,128)(2,1)}, s32[]{:T(128)}, /*index=5*/s32[]{:T(128)}, s32[1]{0:T(128)}) while((s32[]{:T(128)}, f32[16,64,8,2,512]{4,2,3,1,0:T(8,128)}, s32[16]{0:T(128)S(1)}, bf16[8,2,256,512]{3,2,1,0:T(8,128)(2,1)}, ...), condition=%wide.region_2.3_spmd.clone, body=%wide.region_1.2_spmd.clone.sunk | while | flops 538329472 | bytes 23202924 | solution.py:143
  168.7 2.9 fusion.64
  172.3 2.6 copy_dynamic-update-slice_fusion.2
  176.4 2.9 fusion.64
  180.0 2.6 copy_dynamic-update-slice_fusion.2
  184.2 2.9 fusion.64
  187.8 2.5 copy_dynamic-update-slice_fusion.2
  191.9 2.9 fusion.64
  195.5 2.6 copy_dynamic-update-slice_fusion.2
  199.7 2.9 fusion.64
  203.3 2.5 copy_dynamic-update-slice_fusion.2
  207.5 2.9 fusion.64
  211.0 2.6 copy_dynamic-update-slice_fusion.2
  215.2 2.9 fusion.64
  218.8 2.6 copy_dynamic-update-slice_fusion.2
  223.0 2.9 fusion.64
  226.6 2.6 copy_dynamic-update-slice_fusion.2
  230.7 2.9 fusion.64
  234.3 2.6 copy_dynamic-update-slice_fusion.2
  238.5 2.9 fusion.64
  242.1 2.6 copy_dynamic-update-slice_fusion.2
  246.2 2.9 fusion.64
  254.0 2.9 fusion.64
  257.5 2.6 copy_dynamic-update-slice_fusion.2
  261.8 2.9 fusion.64
  269.5 2.9 fusion.64
  273.1 2.6 copy_dynamic-update-slice_fusion.2
  277.2 2.9 fusion.64
  280.8 2.5 copy_dynamic-update-slice_fusion.2
  285.0 2.9 fusion.64
  291.4 9.0 %cosine_convert_fusion.1 = (bf16[512,1024]{1,0:T(8,128)(2,1)S(1)}, bf16[512,1024]{1,0:T(8,128)(2,1)S(1)}) fusion(s32[1024]{0:T(1024)S(1)} %iota_add_fusion.1, s32[512]{0:T(512)S(1)} %iota_add_fusion.2), kind=kLoop, calls=%fused_computation.58 | loop fusion | flops 8912896 | bytes 2103296 | tf_op jit(solution)/shard_map/convert.2
  300.4 186.5 %reduce-scatter.3.cloned.1.call-done = f32[64,8,2,512]{3,1,2,0:T(8,128)} async-done(((f32[1024,8,2,512]{3,1,2,0:T(8,128)}), f32[64,8,2,512]{3,1,2,0:T(8,128)}) %reduce-scatter.3.cloned.1.call-update) | async-done | bytes 2097168 | tf_op jit(solution)/shard_map/reduce_scatter | solution.py:146
  487.0 3.9 fusion.23
  494.6 83.7 %reduce-scatter.5.cloned.1.call-done = f32[64,8,2,128]{3,1,2,0:T(8,128)} async-done(((f32[64,8,2,1024]{3,1,2,0:T(8,128)}), f32[64,8,2,128]{3,1,2,0:T(8,128)}) %reduce-scatter.5.cloned.1.call-update) | async-done | bytes 524304 | tf_op jit(solution)/shard_map/reduce_scatter | solution.py:159
  (352 shorter events, 124.7 us)
Async XLA Ops:
  7.2 479.8 %reduce-scatter.3.cloned.1.call-start = ((), (), s32[]{:S(2)}) async-start(), calls=%async_computation.2 | async-start | bytes 35651584 | tf_op jit(solution)/shard_map/reduce_scatter | solution.py:146
  8.7 51.0 %collective-permute-start = (f32[2,3,256]{2,0,1:T(2,128)S(1)}, f32[2,3,256]{2,0,1:T(2,128)S(1)}, u32[]{:S(2)}, u32[]{:S(2)}) collective-permute-start(f32[2,3,256]{2,0,1:T(2,128)S(1)} %bitcast.261), channel_id=1, source_target_pairs={{1,0},{2,1},{3,2},{4,3},{5,4},{6,5},{7,6},{9,8},{10,9},{11,10},{12... | collective-permute-start | bytes 18440 | tf_op jit(solution)/shard_map/ppermute | solution.py:24
  10.9 49.2 %collective-permute-start.1 = (f32[2,3,512]{2,0,1:T(2,128)S(1)}, f32[2,3,512]{2,0,1:T(2,128)S(1)}, u32[]{:S(2)}, u32[]{:S(2)}) collective-permute-start(f32[2,3,512]{2,0,1:T(2,128)S(1)} %bitcast.260), channel_id=1, source_target_pairs={{8,0},{16,8},{24,16},{32,24},{40,32},{48,40},{56,48},{64,56},{72,6... | collective-permute-start | bytes 36872 | tf_op jit(solution)/shard_map/ppermute | solution.py:24
  14.4 3.1 copy-start.33
  19.3 2.2 copy-start.36
  19.4 2.3 copy-start.35
  45.9 6.4 %copy-start.38 = (f32[2]{0:T(128)S(1)}, f32[2]{0:T(128)}, u32[]{:S(2)}) copy-start(f32[2]{0:T(128)} %param.19) | copy-start | bytes 28
  52.4 44.8 %copy-start.9 = (f32[3,256,512]{2,1,0:T(8,128)}, f32[3,256,512]{2,1,0:T(8,128)S(1)}, u32[]{:S(2)}) copy-start(f32[3,256,512]{2,1,0:T(8,128)S(1)} %add_divide_fusion) | copy-start | bytes 4718596
  60.1 5.2 slice-start.8
  60.1 5.2 slice-start.9
  64.6 3.5 copy-start.3
  65.3 2.7 slice-start.12
  70.0 2.4 copy-start.1
  76.8 12.2 %collective-permute-start.2 = (f32[2,3,256]{2,0,1:T(2,128)S(1)}, f32[2,3,256]{2,0,1:T(2,128)S(1)}, u32[]{:S(2)}, u32[]{:S(2)}) collective-permute-start(f32[2,3,256]{2,0,1:T(2,128)S(1)} %bitcast.263), channel_id=1, source_target_pairs={{0,1},{1,2},{2,3},{3,4},{4,5},{5,6},{6,7},{8,9},{9,10},{10,11},{11... | collective-permute-start | bytes 18440 | tf_op jit(solution)/shard_map/ppermute | solution.py:24
  85.2 4.9 collective-permute-start.3
  90.9 4.1 slice-start.4
  91.0 4.2 slice-start.5
  91.0 4.5 copy-start.20
  91.0 4.8 copy-start.21
  91.0 4.8 copy-start.31
  94.9 2.4 slice-start.10
  99.4 6.7 %copy-start = (f32[3,3,256,512]{3,2,1,0:T(8,128)}, f32[3,3,256,512]{3,2,1,0:T(8,128)S(1)}, u32[]{:S(2)}) copy-start(f32[3,3,256,512]{3,2,1,0:T(8,128)S(1)} %get-tuple-element.139) | copy-start | bytes 14155780
  109.6 9.8 %collective-permute-start.4 = (f32[2,3,256]{2,0,1:T(2,128)S(1)}, f32[2,3,256]{2,0,1:T(2,128)S(1)}, u32[]{:S(2)}, u32[]{:S(2)}) collective-permute-start(f32[2,3,256]{2,0,1:T(2,128)S(1)} %bitcast.262), channel_id=1, source_target_pairs={{1,0},{2,1},{3,2},{4,3},{5,4},{6,5},{7,6},{9,8},{10,9},{11,10},{12... | collective-permute-start | bytes 18440 | tf_op jit(solution)/shard_map/ppermute | solution.py:24
  111.5 9.0 %collective-permute-start.5 = (f32[2,3,512]{2,0,1:T(2,128)}, f32[2,3,512]{2,0,1:T(2,128)S(1)}, u32[]{:S(2)}, u32[]{:S(2)}) collective-permute-start(f32[2,3,512]{2,0,1:T(2,128)} %bitcast.211), channel_id=1, source_target_pairs={{8,0},{16,8},{24,16},{32,24},{40,32},{48,40},{56,48},{64,56},{72,6... | collective-permute-start | bytes 36872 | tf_op jit(solution)/shard_map/ppermute | solution.py:24
  112.8 3.2 copy-start.24
  112.8 3.2 copy-start.25
  112.8 3.2 copy-start.28
  120.3 4.1 slice-start
  120.5 4.1 slice-start.1
  120.5 4.6 copy-start.16
  120.5 5.0 copy-start.17
  120.5 5.0 copy-start.30
  124.4 4.1 slice-start.14
  125.6 2.9 slice-start.15
  125.6 2.9 copy-start.4
  125.6 2.9 copy-start.6
  125.6 3.2 copy-start.8
  130.6 2.4 copy-start.2
  136.1 12.2 %collective-permute-start.6 = (f32[2,3,256]{2,0,1:T(2,128)S(1)}, f32[2,3,256]{2,0,1:T(2,128)S(1)}, u32[]{:S(2)}, u32[]{:S(2)}) collective-permute-start(f32[2,3,256]{2,0,1:T(2,128)S(1)} %bitcast.264), channel_id=1, source_target_pairs={{0,1},{1,2},{2,3},{3,4},{4,5},{5,6},{6,7},{8,9},{9,10},{10,11},{11... | collective-permute-start | bytes 18440 | tf_op jit(solution)/shard_map/ppermute | solution.py:24
  144.4 5.1 collective-permute-start.7
  150.3 3.6 slice-start.6
  150.3 3.7 slice-start.7
  150.3 4.0 copy-start.22
  150.3 4.3 copy-start.23
  150.3 4.4 copy-start.32
  153.8 2.5 slice-start.2
  158.6 2.2 copy-start.11
  291.1 287.2 %reduce-scatter.5.cloned.1.call-start = ((), (), s32[]{:S(2)}) async-start(), calls=%async_computation.3 | async-start | bytes 4718592 | tf_op jit(solution)/shard_map/reduce_scatter | solution.py:159
  (21 other events, 30.8 us)
Sparse Core Ops, SparseCore 0:
  291.2 195.6 reduce-scatter.2
  494.7 83.5 reduce-scatter.4
where the time goes:
time: 598 us; the launch traced here: 588 us
  waiting for transfers between devices  270 us (45%)
  local copies, waits for them, and re-layouts  117 us (20%)
  other arithmetic  101 us (17%)
  matrix products  50.6 us (8%)
  starting transfers between devices  22.2 us (4%)
  between operations  15.2 us (3%)
  loops' own time  11.2 us (2%)
    reduce_scatter x1, waiting for transfers between devices, on_device(): lax.psum_scatter(blocks.reshape((lax.axis_size('gx') * u_local,) + blocks...  187 us
    reduce_scatter x1, waiting for transfers between devices, on_device(): lax.psum_scatter(partial_far, 'gy', scatter_dimension=3, tiled=True)  83.7 us
    dot_general x16, matrix products, one_block(): jnp.einsum('aur,ibrc->uiabc', x_table, currents, preferred_element_type=j...  46.7 us
    dynamic_update_slice x16, local copies, waits for them, and re-layouts, on_device(): lax.map(one_block, jnp.arange(lax.axis_size('gx') * u_local // u_local, d...  40.9 us
    unnamed x12, other arithmetic  22.5 us
    ppermute x8, starting transfers between devices, shifted(): return lax.ppermute(block, axis, route)  21.9 us
    another operation x18, other arithmetic  15.8 us
    unnamed x121, local copies, waits for them, and re-layouts  13.1 us
  transfers between devices with their start and end apart: 10, of which 2 were waited for; matrix products, arithmetic and copies ran while one was open for 13% of the time, Pallas kernels for 0%

commit v1 on v0

v1 whole, which is shorter than its diff:
```python
import functools
import math

import jax
import jax.numpy as jnp
import ml_dtypes
import numpy as np
from jax import lax
from jax.experimental import pallas as pl
from jax.experimental.pallas import tpu as pltpu
from jax.sharding import Mesh, PartitionSpec as P

LZ = 3
NA = 1024
NMAT = 8
N = 4096
NSRC = 4096
ROWS = 256
COLS = 512
OFF = 8
EXT_R = 280
EXT_C = 640
USED_R = 272
CHUNKS = 4
courant = 0.5
source_rate = 0.7
PERIOD = 4 * N
GX = ("ga", "gc")
MIB = 1 << 20
F32 = jnp.float32
BF16 = jnp.bfloat16


def tables():
    cell = np.arange(N, dtype=np.int64)
    t = np.arange(16)[:, None, None]
    q = np.arange(5)[None, :, None]
    m = np.arange(8)[None, None, :]
    w = (64 * m + 4 * t + q)[..., None]
    phase = np.remainder(w * cell, PERIOD) * (2.0 * math.pi / PERIOD)
    x_table = np.stack([np.cos(phase), np.sin(phase)], 2).reshape(16 * 80, N)
    v = np.arange(NA, dtype=np.int64) + NA // 4
    phase = np.remainder(cell[:, None] * v[None, :], PERIOD) * (2.0 * math.pi / PERIOD)
    y_table = np.concatenate([np.cos(phase), -np.sin(phase)], 1)
    y_table = y_table.reshape(8, 2, 256, 2 * NA).transpose(1, 0, 2, 3).reshape(16, 256, 2 * NA)
    return x_table.astype(ml_dtypes.bfloat16), y_table.astype(ml_dtypes.bfloat16)


def params(**more):
    return pltpu.CompilerParams(vmem_limit_bytes=56 * MIB, **more)


def vmem():
    return pl.BlockSpec(memory_space=pltpu.VMEM)


def smem():
    return pl.BlockSpec(memory_space=pltpu.SMEM)


def scale_of(material, eps_ref):
    eps = jnp.full(material.shape, eps_ref[0], F32)
    for k in range(1, NMAT):
        eps = jnp.where(material == k, eps_ref[k], eps)
    return courant / eps


def pack_cols_kernel(e_lo, e_hi, h_lo, h_hi, m_lo, m_hi, eps_ref, left_ref, right_ref):
    rows = left_ref.shape[0]
    lane = lax.broadcasted_iota(jnp.int32, (rows, 128), 1)
    left = jnp.zeros((rows, 128), F32)
    right = jnp.zeros((rows, 128), F32)
    for a in range(7):
        for layer in range(LZ):
            q = (a * LZ + layer) * 2
            if a < 3:
                lo, hi = e_lo[a, layer], e_hi[a, layer]
            elif a < 6:
                lo, hi = h_lo[a - 3, layer], h_hi[a - 3, layer]
            else:
                lo, hi = scale_of(m_lo[layer], eps_ref), scale_of(m_hi[layer], eps_ref)
            here = (lane == q) | (lane == q + 1)
            moved = pltpu.roll(lo, q, 1) if q else lo
            left = jnp.where(here, moved, left)
            right = jnp.where(here, pltpu.roll(hi, (q + 2) % 128, 1), right)
    left_ref[...] = left
    right_ref[...] = right


def pack_cols(e, h, material, eps):
    rows = 32
    lo4 = pl.BlockSpec((3, LZ, rows, 128), lambda r: (0, 0, r, 0))
    hi4 = pl.BlockSpec((3, LZ, rows, 128), lambda r: (0, 0, r, COLS // 128 - 1))
    lo3 = pl.BlockSpec((LZ, rows, 128), lambda r: (0, r, 0))
    hi3 = pl.BlockSpec((LZ, rows, 128), lambda r: (0, r, COLS // 128 - 1))
    out = pl.BlockSpec((rows, 128), lambda r: (r, 0))
    return pl.pallas_call(
        pack_cols_kernel,
        grid=(ROWS // rows,),
        in_specs=[lo4, hi4, lo4, hi4, lo3, hi3, smem()],
        out_specs=[out, out],
        out_shape=[jax.ShapeDtypeStruct((ROWS, 128), F32)] * 2,
        compiler_params=params(),
        name="pack_cols",
    )(e, e, h, h, material, material, eps)


def rim_tile(from_left, from_right, index):
    lane = lax.broadcasted_iota(jnp.int32, from_left.shape, 1)
    q = 2 * index
    right = pltpu.roll(from_right, (128 - q) % 128, 1) if q else from_right
    left = pltpu.roll(from_left, 126 - q, 1)
    return jnp.where(lane < 2, right, jnp.where(lane >= 126, left, 0.0))


def pack_rows_kernel(
    e_lo, e_hi, h_lo, h_hi, s_lo, s_hi, fl_lo, fl_hi, fr_lo, fr_hi, up_ref, down_ref
):
    sub = lax.broadcasted_iota(jnp.int32, (8, EXT_C), 0)
    up = down = None
    for a in range(7):
        for layer in range(LZ):
            index = a * LZ + layer
            if a < 3:
                lo, hi = e_lo[a, layer], e_hi[a, layer]
            elif a < 6:
                lo, hi = h_lo[a - 3, layer], h_hi[a - 3, layer]
            else:
                lo, hi = s_lo[layer], s_hi[layer]
            lo = jnp.concatenate([lo, rim_tile(fl_lo[...], fr_lo[...], index)], 1)
            hi = jnp.concatenate([hi, rim_tile(fl_hi[...], fr_hi[...], index)], 1)
            p = 2 * (index % 4)
            if p == 0:
                up = jnp.zeros((8, EXT_C), F32)
                down = jnp.zeros((8, EXT_C), F32)
            here = (sub == p) | (sub == p + 1)
            up = jnp.where(here, pltpu.roll(lo, p, 0) if p else lo, up)
            down = jnp.where(here, pltpu.roll(hi, (p + 2) % 8, 0) if p != 6 else hi, down)
            tile = index // 4
            up_ref[8 * tile : 8 * tile + 8, :] = up
            down_ref[8 * tile : 8 * tile + 8, :] = down


def pack_rows(e, h, scale, from_left, from_right):
    last = ROWS // 8 - 1
    lo4 = pl.BlockSpec((3, LZ, 8, COLS), lambda r: (0, 0, 0, 0))
    hi4 = pl.BlockSpec((3, LZ, 8, COLS), lambda r: (0, 0, last, 0))
    lo3 = pl.BlockSpec((LZ, 8, COLS), lambda r: (0, 0, 0))
    hi3 = pl.BlockSpec((LZ, 8, COLS), lambda r: (0, last, 0))
    lo2 = pl.BlockSpec((8, 128), lambda r: (0, 0))
    hi2 = pl.BlockSpec((8, 128), lambda r: (last, 0))
    out = pl.BlockSpec((48, EXT_C), lambda r: (0, 0))
    return pl.pallas_call(
        pack_rows_kernel,
        grid=(1,),
        in_specs=[lo4, hi4, lo4, hi4, lo3, hi3, lo2, hi2, lo2, hi2],
        out_specs=[out, out],
        out_shape=[jax.ShapeDtypeStruct((48, EXT_C), F32)] * 2,
        compiler_params=params(),
        name="pack_rows",
    )(e, e, h, h, scale, scale, from_left, from_left, from_right, from_right)


def prepare_kernel(material_ref, eps_ref, pos_ref, amp_ref, place_ref, scale_ref, grid_ref):
    def scale_strip(s, _):
        r = pl.multiple_of(s * 8, 8)
        for layer in range(LZ):
            scale_ref[layer, pl.ds(r, 8), :] = scale_of(material_ref[layer, pl.ds(r, 8), :], eps_ref)
        return 0

    lax.fori_loop(0, ROWS // 8, scale_strip, 0)

    groups = NSRC // 128
    row = pos_ref[1] - place_ref[0] * ROWS + OFF
    col = pos_ref[2] - place_ref[1] * COLS
    inside = (row >= OFF - 1) & (row <= ROWS + OFF) & (col >= -1) & (col <= COLS)
    col = jnp.where(col < 0, EXT_C - 1, col)
    taken = jnp.where(inside, 1.0, 0.0)
    lane_a = lax.broadcasted_iota(jnp.int32, (128, 128), 0)
    lane_b = lax.broadcasted_iota(jnp.int32, (128, 128), 1)
    before = jnp.where(lane_a < lane_b, 1.0, 0.0).astype(BF16)
    group_a = lax.broadcasted_iota(jnp.int32, (groups, groups), 0)
    group_b = lax.broadcasted_iota(jnp.int32, (groups, groups), 1)
    earlier = jnp.where(group_b < group_a, 1.0, 0.0).astype(BF16)
    in_group = jnp.dot(taken.astype(BF16), before, preferred_element_type=F32)
    ahead = jnp.dot(earlier, taken.astype(BF16), preferred_element_type=F32)
    rank = in_group + jnp.sum(ahead, axis=1, keepdims=True)
    rank = jnp.where(inside, rank, -1.0)
    features = (
        row.astype(F32),
        col.astype(F32),
        pos_ref[0].astype(F32),
        amp_ref[...],
    )
    count = jnp.sum(taken).astype(jnp.int32)
    slot = lax.broadcasted_iota(jnp.int32, (128, 128), 0).astype(F32)
    feature_lane = lax.broadcasted_iota(jnp.int32, (128, 128), 1)
    row_of = lax.broadcasted_iota(jnp.int32, (USED_R, 128), 0).astype(F32)
    col_of = lax.broadcasted_iota(jnp.int32, (EXT_C, 128), 0).astype(F32)
    grid_ref[...] = jnp.zeros(grid_ref.shape, F32)

    def one_pass(p, _):
        base = (p * 128).astype(F32)
        sums = [jnp.zeros((128, 128), F32) for _ in features]
        found = jnp.zeros((128, 128), F32)
        for g in range(groups):
            chosen = slot == rank[g : g + 1, :] - base
            found = jnp.where(chosen, 1.0, found)
            for f, feature in enumerate(features):
                sums[f] = jnp.where(chosen, feature[g : g + 1, :], sums[f])
        packed = jnp.zeros((128, 128), F32)
        for f, total in enumerate(sums + [found]):
            packed = jnp.where(feature_lane == f, jnp.sum(total, axis=1, keepdims=True), packed)
        packed = packed.T
        src_row, src_col, src_layer = packed[0:1], packed[1:2], packed[2:3]
        amp, valid = packed[3:4], packed[4:5]
        amp_1 = amp.astype(BF16).astype(F32)
        amp_2 = (amp - amp_1).astype(BF16).astype(F32)
        amp_3 = amp - amp_1 - amp_2
        at_col = jnp.where(col_of == src_col, 1.0, 0.0).astype(BF16)
        at_col = jnp.concatenate([at_col] * 3, 1)
        for layer in range(LZ):
            at_row = (row_of == src_row) & (src_layer == layer) & (valid > 0.0)
            weights = jnp.concatenate(
                [jnp.where(at_row, part, 0.0).astype(BF16) for part in (amp_1, amp_2, amp_3)], 1
            )
            grid_ref[layer] += lax.dot_general(
                weights, at_col, (((1,), (1,)), ((), ())), preferred_element_type=F32
            )
        return 0

    lax.fori_loop(0, (count + 127) // 128, one_pass, 0)


def prepare(material, eps, pos, amp, place):
    return pl.pallas_call(
        prepare_kernel,
        in_specs=[vmem(), smem(), vmem(), vmem(), smem()],
        out_specs=[vmem(), vmem()],
        out_shape=[
            jax.ShapeDtypeStruct((LZ, ROWS, COLS), F32),
            jax.ShapeDtypeStruct((LZ, USED_R, EXT_C), F32),
        ],
        compiler_params=params(),
        cost_estimate=pl.CostEstimate(flops=3_000_000_000, bytes_accessed=6_000_000, transcendentals=0),
        name="prepare",
    )(material, eps, pos, amp, place)


def yee_kernel(
    with_fields,
    with_face,
    e_in,
    h_in,
    scale_in,
    grid_in,
    from_left,
    from_right,
    from_top,
    from_bottom,
    place_ref,
    *refs,
):
    refs = list(refs)
    e_out, h_out = (refs.pop(0), refs.pop(0)) if with_fields else (None, None)
    face_out = refs.pop(0) if with_face else None
    e, h, scale, grid = refs[:4]
    refs = refs[4:]
    first = refs.pop(0) if with_face else None
    in_sem, out_sem = refs

    copies = []
    for layer in range(LZ):
        for a in range(3):
            for source, target in ((e_in, e), (h_in, h)):
                copies.append(
                    pltpu.make_async_copy(
                        source.at[a, layer],
                        target.at[a, layer, pl.ds(OFF, ROWS), pl.ds(0, COLS)],
                        in_sem.at[len(copies)],
                    )
                )
        copies.append(
            pltpu.make_async_copy(
                scale_in.at[layer],
                scale.at[layer, pl.ds(OFF, ROWS), pl.ds(0, COLS)],
                in_sem.at[len(copies)],
            )
        )
    copies.append(pltpu.make_async_copy(grid_in, grid, in_sem.at[len(copies)]))
    for copy in copies:
        copy.start()

    sub = lax.broadcasted_iota(jnp.int32, (8, EXT_C), 0)
    lane = lax.broadcasted_iota(jnp.int32, (8, EXT_C), 1)

    def array_of(a, layer):
        if a < 3:
            return e.at[a, layer]
        if a < 6:
            return h.at[a - 3, layer]
        return scale.at[layer]

    for a in range(7):
        for layer in range(LZ):
            index = a * LZ + layer
            target = array_of(a, layer)
            p, tile = 2 * (index % 4), index // 4
            top = from_top[8 * tile : 8 * tile + 8, :]
            top = pltpu.roll(top, (6 - p) % 8, 0) if p != 6 else top
            target[0:8, :] = jnp.where(sub >= 6, top, 0.0)
            bottom = from_bottom[8 * tile : 8 * tile + 8, :]
            bottom = pltpu.roll(bottom, (8 - p) % 8, 0) if p else bottom
            target[ROWS + OFF : ROWS + OFF + 8, :] = jnp.where(sub < 2, bottom, 0.0)
            if a < 3:
                target[USED_R : USED_R + 8, :] = jnp.zeros((8, EXT_C), F32)

    def rim_strip(s, _):
        r = pl.multiple_of(s * 8, 8)
        left = from_left[pl.ds(r, 8), :]
        right = from_right[pl.ds(r, 8), :]
        for a in range(7):
            for layer in range(LZ):
                array_of(a, layer)[pl.ds(pl.multiple_of(r + OFF, 8), 8), COLS:EXT_C] = rim_tile(
                    left, right, a * LZ + layer
                )
        return 0

    lax.fori_loop(0, ROWS // 8, rim_strip, 0)

    row_place, col_place = place_ref[0], place_ref[1]
    half = jnp.full((8, EXT_C), courant, F32)
    half = jnp.where((lane >= COLS + 64) & (col_place == 0), 0.0, half)
    half = jnp.where((lane >= COLS) & (lane < COLS + 64) & (col_place == 7), 0.0, half)
    half_top = jnp.where(row_place == 0, 0.0, half)
    half_bottom = jnp.where(row_place == 15, 0.0, half)

    for copy in copies:
        copy.wait()

    def x_next(ref, here, r):
        after = ref[pl.ds(pl.multiple_of(r + 8, 8), 8), :]
        return jnp.where(sub == 7, pltpu.roll(after, 7, 0), pltpu.roll(here, 7, 0))

    def x_last(ref, here, r):
        if isinstance(r, int):
            return pltpu.roll(here, 1, 0)
        before = ref[pl.ds(pl.multiple_of(r - 8, 8), 8), :]
        return jnp.where(sub == 0, pltpu.roll(before, 1, 0), pltpu.roll(here, 1, 0))

    def y_next(here):
        return pltpu.roll(here, EXT_C - 1, 1)

    def y_last(here):
        return pltpu.roll(here, 1, 1)

    def update_h(r, coef):
        rows = pl.ds(r, 8)
        for layer in range(LZ):
            ex, ey, ez = (e[a, layer, rows, :] for a in range(3))
            if layer + 1 < LZ:
                ex_up, ey_up = e[0, layer + 1, rows, :], e[1, layer + 1, rows, :]
            else:
                ex_up = ey_up = 0.0
            h[0, layer, rows, :] -= coef * (y_next(ez) - ez - (ey_up - ey))
            h[1, layer, rows, :] -= coef * (ex_up - ex - (x_next(e.at[2, layer], ez, r) - ez))
            h[2, layer, rows, :] -= coef * (x_next(e.at[1, layer], ey, r) - ey - (y_next(ex) - ex))

    def update_e(r, moment):
        rows = pl.ds(r, 8)
        strength = math.sin(source_rate * moment)
        for layer in range(LZ):
            hx, hy, hz = (h[a, layer, rows, :] for a in range(3))
            if layer > 0:
                hx_low, hy_low = h[0, layer - 1, rows, :], h[1, layer - 1, rows, :]
            else:
                hx_low = hy_low = 0.0
            rate = scale[layer, rows, :]
            e[0, layer, rows, :] += rate * (hz - y_last(hz) - (hy - hy_low))
            e[1, layer, rows, :] += rate * (hx - hx_low - (hz - x_last(h.at[2, layer], hz, r)))
            e[2, layer, rows, :] = (
                e[2, layer, rows, :]
                + rate * (hy - x_last(h.at[1, layer], hy, r) - (hx - y_last(hx)))
                + strength * grid[layer, rows, :]
            )

    def face(r):
        rows = pl.ds(r, 8)
        return [
            h[1, 1, rows, 0:COLS],
            h[0, 1, rows, 0:COLS],
            e[1, 1, rows, 0:COLS],
            e[0, 1, rows, 0:COLS],
        ]

    update_h(0, half_top)
    update_e(0, 1.0)

    def first_step(s, _):
        r = pl.multiple_of(s * 8, 8)
        update_h(r, half)
        update_e(r, 1.0)
        if with_face:
            for k, now in enumerate(face(r)):
                first[k, pl.ds(pl.multiple_of(r - OFF, 8), 8), :] = now
        return 0

    lax.fori_loop(1, 1 + ROWS // 8, first_step, 0)
    update_h(pl.multiple_of(jnp.int32(ROWS + OFF), 8), half_bottom)
    update_e(pl.multiple_of(jnp.int32(ROWS + OFF), 8), 1.0)

    update_h(0, half_top)
    signs = (-1.0, 1.0, 1.0, -1.0)

    def second_step(s, _):
        own = pl.multiple_of(s * 16, 16)
        pieces = [[] for _ in range(8)]
        for part in range(2):
            r = pl.multiple_of(own + OFF + 8 * part, 8)
            update_h(r, half)
            update_e(r, 2.0)
            if with_face:
                for k, now in enumerate(face(r)):
                    then = first[k, pl.ds(pl.multiple_of(own + 8 * part, 8), 8), :]
                    pieces[2 * k].append(signs[k] * (then + now))
                    pieces[2 * k + 1].append(signs[k] * (then - now))
        if with_face:
            for k in range(8):
                block = jnp.concatenate(pieces[k], 0).astype(BF16)
                face_out[2 * k, pl.ds(own, 16), :] = block[:, 0:256]
                face_out[2 * k + 1, pl.ds(own, 16), :] = block[:, 256:512]
        return 0

    span = ROWS // CHUNKS
    sent = []
    for chunk in range(CHUNKS):
        lax.fori_loop(chunk * (span // 16), (chunk + 1) * (span // 16), second_step, 0)
        if with_fields:
            window = pl.ds(OFF + chunk * span, span)
            target_rows = pl.ds(chunk * span, span)
            for layer in range(LZ):
                for a in range(3):
                    for source, target in ((e, e_out), (h, h_out)):
                        copy = pltpu.make_async_copy(
                            source.at[a, layer, window, pl.ds(0, COLS)],
                            target.at[a, layer, target_rows, :],
                            out_sem.at[len(sent)],
                        )
                        copy.start()
                        sent.append(copy)
    for copy in sent:
        copy.wait()


def yee(with_fields, with_face, e, h, scale, grid, rims, place):
    field = jax.ShapeDtypeStruct((3, LZ, ROWS, COLS), F32)
    anywhere = pl.BlockSpec(memory_space=pl.ANY)
    out_shape = []
    out_specs = []
    scratch = [
        pltpu.VMEM((3, LZ, EXT_R, EXT_C), F32),
        pltpu.VMEM((3, LZ, EXT_R, EXT_C), F32),
        pltpu.VMEM((LZ, EXT_R, EXT_C), F32),
        pltpu.VMEM((LZ, USED_R, EXT_C), F32),
    ]
    if with_fields:
        out_shape += [field, field]
        out_specs += [anywhere, anywhere]
    if with_face:
        out_shape.append(jax.ShapeDtypeStruct((16, ROWS, 256), BF16))
        out_specs.append(vmem())
        scratch.append(pltpu.VMEM((4, ROWS, COLS), F32))
    scratch += [
        pltpu.SemaphoreType.DMA((7 * LZ + 1,)),
        pltpu.SemaphoreType.DMA((CHUNKS * 6 * LZ,)),
    ]
    return pl.pallas_call(
        functools.partial(yee_kernel, with_fields, with_face),
        in_specs=[anywhere] * 4 + [vmem()] * 4 + [smem()],
        out_specs=out_specs,
        out_shape=out_shape,
        scratch_shapes=scratch,
        compiler_params=params(),
        cost_estimate=pl.CostEstimate(
            flops=3_000_000_000, bytes_accessed=24_000_000, transcendentals=0
        ),
        name="yee_fields" if with_fields else "yee_face",
    )(e, h, scale, grid, *rims, place)


def columns_kernel(rows_ref, table_ref, out_ref, total):
    step = pl.program_id(0)

    @pl.when(step == 0)
    def _():
        total[...] = jnp.zeros(total.shape, F32)

    total[...] += jnp.dot(rows_ref[0], table_ref[0], preferred_element_type=F32)

    @pl.when(step == 15)
    def _():
        for q in range(4):
            for plus in (True, False):
                base = 16 * (q if plus else 4 - q)
                cos_re, cos_im = total[base : base + 8, 0:NA], total[base : base + 8, NA : 2 * NA]
                sin_re = total[base + 8 : base + 16, 0:NA]
                sin_im = total[base + 8 : base + 16, NA : 2 * NA]
                if plus:
                    parts = (cos_re + sin_im, cos_im - sin_re)
                else:
                    parts = (cos_re - sin_im, cos_im + sin_re)
                for ri, value in enumerate(parts):
                    for j in range(8):
                        block = value[:, 128 * j : 128 * j + 128]
                        for m in range(8):
                            owner = 8 + m if plus else 7 - m
                            row = (owner * 8 + j) * 8 + 2 * q + ri
                            out_ref[row : row + 1, :] = block[m : m + 1, :]


def columns(rows, table):
    return pl.pallas_call(
        columns_kernel,
        grid=(16,),
        in_specs=[
            pl.BlockSpec((1, 80, 256), lambda t: (t, 0, 0)),
            pl.BlockSpec((1, 256, 2 * NA), lambda t: (t, 0, 0)),
        ],
        out_specs=pl.BlockSpec((1024, 128), lambda t: (0, 0)),
        out_shape=jax.ShapeDtypeStruct((1024, 128), F32),
        scratch_shapes=[pltpu.VMEM((80, 2 * NA), F32)],
        compiler_params=params(),
        name="columns",
    )(rows, table)


def combine_kernel(parts_ref, coef_ref, place_ref, out_ref):
    sub = lax.broadcasted_iota(jnp.int32, (8, 128), 0)
    real_row = (sub % 2) == 0
    side = jnp.where(real_row, -1.0, 1.0)

    def swap(value):
        return jnp.where(real_row, pltpu.roll(value, 7, 0), pltpu.roll(value, 1, 0)) * side

    def one_block(t, _):
        where = jnp.where(place_ref[0] >= 8, t, 15 - t)
        for comp in range(4):
            total = parts_ref[(2 * comp) * 16 + t]
            change = parts_ref[(2 * comp + 1) * 16 + t]
            total_swap, change_swap = swap(total), swap(change)
            for f in range(2):
                value = (
                    coef_ref[f, 0] * total
                    + coef_ref[f, 1] * total_swap
                    + coef_ref[f, 3] * change
                    - coef_ref[f, 2] * change_swap
                )
                item = f * 4 + comp
                for q in range(4):
                    out_ref[where, 16 * q + 2 * item : 16 * q + 2 * item + 2, :] = value[
                        2 * q : 2 * q + 2, :
                    ]
        return 0

    lax.fori_loop(0, 16, one_block, 0)


def combine(parts, coef, place):
    return pl.pallas_call(
        combine_kernel,
        in_specs=[vmem(), smem(), smem()],
        out_specs=vmem(),
        out_shape=jax.ShapeDtypeStruct((16, 64, 128), F32),
        compiler_params=params(),
        name="combine",
    )(parts, coef, place)


def on_device(x_table, y_table, e, h, material, eps, src_pos, src_amp, freqs):
    row_place = lax.axis_index(GX)
    col_place = lax.axis_index("gy")
    place = jnp.stack([row_place, col_place]).astype(jnp.int32)
    left, right = pack_cols(e, h, material, eps)
    from_left = lax.ppermute(right, "gy", [(k, k + 1) for k in range(7)])
    from_right = lax.ppermute(left, "gy", [(k + 1, k) for k in range(7)])
    pos = src_pos.T.reshape(3, NSRC // 128, 128)
    amp = src_amp.reshape(NSRC // 128, 128)
    scale, grid = prepare(material, eps, pos, amp, place)
    up, down = pack_rows(e, h, scale, from_left, from_right)
    from_top = lax.ppermute(down, GX, [(k, k + 1) for k in range(15)])
    from_bottom = lax.ppermute(up, GX, [(k + 1, k) for k in range(15)])
    rims = (from_left, from_right, from_top, from_bottom)
    (face,) = yee(False, True, e, h, scale, grid, rims, place)
    e_out, h_out = yee(True, False, e, h, scale, grid, rims, place)

    half = jnp.cos(freqs * 0.5), jnp.sin(freqs * 0.5)
    turn = jnp.cos(freqs * 1.5), jnp.sin(freqs * 1.5)
    coef = jnp.stack(
        [turn[0] * half[0], turn[1] * half[0], turn[0] * half[1], turn[1] * half[1]], 1
    ) * (1.0 / N)

    face = lax.all_to_all(face, GX, 0, 0, tiled=True)
    rows = jnp.dot(x_table, face.reshape(N, 256), preferred_element_type=F32).astype(BF16)
    rows = lax.all_to_all(rows.reshape(16, 80, 256), ("gc", "gy"), 0, 0, tiled=True)
    far = columns(rows, y_table)
    far = lax.all_to_all(far.reshape(128, 8, 128), GX + ("gy",), 0, 0, tiled=True)
    far = combine(far, coef, place)
    return e_out, h_out, far.reshape(64, 8, 2, 128)


def solution(mesh):
    fine = Mesh(mesh.devices.reshape(8, 2, 8), ("ga", "gc", "gy"))
    field = P(None, None, GX, "gy")
    placed = (P(), P(), field, field, P(None, GX, "gy"), P(), P(), P(), P())
    mapped = jax.shard_map(
        on_device,
        mesh=fine,
        in_specs=placed,
        out_specs=(field, field, P(GX, None, None, "gy")),
        check_vma=False,
    )
    x_table, y_table = tables()

    def program(e_field, h_field, material, eps_table, src_pos, src_amp, freqs):
        return mapped(
            x_table, y_table, e_field, h_field, material, eps_table, src_pos, src_amp, freqs
        )

    return program
```

time: 598 us -> 162 us (0.27); the launches traced: 588 us -> 161 us
  waiting for transfers between devices: 270 us -> 3.77 us
  local copies, waits for them, and re-layouts: 117 us -> 3.38 us
  other arithmetic: 101 us -> 1.34 us
  Pallas kernels: 0 us -> 73.1 us
  blocking collectives: 0 us -> 58.9 us
  matrix products: 50.6 us -> 7.09 us
  between operations: 15.2 us -> 0.79 us
  loops' own time: 11.2 us -> 0 us
  starting transfers between devices: 22.2 us -> 12.6 us
    reduce_scatter x2 -> x0, waiting for transfers between devices: 270 us -> none  [the longest x1 187 us: on_device(): lax.psum_scatter(blocks.reshape((lax.axis_size('gx') * u_local,) + blocks...]
    pallas_call x0 -> x7, Pallas kernels: none -> 73.1 us  [the longest x2 41.1 us: yee(): pl.pallas_call(functools.partial(yee_kernel, with_fields, with_face), in_...]
    all_to_all x0 -> x2, blocking collectives: none -> 58.9 us  [the longest x1 36.9 us: on_device(): face = lax.all_to_all(face, GX, 0, 0, tiled=True)]
    dot_general x17 -> x1, matrix products: 50.6 us -> 7.09 us  [on_device(): jnp.dot(x_table, face.reshape(N, 256), preferred_element_type=F32)]
    dynamic_update_slice x16 -> x0, local copies, waits for them, and re-layouts: 40.9 us -> none  [on_device(): lax.map(one_block, jnp.arange(lax.axis_size('gx') * u_local // u_local, d...]
    another operation x28 -> x2, other arithmetic: 30.2 us -> 0.7 us  [the longest x1 0.65 us: on_device(): place = jnp.stack([row_place, col_place]).astype(jnp.int32)]
    slice x23 -> x0, local copies, waits for them, and re-layouts: 26 us -> none  [the longest x6 8.47 us: forward(): inner = lax.slice_in_dim(field, 1, field.shape[dimension], axis=dimension)]
    unnamed x12 -> x0, other arithmetic: 22.5 us -> none
  transfers between devices with their start and end apart: 10 -> 5, of which waited for: 2 -> 1; matrix products, arithmetic and copies ran while one was open for 13% -> 1% of each run, Pallas kernels for 0% -> 17%
where the time goes in v1:
time: 162 us; the launch traced here: 161 us
  Pallas kernels  73.1 us (45%)
  blocking collectives  58.9 us (36%)
  starting transfers between devices  12.6 us (8%)
  matrix products  7.09 us (4%)
  waiting for transfers between devices  3.77 us (2%)
  local copies, waits for them, and re-layouts  3.38 us (2%)
    pallas_call x2, Pallas kernels, yee(): pl.pallas_call(functools.partial(yee_kernel, with_fields, with_face), in_...  41.1 us
    all_to_all x1, blocking collectives, on_device(): face = lax.all_to_all(face, GX, 0, 0, tiled=True)  36.9 us
    all_to_all x1, blocking collectives, on_device(): lax.all_to_all(rows.reshape(16, 80, 256), ('gc', 'gy'), 0, 0, tiled=True)  22 us
    pallas_call x1, Pallas kernels, columns(): pl.pallas_call(columns_kernel, grid=(16,), in_specs=[pl.BlockSpec((1, 80,...  14.5 us
    dot_general x1, matrix products, on_device(): jnp.dot(x_table, face.reshape(N, 256), preferred_element_type=F32)  7.09 us
    pallas_call x1, Pallas kernels, pack_cols(): pl.pallas_call(pack_cols_kernel, grid=(ROWS // rows,), in_specs=[lo4, hi4...  6.79 us
    pallas_call x1, Pallas kernels, prepare(): pl.pallas_call(prepare_kernel, in_specs=[vmem(), smem(), vmem(), vmem(),...  6.54 us
    all_to_all x1, starting transfers between devices, on_device(): lax.all_to_all(far.reshape(128, 8, 128), GX + ('gy',), 0, 0, tiled=True)  4.62 us
  transfers between devices with their start and end apart: 5, of which 1 were waited for; matrix products, arithmetic and copies ran while one was open for 1% of the time, Pallas kernels for 17%

profile of v1, /device:TPU:0, one launch (start us, length us, event | category | flops | bytes accessed | tf_op | source)
XLA Modules:
  0.0 160.9 jit_solution(7607617431127047991)
XLA Ops:
  0.6 0.0 copy-start.5
  0.6 6.8 %pack_cols.1 = (f32[256,128]{1,0:T(8,128)}, f32[256,128]{1,0:T(8,128)}) custom-call(f32[3,3,256,512]{3,2,1,0:T(8,128)} %e_in.3, f32[3,3,256,512]{3,2,1,0:T(8,128)} %e_in.3, f32[3,3,256,512]{3,2,1,0:T(8,128)} %h_in.3, f32[3,3,256,512]{3,2,1,0:T(8,128)} %h_in.3, s32[3,256,512]{2,1,0:T(8,128)} %m_hi.1, s32[3,256,512]{2,1,0:T(8,128)} %m_hi.1, f32[8]{0:T(128)} %eps_ref.3), custom_call_target="tpu_custom_call" | custom-call | tf_op jit(solution)/shard_map/pack_cols/pallas_call | solution.py:97
  7.4 3.9 %collective-permute-start = (f32[256,128]{1,0:T(8,128)}, f32[256,128]{1,0:T(8,128)S(1)}, u32[]{:S(2)}, u32[]{:S(2)}) collective-permute-start(f32[256,128]{1,0:T(8,128)} %get-tuple-element.13), channel_id=1, source_target_pairs={{0,1},{1,2},{2,3},{3,4},{4,5},{5,6},{6,7},{8,9},{9,10},{10,11},{11... | collective-permute-start | bytes 393224 | tf_op jit(solution)/shard_map/ppermute | solution.py:584
  11.3 1.3 collective-permute-start.1
  12.6 0.0 copy-done.5
  12.7 0.6 copy.19
  13.3 0.6 pad_add_fusion.place_ref
  13.9 6.5 %prepare.1 = (f32[3,256,512]{2,1,0:T(8,128)}, f32[3,272,640]{2,1,0:T(8,128)}) custom-call(s32[3,256,512]{2,1,0:T(8,128)} %m_hi.1, f32[8]{0:T(128)} %eps_ref.3, s32[3,32,128]{2,1,0:T(8,128)} %bitcast.29, f32[32,128]{1,0:T(8,128)} %bitcast.30, s32[2]{0:T(128)} %pad_add_fusion.place_ref), custom_call_target="tpu_custom_call" | custom-call | flops 3000000000 | bytes 6000000 | tf_op jit(solution)/shard_map/prepare/pallas_call | solution.py:236
  20.5 0.0 collective-permute-done.fl_lo.fl_hi.from_left
  20.5 0.0 copy-start
  20.5 0.0 collective-permute-done.1.fr_lo.fr_hi.from_right
  20.5 0.0 copy-start.1
  20.5 0.6 copy-done
  21.1 0.1 copy-done.1
  21.2 2.0 %pack_rows.1 = (f32[48,640]{1,0:T(8,128)}, f32[48,640]{1,0:T(8,128)}) custom-call(f32[3,3,256,512]{3,2,1,0:T(8,128)} %e_in.3, f32[3,3,256,512]{3,2,1,0:T(8,128)} %e_in.3, f32[3,3,256,512]{3,2,1,0:T(8,128)} %h_in.3, f32[3,3,256,512]{3,2,1,0:T(8,128)} %h_in.3, f32[3,256,512]{2,1,0:T(8,128)} %get-tuple-element.11.s_lo.s_hi.scale_in, ...), custom_call_target="tpu_custom_call" | custom-call | tf_op jit(solution)/shard_map/pack_rows/pallas_call | solution.py:153
  23.2 1.5 collective-permute-start.2
  24.6 1.3 collective-permute-start.3
  25.9 0.0 collective-permute-done.2.from_top
  26.0 0.0 copy-start.3
  26.0 3.8 %collective-permute-done.3.from_bottom = f32[48,640]{1,0:T(8,128)S(1)} collective-permute-done((f32[48,640]{1,0:T(8,128)}, f32[48,640]{1,0:T(8,128)S(1)}, u32[]{:S(2)}, u32[]{:S(2)}) %collective-permute-start.3) | collective-permute-done | bytes 122912 | tf_op jit(solution)/shard_map/ppermute | solution.py:591
  29.7 0.0 copy-start.4
  29.7 0.0 copy-done.3
  29.7 0.6 copy-done.4
  30.4 20.5 %yee_face.1 = bf16[16,256,256]{2,1,0:T(8,128)(2,1)} custom-call(f32[3,3,256,512]{3,2,1,0:T(8,128)} %e_in.3, f32[3,3,256,512]{3,2,1,0:T(8,128)} %h_in.3, f32[3,256,512]{2,1,0:T(8,128)} %get-tuple-element.11.s_lo.s_hi.scale_in, f32[3,272,640]{2,1,0:T(8,128)} %get-tuple-element.12.grid_in, f32[256,128]{1,0:T(8,128)} %copy-done, f32[256,128]{1,0:T(8,128)} %copy-done.1, ...), custom_call_target="tpu_custom_call" | custom-call | flops 3000000000 | bytes 24000000 | tf_op jit(solution)/shard_map/yee_face/pallas_call | solution.py:477
  50.9 36.9 %all_to_all.15 = bf16[16,256,256]{2,1,0:T(8,128)(2,1)S(1)} all-to-all(bf16[16,256,256]{2,1,0:T(8,128)(2,1)} %yee_face.1), channel_id=1, replica_groups=mesh['ga'=8,'gc'=2,'gy'=8] {'ga','gc'}, dimensions={0} | all-to-all | bytes 4194304 | tf_op jit(solution)/shard_map/all_to_all | solution.py:602
  87.8 7.1 %fusion = bf16[1280,256]{0,1:T(8,128)(2,1)S(1)} fusion(bf16[4096,256]{1,0:T(8,128)(2,1)S(1)} %bitcast.26, bf16[1280,4096]{1,0:T(8,128)(2,1)} %constant.25.clone), kind=kOutput, calls=%fused_computation.1 | convolution fusion | flops 2684682240 | bytes 13238272 | tf_op jit(solution)/shard_map/dot_general | solution.py:603
  94.9 0.2 copy.12
  95.1 22.0 %all_to_all.16.rows_ref = bf16[16,80,256]{2,1,0:T(8,128)(2,1)} all-to-all(bf16[16,80,256]{2,1,0:T(8,128)(2,1)S(1)} %bitcast.24), channel_id=1, replica_groups=mesh['ga'=8,'gc'=2,'gy'=8] {'gc','gy'}, dimensions={0} | all-to-all | bytes 1310720 | tf_op jit(solution)/shard_map/all_to_all | solution.py:604
  117.2 0.0 copy-start.6
  117.2 14.5 %columns.1 = f32[1024,128]{1,0:T(8,128)} custom-call(bf16[16,80,256]{2,1,0:T(8,128)(2,1)} %all_to_all.16.rows_ref, bf16[16,256,2048]{2,1,0:T(8,128)(2,1)} %constant.26.clone.table_ref), custom_call_target="tpu_custom_call" | custom-call | tf_op jit(solution)/shard_map/columns/pallas_call | solution.py:522
  131.6 4.6 %all-to-all-start.2 = ((f32[128,8,128]{2,1,0:T(8,128)}), f32[128,8,128]{2,1,0:T(8,128)S(1)}, u32[]{:S(2)}, u32[]{:S(2)}) async-start(f32[128,8,128]{2,1,0:T(8,128)} %bitcast.25), calls=%async_computation.2 | async-start | bytes 1048576 | tf_op jit(solution)/shard_map/all_to_all | solution.py:606
  136.3 0.0 copy-done.6
  136.3 0.1 multiply_bitcast_fusion.3
  136.3 0.1 copy.13
  136.4 0.1 copy.14
  136.5 0.1 copy.15
  136.6 0.1 copy.16
  136.7 0.6 maximum_multiply_fusion.coef_ref
  137.4 20.5 %yee_fields.1 = (f32[3,3,256,512]{3,2,1,0:T(8,128)}, f32[3,3,256,512]{3,2,1,0:T(8,128)}) custom-call(f32[3,3,256,512]{3,2,1,0:T(8,128)} %e_in.3, f32[3,3,256,512]{3,2,1,0:T(8,128)} %h_in.3, f32[3,256,512]{2,1,0:T(8,128)} %get-tuple-element.11.s_lo.s_hi.scale_in, f32[3,272,640]{2,1,0:T(8,128)} %get-tuple-element.12.grid_in, f32[256,128]{1,0:T(8,128)} %copy-done, ...), custom_call_target="tpu_custom_call" | custom-call | flops 3000000000 | bytes 24000000 | tf_op jit(solution)/shard_map/yee_fields/pallas_call | solution.py:477
  157.9 0.0 all-to-all-done.2.parts_ref
  157.9 0.0 copy-start.2
  157.9 0.8 copy-done.2
  158.7 2.2 %combine.1 = f32[16,64,128]{2,1,0:T(8,128)} custom-call(f32[128,8,128]{2,1,0:T(8,128)} %copy-done.2, f32[2,4]{1,0:T(2,128)} %maximum_multiply_fusion.coef_ref, s32[2]{0:T(128)} %pad_add_fusion.place_ref), custom_call_target="tpu_custom_call" | custom-call | tf_op jit(solution)/shard_map/combine/pallas_call | solution.py:569
Async XLA Ops:
  0.6 12.0 %copy-start.5 = (s32[4096,3]{0,1:T(4,128)S(1)}, s32[4096,3]{0,1:T(4,128)}, u32[]{:S(2)}) copy-start(s32[4096,3]{0,1:T(4,128)} %param.13) | copy-start | bytes 147460
  7.4 13.0 %collective-permute-start = (f32[256,128]{1,0:T(8,128)}, f32[256,128]{1,0:T(8,128)S(1)}, u32[]{:S(2)}, u32[]{:S(2)}) collective-permute-start(f32[256,128]{1,0:T(8,128)} %get-tuple-element.13), channel_id=1, source_target_pairs={{0,1},{1,2},{2,3},{3,4},{4,5},{5,6},{6,7},{8,9},{9,10},{10,11},{11... | collective-permute-start | bytes 393224 | tf_op jit(solution)/shard_map/ppermute | solution.py:584
  11.3 9.1 %collective-permute-start.1 = (f32[256,128]{1,0:T(8,128)}, f32[256,128]{1,0:T(8,128)S(1)}, u32[]{:S(2)}, u32[]{:S(2)}) collective-permute-start(f32[256,128]{1,0:T(8,128)} %get-tuple-element.14), channel_id=1, source_target_pairs={{1,0},{2,1},{3,2},{4,3},{5,4},{6,5},{7,6},{9,8},{10,9},{11,10},{12... | collective-permute-start | bytes 393224 | tf_op jit(solution)/shard_map/ppermute | solution.py:585
  20.5 0.7 copy-start
  20.5 0.7 copy-start.1
  23.2 2.8 %collective-permute-start.2 = (f32[48,640]{1,0:T(8,128)}, f32[48,640]{1,0:T(8,128)S(1)}, u32[]{:S(2)}, u32[]{:S(2)}) collective-permute-start(f32[48,640]{1,0:T(8,128)} %get-tuple-element.15), channel_id=1, source_target_pairs={{0,8},{8,16},{16,24},{24,32},{32,40},{40,48},{48,56},{56,64},{64,7... | collective-permute-start | bytes 368648 | tf_op jit(solution)/shard_map/ppermute | solution.py:590
  24.6 5.1 %collective-permute-start.3 = (f32[48,640]{1,0:T(8,128)}, f32[48,640]{1,0:T(8,128)S(1)}, u32[]{:S(2)}, u32[]{:S(2)}) collective-permute-start(f32[48,640]{1,0:T(8,128)} %get-tuple-element.16), channel_id=1, source_target_pairs={{8,0},{16,8},{24,16},{32,24},{40,32},{48,40},{56,48},{64,56},{72,6... | collective-permute-start | bytes 368648 | tf_op jit(solution)/shard_map/ppermute | solution.py:591
  26.0 3.8 %copy-start.3 = (f32[48,640]{1,0:T(8,128)}, f32[48,640]{1,0:T(8,128)S(1)}, u32[]{:S(2)}) copy-start(f32[48,640]{1,0:T(8,128)S(1)} %collective-permute-done.2.from_top) | copy-start | bytes 368644
  29.7 0.6 copy-start.4
  117.2 19.1 %copy-start.6 = (f32[2]{0:T(128)S(1)}, f32[2]{0:T(128)}, u32[]{:S(2)}) copy-start(f32[2]{0:T(128)} %param.15) | copy-start | bytes 28
  131.6 26.2 %all-to-all-start.2 = ((f32[128,8,128]{2,1,0:T(8,128)}), f32[128,8,128]{2,1,0:T(8,128)S(1)}, u32[]{:S(2)}, u32[]{:S(2)}) async-start(f32[128,8,128]{2,1,0:T(8,128)} %bitcast.25), calls=%async_computation.2 | async-start | bytes 1048576 | tf_op jit(solution)/shard_map/all_to_all | solution.py:606
  157.9 0.8 copy-start.2

commit v2 on v1

v2 whole, which is shorter than its diff:
```python
import functools
import math

import jax
import jax.numpy as jnp
import ml_dtypes
import numpy as np
from jax import lax
from jax.experimental import pallas as pl
from jax.experimental.pallas import tpu as pltpu
from jax.sharding import Mesh, PartitionSpec as P

LZ = 3
NA = 1024
NMAT = 8
N = 4096
NSRC = 4096
ROWS = 256
COLS = 512
OFF = 8
EXT_R = 280
EXT_C = 640
TILES = 5
GROUP = 4
USED_R = 272
CHUNKS = 4
courant = 0.5
source_rate = 0.7
PERIOD = 4 * N
GX = ("ga", "gc")
MIB = 1 << 20
F32 = jnp.float32
BF16 = jnp.bfloat16


def tables():
    cell = np.arange(N, dtype=np.int64)
    t = np.arange(16)[:, None, None]
    q = np.arange(5)[None, :, None]
    m = np.arange(8)[None, None, :]
    w = (64 * m + 4 * t + q)[..., None]
    phase = np.remainder(w * cell, PERIOD) * (2.0 * math.pi / PERIOD)
    x_table = np.stack([np.cos(phase), np.sin(phase)], 2).reshape(16 * 80, N)
    v = np.arange(NA, dtype=np.int64) + NA // 4
    phase = np.remainder(cell[:, None] * v[None, :], PERIOD) * (2.0 * math.pi / PERIOD)
    y_table = np.concatenate([np.cos(phase), -np.sin(phase)], 1)
    y_table = y_table.reshape(8, 2, 256, 2 * NA).transpose(1, 0, 2, 3).reshape(16, 256, 2 * NA)
    return x_table.astype(ml_dtypes.bfloat16), y_table.astype(ml_dtypes.bfloat16)


def params(mib):
    return pltpu.CompilerParams(vmem_limit_bytes=mib * MIB)


def vmem():
    return pl.BlockSpec(memory_space=pltpu.VMEM)


def smem():
    return pl.BlockSpec(memory_space=pltpu.SMEM)


def scale_of(material, eps_ref):
    shape = (8, material.shape[-1])
    scale = None
    for k in range(NMAT):
        rate = (courant / jnp.full(shape, eps_ref[k], F32))[0:1]
        scale = rate if scale is None else jnp.where(material == k, rate, scale)
    return scale


def scale_kernel(material_ref, eps_ref, scale_ref):
    def strip(s, _):
        r = pl.multiple_of(s * 16, 16)
        for layer in range(LZ):
            scale_ref[layer, pl.ds(r, 16), :] = scale_of(
                material_ref[layer, pl.ds(r, 16), :], eps_ref
            )
        return 0

    lax.fori_loop(0, ROWS // 16, strip, 0)


def scales(material, eps):
    return pl.pallas_call(
        scale_kernel,
        in_specs=[vmem(), smem()],
        out_specs=vmem(),
        out_shape=jax.ShapeDtypeStruct((LZ, ROWS, COLS), F32),
        compiler_params=params(8),
        cost_estimate=pl.CostEstimate(
            flops=1_500_000_000, bytes_accessed=3_000_000, transcendentals=0
        ),
        name="scales",
    )(material, eps)


def pack_rows_kernel(e_lo, e_hi, h_lo, h_hi, m_lo, m_hi, eps_ref, up_ref, down_ref):
    sub = lax.broadcasted_iota(jnp.int32, (8, COLS), 0)
    up = down = None
    for a in range(7):
        for layer in range(LZ):
            index = a * LZ + layer
            if a < 3:
                lo, hi = e_lo[a, layer], e_hi[a, layer]
            elif a < 6:
                lo, hi = h_lo[a - 3, layer], h_hi[a - 3, layer]
            else:
                lo, hi = scale_of(m_lo[layer], eps_ref), scale_of(m_hi[layer], eps_ref)
            p = 2 * (index % 4)
            if p == 0:
                up = jnp.zeros((8, COLS), F32)
                down = jnp.zeros((8, COLS), F32)
            here = (sub == p) | (sub == p + 1)
            up = jnp.where(here, pltpu.roll(lo, p, 0) if p else lo, up)
            down = jnp.where(here, pltpu.roll(hi, (p + 2) % 8, 0) if p != 6 else hi, down)
            tile = index // 4
            up_ref[8 * tile : 8 * tile + 8, :] = up
            down_ref[8 * tile : 8 * tile + 8, :] = down


def pack_rows(e, h, material, eps):
    last = ROWS // 8 - 1
    lo4 = pl.BlockSpec((3, LZ, 8, COLS), lambda r: (0, 0, 0, 0))
    hi4 = pl.BlockSpec((3, LZ, 8, COLS), lambda r: (0, 0, last, 0))
    lo3 = pl.BlockSpec((LZ, 8, COLS), lambda r: (0, 0, 0))
    hi3 = pl.BlockSpec((LZ, 8, COLS), lambda r: (0, last, 0))
    out = pl.BlockSpec((48, COLS), lambda r: (0, 0))
    return pl.pallas_call(
        pack_rows_kernel,
        grid=(1,),
        in_specs=[lo4, hi4, lo4, hi4, lo3, hi3, smem()],
        out_specs=[out, out],
        out_shape=[jax.ShapeDtypeStruct((48, COLS), F32)] * 2,
        compiler_params=params(8),
        name="pack_rows",
    )(e, e, h, h, material, material, eps)


def rim_rows(packed, index, to_top):
    p, tile = 2 * (index % 4), index // 4
    value = packed[8 * tile : 8 * tile + 8, :]
    sub = lax.broadcasted_iota(jnp.int32, value.shape, 0)
    shift = (6 - p) % 8 if to_top else (8 - p) % 8
    value = pltpu.roll(value, shift, 0) if shift else value
    return jnp.where(sub >= 6 if to_top else sub < 2, value, 0.0)


def pack_cols_kernel(
    e_lo, e_hi, h_lo, h_hi, s_lo, s_hi, top_lo, top_hi, bot_lo, bot_hi, left_ref, right_ref
):
    rows = 32

    def packed(pair_of, shape):
        lane = lax.broadcasted_iota(jnp.int32, shape, 1)
        left = jnp.zeros(shape, F32)
        right = jnp.zeros(shape, F32)
        for index in range(7 * LZ):
            q = 2 * index
            lo, hi = pair_of(index)
            here = (lane == q) | (lane == q + 1)
            left = jnp.where(here, pltpu.roll(lo, q, 1) if q else lo, left)
            right = jnp.where(here, pltpu.roll(hi, q + 2, 1), right)
        return left, right

    def strip(s, _):
        r = pl.multiple_of(s * rows, rows)
        span = pl.ds(r, rows)

        def pair_of(index):
            a, layer = index // LZ, index % LZ
            if a < 3:
                return e_lo[a, layer, span, :], e_hi[a, layer, span, :]
            if a < 6:
                return h_lo[a - 3, layer, span, :], h_hi[a - 3, layer, span, :]
            return s_lo[layer, span, :], s_hi[layer, span, :]

        left, right = packed(pair_of, (rows, 128))
        target = pl.ds(pl.multiple_of(r + OFF, 8), rows)
        left_ref[target, :] = left
        right_ref[target, :] = right
        return 0

    lax.fori_loop(0, ROWS // rows, strip, 0)
    for to_top, lo, hi, r in ((True, top_lo, top_hi, 0), (False, bot_lo, bot_hi, ROWS + OFF)):
        left, right = packed(
            lambda index: (rim_rows(lo, index, to_top), rim_rows(hi, index, to_top)), (8, 128)
        )
        left_ref[r : r + 8, :] = left
        right_ref[r : r + 8, :] = right


def pack_cols(e, h, scale, from_top, from_bottom):
    end = COLS // 128 - 1
    lo4 = pl.BlockSpec((3, LZ, ROWS, 128), lambda r: (0, 0, 0, 0))
    hi4 = pl.BlockSpec((3, LZ, ROWS, 128), lambda r: (0, 0, 0, end))
    lo3 = pl.BlockSpec((LZ, ROWS, 128), lambda r: (0, 0, 0))
    hi3 = pl.BlockSpec((LZ, ROWS, 128), lambda r: (0, 0, end))
    lo2 = pl.BlockSpec((48, 128), lambda r: (0, 0))
    hi2 = pl.BlockSpec((48, 128), lambda r: (0, end))
    out = pl.BlockSpec((USED_R, 128), lambda r: (0, 0))
    return pl.pallas_call(
        pack_cols_kernel,
        grid=(1,),
        in_specs=[lo4, hi4, lo4, hi4, lo3, hi3, lo2, hi2, lo2, hi2],
        out_specs=[out, out],
        out_shape=[jax.ShapeDtypeStruct((USED_R, 128), F32)] * 2,
        compiler_params=params(16),
        name="pack_cols",
    )(e, e, h, h, scale, scale, from_top, from_top, from_bottom, from_bottom)


def rim_tile(from_left, from_right, index):
    lane = lax.broadcasted_iota(jnp.int32, from_left.shape, 1)
    q = 2 * index
    right = pltpu.roll(from_right, 128 - q, 1) if q else from_right
    left = pltpu.roll(from_left, 126 - q, 1)
    return jnp.where(lane < 2, right, jnp.where(lane >= 126, left, 0.0))


def sources_kernel(pos_ref, amp_ref, place_ref, grid_ref):
    groups = NSRC // 128
    row = pos_ref[1] - place_ref[0] * ROWS + OFF
    col = pos_ref[2] - place_ref[1] * COLS
    inside = (row >= OFF - 1) & (row <= ROWS + OFF) & (col >= -1) & (col <= COLS)
    col = jnp.where(col < 0, EXT_C - 1, col)
    taken = jnp.where(inside, 1.0, 0.0)
    lane_a = lax.broadcasted_iota(jnp.int32, (128, 128), 0)
    lane_b = lax.broadcasted_iota(jnp.int32, (128, 128), 1)
    before = jnp.where(lane_a < lane_b, 1.0, 0.0).astype(BF16)
    group_a = lax.broadcasted_iota(jnp.int32, (groups, groups), 0)
    group_b = lax.broadcasted_iota(jnp.int32, (groups, groups), 1)
    earlier = jnp.where(group_b < group_a, 1.0, 0.0).astype(BF16)
    in_group = jnp.dot(taken.astype(BF16), before, preferred_element_type=F32)
    ahead = jnp.dot(earlier, taken.astype(BF16), preferred_element_type=F32)
    rank = in_group + jnp.sum(ahead, axis=1, keepdims=True)
    rank = jnp.where(inside, rank, -1.0)
    features = (
        row.astype(F32),
        col.astype(F32),
        pos_ref[0].astype(F32),
        amp_ref[...],
    )
    count = jnp.sum(taken).astype(jnp.int32)
    slot = lax.broadcasted_iota(jnp.int32, (128, 128), 0).astype(F32)
    feature_lane = lax.broadcasted_iota(jnp.int32, (128, 128), 1)
    row_of = lax.broadcasted_iota(jnp.int32, (USED_R, 128), 0).astype(F32)
    col_of = lax.broadcasted_iota(jnp.int32, (EXT_C, 128), 0).astype(F32)
    grid_ref[...] = jnp.zeros(grid_ref.shape, F32)

    def one_pass(p, _):
        base = (p * 128).astype(F32)
        sums = [jnp.zeros((128, 128), F32) for _ in features]
        found = jnp.zeros((128, 128), F32)
        for g in range(groups):
            chosen = slot == rank[g : g + 1, :] - base
            found = jnp.where(chosen, 1.0, found)
            for f, feature in enumerate(features):
                sums[f] = jnp.where(chosen, feature[g : g + 1, :], sums[f])
        packed = jnp.zeros((128, 128), F32)
        for f, total in enumerate(sums + [found]):
            packed = jnp.where(feature_lane == f, jnp.sum(total, axis=1, keepdims=True), packed)
        packed = packed.T
        src_row, src_col, src_layer = packed[0:1], packed[1:2], packed[2:3]
        amp, valid = packed[3:4], packed[4:5]
        amp_1 = amp.astype(BF16).astype(F32)
        amp_2 = (amp - amp_1).astype(BF16).astype(F32)
        amp_3 = amp - amp_1 - amp_2
        at_col = jnp.where(col_of == src_col, 1.0, 0.0).astype(BF16)
        at_col = jnp.concatenate([at_col] * 3, 1)
        for layer in range(LZ):
            at_row = (row_of == src_row) & (src_layer == layer) & (valid > 0.0)
            weights = jnp.concatenate(
                [jnp.where(at_row, part, 0.0).astype(BF16) for part in (amp_1, amp_2, amp_3)], 1
            )
            added = lax.dot_general(
                weights, at_col, (((1,), (1,)), ((), ())), preferred_element_type=F32
            )
            for tile in range(TILES):
                grid_ref[layer, tile] += added[:, 128 * tile : 128 * tile + 128]
        return 0

    lax.fori_loop(0, (count + 127) // 128, one_pass, 0)


def sources(pos, amp, place):
    return pl.pallas_call(
        sources_kernel,
        in_specs=[vmem(), vmem(), smem()],
        out_specs=vmem(),
        out_shape=jax.ShapeDtypeStruct((LZ, TILES, USED_R, 128), F32),
        compiler_params=params(12),
        cost_estimate=pl.CostEstimate(
            flops=3_000_000_000, bytes_accessed=3_000_000, transcendentals=0
        ),
        name="sources",
    )(pos, amp, place)


def yee_kernel(
    with_fields,
    with_face,
    e_in,
    h_in,
    scale_in,
    grid_in,
    from_left,
    from_right,
    from_top,
    from_bottom,
    place_ref,
    *refs,
):
    refs = list(refs)
    e_out, h_out = (refs.pop(0), refs.pop(0)) if with_fields else (None, None)
    face_out = refs.pop(0) if with_face else None
    e, h, scale, grid = refs[:4]
    refs = refs[4:]
    first = refs.pop(0) if with_face else None
    in_sem, grid_sem, out_sem = refs
    span = ROWS // CHUNKS
    own_tiles = COLS // 128

    arrivals = []
    for chunk in range(CHUNKS):
        here = []
        source_rows = pl.ds(chunk * span, span)
        target_rows = pl.ds(OFF + chunk * span, span)
        for tile in range(own_tiles):
            cols = pl.ds(128 * tile, 128)
            pairs = (
                (e_in.at[:, :, source_rows, cols], e.at[:, :, tile, target_rows, :]),
                (h_in.at[:, :, source_rows, cols], h.at[:, :, tile, target_rows, :]),
                (scale_in.at[:, source_rows, cols], scale.at[:, tile, target_rows, :]),
            )
            for source, target in pairs:
                copy = pltpu.make_async_copy(source, target, in_sem.at[chunk, len(here)])
                copy.start()
                here.append(copy)
        arrivals.append(here)
    grid_copy = pltpu.make_async_copy(grid_in, grid, grid_sem)
    grid_copy.start()

    sub = lax.broadcasted_iota(jnp.int32, (8, 128), 0)
    lane = lax.broadcasted_iota(jnp.int32, (8, 128), 1)

    def array_of(a, layer):
        if a < 3:
            return e.at[a, layer]
        if a < 6:
            return h.at[a - 3, layer]
        return scale.at[layer]

    for index in range(7 * LZ):
        target = array_of(index // LZ, index % LZ)
        top = rim_rows(from_top, index, True)
        bottom = rim_rows(from_bottom, index, False)
        for tile in range(own_tiles):
            cols = slice(128 * tile, 128 * tile + 128)
            target[tile, 0:8, :] = top[:, cols]
            target[tile, ROWS + OFF : ROWS + OFF + 8, :] = bottom[:, cols]
        for tile in range(TILES):
            target[tile, USED_R : USED_R + 8, :] = jnp.zeros((8, 128), F32)

    def rim_strip(s, _):
        r = pl.multiple_of(s * 8, 8)
        left = from_left[pl.ds(r, 8), :]
        right = from_right[pl.ds(r, 8), :]
        for index in range(7 * LZ):
            array_of(index // LZ, index % LZ)[own_tiles, pl.ds(r, 8), :] = rim_tile(
                left, right, index
            )
        return 0

    lax.fori_loop(0, USED_R // 8, rim_strip, 0)

    row_place, col_place = place_ref[0], place_ref[1]
    rim_half = jnp.full((8, 128), courant, F32)
    rim_half = jnp.where((lane >= 64) & (col_place == 0), 0.0, rim_half)
    rim_half = jnp.where((lane < 64) & (col_place == 7), 0.0, rim_half)
    inner_half = jnp.full((8, 128), courant, F32)
    half = [inner_half] * own_tiles + [rim_half]
    half_top = [jnp.where(row_place == 0, 0.0, value) for value in half]
    half_bottom = [jnp.where(row_place == 15, 0.0, value) for value in half]

    def load(ref, a, layer, r):
        return [ref[a, layer, tile, pl.ds(r, 8), :] for tile in range(TILES)]

    def y_next(here):
        moved = [pltpu.roll(value, 127, 1) for value in here]
        return [
            jnp.where(lane == 127, moved[(tile + 1) % TILES], moved[tile]) for tile in range(TILES)
        ]

    def y_last(here):
        moved = [pltpu.roll(value, 1, 1) for value in here]
        return [
            jnp.where(lane == 0, moved[(tile - 1) % TILES], moved[tile]) for tile in range(TILES)
        ]

    zero = [jnp.zeros((8, 128), F32)] * TILES

    def update_h(r, coef):
        for layer in range(LZ):
            ex, ey, ez = (load(e, a, layer, r) for a in range(3))
            top = layer + 1 == LZ
            ex_up = zero if top else load(e, 0, layer + 1, r)
            ey_up = zero if top else load(e, 1, layer + 1, r)
            ey_x, ez_x = load(e, 1, layer, r + 1), load(e, 2, layer, r + 1)
            ex_y, ez_y = y_next(ex), y_next(ez)
            for t in range(TILES):
                curls = (
                    ez_y[t] - ez[t] - (ey_up[t] - ey[t]),
                    ex_up[t] - ex[t] - (ez_x[t] - ez[t]),
                    ey_x[t] - ey[t] - (ex_y[t] - ex[t]),
                )
                for a in range(3):
                    h[a, layer, t, pl.ds(r, 8), :] -= coef[t] * curls[a]

    def update_e(r, moment):
        strength = math.sin(source_rate * moment)
        for layer in range(LZ):
            hx, hy, hz = (load(h, a, layer, r) for a in range(3))
            hx_low = load(h, 0, layer - 1, r) if layer else zero
            hy_low = load(h, 1, layer - 1, r) if layer else zero
            if isinstance(r, int) and r == 0:
                hy_x = [pltpu.roll(value, 1, 0) for value in hy]
                hz_x = [pltpu.roll(value, 1, 0) for value in hz]
            else:
                hy_x, hz_x = load(h, 1, layer, r - 1), load(h, 2, layer, r - 1)
            hx_y, hz_y = y_last(hx), y_last(hz)
            for t in range(TILES):
                rows = pl.ds(r, 8)
                rate = scale[layer, t, rows, :]
                e[0, layer, t, rows, :] += rate * (hz[t] - hz_y[t] - (hy[t] - hy_low[t]))
                e[1, layer, t, rows, :] += rate * (hx[t] - hx_low[t] - (hz[t] - hz_x[t]))
                e[2, layer, t, rows, :] = (
                    e[2, layer, t, rows, :]
                    + rate * (hy[t] - hy_x[t] - (hx[t] - hx_y[t]))
                    + strength * grid[layer, t, rows, :]
                )

    face_of = ((h, 1, -1.0), (h, 0, 1.0), (e, 1, 1.0), (e, 0, -1.0))

    def first_step(s, _):
        r = pl.multiple_of(s * 8, 8)
        update_h(r, half)
        update_e(r, 1.0)
        if with_face:
            for k, (ref, a, _sign) in enumerate(face_of):
                for tile in range(own_tiles):
                    first[k, tile, pl.ds(pl.multiple_of(r - OFF, 8), 8), :] = ref[
                        a, 1, tile, pl.ds(r, 8), :
                    ]
        return 0

    def second_step(s, _):
        own = pl.multiple_of(s * 16, 16)
        for part in range(2):
            r = pl.multiple_of(own + OFF + 8 * part, 8)
            update_h(r, half)
            update_e(r, 2.0)
        if with_face:
            now_rows = pl.ds(pl.multiple_of(own + OFF, 8), 16)
            for k, (ref, a, sign) in enumerate(face_of):
                for tile in range(own_tiles):
                    then = first[k, tile, pl.ds(own, 16), :]
                    now = ref[a, 1, tile, now_rows, :]
                    cols = pl.ds(128 * (tile % 2), 128)
                    target = 4 * k + tile // 2
                    face_out[target, pl.ds(own, 16), cols] = (sign * (then + now)).astype(BF16)
                    face_out[target + 2, pl.ds(own, 16), cols] = (sign * (then - now)).astype(BF16)
        return 0

    strips = span // 8
    for copy in arrivals[0]:
        copy.wait()
    grid_copy.wait()
    update_h(0, half_top)
    update_e(0, 1.0)
    for chunk in range(CHUNKS):
        begin = 1 + chunk * strips
        if chunk + 1 < CHUNKS:
            lax.fori_loop(begin, begin + strips - 1, first_step, 0)
            for copy in arrivals[chunk + 1]:
                copy.wait()
            first_step(jnp.int32(begin + strips - 1), 0)
        else:
            lax.fori_loop(begin, begin + strips, first_step, 0)
    update_h(ROWS + OFF, half_bottom)
    update_e(ROWS + OFF, 1.0)

    update_h(0, half_top)
    sent = []
    for chunk in range(CHUNKS):
        lax.fori_loop(chunk * (span // 16), (chunk + 1) * (span // 16), second_step, 0)
        if with_fields:
            source_rows = pl.ds(OFF + chunk * span, span)
            target_rows = pl.ds(chunk * span, span)
            for tile in range(own_tiles):
                cols = pl.ds(128 * tile, 128)
                for source, target in ((e, e_out), (h, h_out)):
                    copy = pltpu.make_async_copy(
                        source.at[:, :, tile, source_rows, :],
                        target.at[:, :, target_rows, cols],
                        out_sem.at[len(sent)],
                    )
                    copy.start()
                    sent.append(copy)
    for copy in sent:
        copy.wait()


def yee(with_fields, with_face, e, h, scale, grid, rims, place):
    field = jax.ShapeDtypeStruct((3, LZ, ROWS, COLS), F32)
    anywhere = pl.BlockSpec(memory_space=pl.ANY)
    out_shape = []
    out_specs = []
    scratch = [
        pltpu.VMEM((3, LZ, TILES, EXT_R, 128), F32),
        pltpu.VMEM((3, LZ, TILES, EXT_R, 128), F32),
        pltpu.VMEM((LZ, TILES, EXT_R, 128), F32),
        pltpu.VMEM((LZ, TILES, USED_R, 128), F32),
    ]
    if with_fields:
        out_shape += [field, field]
        out_specs += [anywhere, anywhere]
    if with_face:
        out_shape.append(jax.ShapeDtypeStruct((16, ROWS, 256), BF16))
        out_specs.append(vmem())
        scratch.append(pltpu.VMEM((4, COLS // 128, ROWS, 128), F32))
    scratch += [
        pltpu.SemaphoreType.DMA((CHUNKS, 3 * COLS // 128)),
        pltpu.SemaphoreType.DMA,
        pltpu.SemaphoreType.DMA((CHUNKS * 2 * COLS // 128,)),
    ]
    return pl.pallas_call(
        functools.partial(yee_kernel, with_fields, with_face),
        in_specs=[anywhere] * 4 + [vmem()] * 4 + [smem()],
        out_specs=out_specs,
        out_shape=out_shape,
        scratch_shapes=scratch,
        compiler_params=params(28),
        cost_estimate=pl.CostEstimate(
            flops=5_000_000_000, bytes_accessed=40_000_000, transcendentals=0
        ),
        name="yee_fields" if with_fields else "yee_face",
    )(e, h, scale, grid, *rims, place)


def rows_kernel(field_ref, table_ref, out_ref):
    total = jnp.dot(table_ref[...], field_ref[...], preferred_element_type=F32)
    out_ref[...] = total.astype(BF16)


def rows_transform(field, table):
    step = 320
    return pl.pallas_call(
        rows_kernel,
        grid=(1280 // step,),
        in_specs=[
            pl.BlockSpec((N, 256), lambda t: (0, 0)),
            pl.BlockSpec((step, N), lambda t: (t, 0)),
        ],
        out_specs=pl.BlockSpec((step, 256), lambda t: (t, 0)),
        out_shape=jax.ShapeDtypeStruct((1280, 256), BF16),
        compiler_params=params(16),
        name="rows_transform",
    )(field, table)


def columns_kernel(rows_ref, table_ref, out_ref, total, spread):
    step = pl.program_id(0)
    part = jnp.dot(rows_ref[0], table_ref[0], preferred_element_type=F32)
    for g in range(1, GROUP):
        part += jnp.dot(rows_ref[g], table_ref[g], preferred_element_type=F32)

    @pl.when(step == 0)
    def _():
        total[...] = part

    @pl.when(step > 0)
    def _():
        total[...] += part

    @pl.when(step == 16 // GROUP - 1)
    def _():
        sub = lax.broadcasted_iota(jnp.int32, (8, NA), 0)

        def flip(value):
            value = pltpu.roll(value, 4, 0)
            value = jnp.where(sub % 4 < 2, pltpu.roll(value, 6, 0), pltpu.roll(value, 2, 0))
            return jnp.where(sub % 2 == 0, pltpu.roll(value, 7, 0), pltpu.roll(value, 1, 0))

        for q in range(4):
            for plus in (True, False):
                base = 16 * (q if plus else 4 - q)
                cos_re, cos_im = total[base : base + 8, 0:NA], total[base : base + 8, NA : 2 * NA]
                sin_re = total[base + 8 : base + 16, 0:NA]
                sin_im = total[base + 8 : base + 16, NA : 2 * NA]
                if plus:
                    parts = (cos_re + sin_im, cos_im - sin_re)
                else:
                    parts = (flip(cos_re - sin_im), flip(cos_im + sin_re))
                for ri, value in enumerate(parts):
                    for j in range(8):
                        start = ((8 if plus else 0) * 8 + j) * 8 + 2 * q + ri
                        spread[pl.ds(start, 8, stride=64), :] = value[:, 128 * j : 128 * j + 128]
        out_ref[...] = spread[...].astype(BF16)


def columns(rows, table):
    return pl.pallas_call(
        columns_kernel,
        grid=(16 // GROUP,),
        in_specs=[
            pl.BlockSpec((GROUP, 80, 256), lambda t: (t, 0, 0)),
            pl.BlockSpec((GROUP, 256, 2 * NA), lambda t: (t, 0, 0)),
        ],
        out_specs=pl.BlockSpec((1024, 128), lambda t: (0, 0)),
        out_shape=jax.ShapeDtypeStruct((1024, 128), BF16),
        scratch_shapes=[pltpu.VMEM((80, 2 * NA), F32), pltpu.VMEM((1024, 128), F32)],
        compiler_params=params(24),
        name="columns",
    )(rows, table)


def combine_kernel(parts_ref, coef_ref, place_ref, out_ref):
    sub = lax.broadcasted_iota(jnp.int32, (8, 128), 0)
    real_row = (sub % 2) == 0
    side = jnp.where(real_row, -1.0, 1.0)

    def swap(value):
        return jnp.where(real_row, pltpu.roll(value, 7, 0), pltpu.roll(value, 1, 0)) * side

    def two_blocks(pair, _):
        for comp in range(4):
            totals = parts_ref[(2 * comp) * 8 + pair].astype(F32)
            changes = parts_ref[(2 * comp + 1) * 8 + pair].astype(F32)
            for odd in range(2):
                t = 2 * pair + odd
                where = jnp.where(place_ref[0] >= 8, t, 15 - t)
                total = totals[8 * odd : 8 * odd + 8]
                change = changes[8 * odd : 8 * odd + 8]
                total_swap, change_swap = swap(total), swap(change)
                for f in range(2):
                    value = (
                        coef_ref[f, 0] * total
                        + coef_ref[f, 1] * total_swap
                        + coef_ref[f, 3] * change
                        - coef_ref[f, 2] * change_swap
                    )
                    item = f * 4 + comp
                    for q in range(4):
                        out_ref[where, 16 * q + 2 * item : 16 * q + 2 * item + 2, :] = value[
                            2 * q : 2 * q + 2, :
                        ]
        return 0

    lax.fori_loop(0, 8, two_blocks, 0)


def combine(parts, coef, place):
    return pl.pallas_call(
        combine_kernel,
        in_specs=[vmem(), smem(), smem()],
        out_specs=vmem(),
        out_shape=jax.ShapeDtypeStruct((16, 64, 128), F32),
        compiler_params=params(8),
        name="combine",
    )(parts, coef, place)


def on_device(x_table, y_table, e, h, material, eps, src_pos, src_amp, freqs):
    row_place = lax.axis_index(GX)
    col_place = lax.axis_index("gy")
    place = jnp.stack([row_place, col_place]).astype(jnp.int32)
    up, down = pack_rows(e, h, material, eps)
    from_top = lax.ppermute(down, GX, [(k, k + 1) for k in range(15)])
    from_bottom = lax.ppermute(up, GX, [(k + 1, k) for k in range(15)])
    scale = scales(material, eps)
    left, right = pack_cols(e, h, scale, from_top, from_bottom)
    from_left = lax.ppermute(right, "gy", [(k, k + 1) for k in range(7)])
    from_right = lax.ppermute(left, "gy", [(k + 1, k) for k in range(7)])
    pos = src_pos.T.reshape(3, NSRC // 128, 128)
    amp = src_amp.reshape(NSRC // 128, 128)
    pos, amp, left = lax.optimization_barrier((pos, amp, left))
    grid = sources(pos, amp, place)
    rims = (from_left, from_right, from_top, from_bottom)
    (face,) = yee(False, True, e, h, scale, grid, rims, place)
    e_out, h_out = yee(True, False, e, h, scale, grid, rims, place)

    half = jnp.cos(freqs * 0.5), jnp.sin(freqs * 0.5)
    turn = jnp.cos(freqs * 1.5), jnp.sin(freqs * 1.5)
    coef = jnp.stack(
        [turn[0] * half[0], turn[1] * half[0], turn[0] * half[1], turn[1] * half[1]], 1
    ) * (1.0 / N)

    face = lax.all_to_all(face, GX, 0, 0, tiled=True)
    face, e_out, h_out = lax.optimization_barrier((face, e_out, h_out))
    rows = rows_transform(face.reshape(N, 256), x_table)
    rows = lax.all_to_all(rows.reshape(16, 80, 256), ("gc", "gy"), 0, 0, tiled=True)
    far = columns(rows, y_table)
    far = lax.all_to_all(far.reshape(128, 8, 128), GX + ("gy",), 0, 0, tiled=True)
    far = combine(far.reshape(64, 16, 128), coef, place)
    return e_out, h_out, far.reshape(64, 8, 2, 128)


def solution(mesh):
    fine = Mesh(mesh.devices.reshape(8, 2, 8), ("ga", "gc", "gy"))
    field = P(None, None, GX, "gy")
    placed = (P(), P(), field, field, P(None, GX, "gy"), P(), P(), P(), P())
    mapped = jax.shard_map(
        on_device,
        mesh=fine,
        in_specs=placed,
        out_specs=(field, field, P(GX, None, None, "gy")),
        check_vma=False,
    )
    x_table, y_table = tables()

    def program(e_field, h_field, material, eps_table, src_pos, src_amp, freqs):
        return mapped(
            x_table, y_table, e_field, h_field, material, eps_table, src_pos, src_amp, freqs
        )

    return program
```

time: 162 us -> 152 us (0.938)
  blocking collectives: 58.9 us -> 26.1 us
  local copies, waits for them, and re-layouts: 3.38 us -> 31.9 us
  Pallas kernels: 73.1 us -> 54.1 us
  starting transfers between devices: 12.6 us -> 24.1 us
  waiting for transfers between devices: 3.77 us -> 14.3 us
  matrix products: 7.09 us -> 0 us
    all_to_all x1 -> x0, blocking collectives: 36.9 us -> none  [on_device(): face = lax.all_to_all(face, GX, 0, 0, tiled=True)]
    unnamed x15 -> x43, local copies, waits for them, and re-layouts: 2.77 us -> 31.5 us
    pallas_call x3 -> x5, Pallas kernels: 27.8 us -> 14.8 us  [the longest x1 4.77 us: columns(): pl.pallas_call(columns_kernel, grid=(16 // GROUP,), in_specs=[pl.BlockSpe...]
    all_to_all x1, waiting for transfers between devices: 0.01 us -> 10.1 us  [on_device(): lax.all_to_all(far.reshape(128, 8, 128), GX + ('gy',), 0, 0, tiled=True)]
    all_to_all x0 -> x1, starting transfers between devices: none -> 8.55 us  [on_device(): face = lax.all_to_all(face, GX, 0, 0, tiled=True)]
    dot_general x1 -> x0, matrix products: 7.09 us -> none  [on_device(): jnp.dot(x_table, face.reshape(N, 256), preferred_element_type=F32)]
    all_to_all x1, blocking collectives: 22 us -> 26.1 us  [on_device(): lax.all_to_all(rows.reshape(16, 80, 256), ('gc', 'gy'), 0, 0, tiled=True)]
    pallas_call x2, Pallas kernels: 41.1 us -> 37 us  [yee(): pl.pallas_call(functools.partial(yee_kernel, with_fields, with_face), in_...]
  transfers between devices with their start and end apart: 5 -> 6, of which waited for: 1 -> 3; matrix products, arithmetic and copies ran while one was open for 1% -> 0% of each run, Pallas kernels for 17% -> 15%
where the time goes in v2:
time: 152 us
  Pallas kernels  54.1 us (36%)
  local copies, waits for them, and re-layouts  31.9 us (21%)
  blocking collectives  26.1 us (17%)
  starting transfers between devices  24.1 us (16%)
  waiting for transfers between devices  14.3 us (9%)
    pallas_call x2, Pallas kernels, yee(): pl.pallas_call(functools.partial(yee_kernel, with_fields, with_face), in_...  37 us
    unnamed x43, local copies, waits for them, and re-layouts  31.5 us
    all_to_all x1, blocking collectives, on_device(): lax.all_to_all(rows.reshape(16, 80, 256), ('gc', 'gy'), 0, 0, tiled=True)  26.1 us
    all_to_all x1, waiting for transfers between devices, on_device(): lax.all_to_all(far.reshape(128, 8, 128), GX + ('gy',), 0, 0, tiled=True)  10.1 us
    all_to_all x1, starting transfers between devices, on_device(): face = lax.all_to_all(face, GX, 0, 0, tiled=True)  8.55 us
    all_to_all x1, starting transfers between devices, on_device(): lax.all_to_all(far.reshape(128, 8, 128), GX + ('gy',), 0, 0, tiled=True)  6.73 us
    ppermute x1, starting transfers between devices, on_device(): from_left = lax.ppermute(right, 'gy', [(k, k + 1) for k in range(7)])  4.82 us
    pallas_call x1, Pallas kernels, columns(): pl.pallas_call(columns_kernel, grid=(16 // GROUP,), in_specs=[pl.BlockSpe...  4.77 us
  transfers between devices with their start and end apart: 6, of which 3 were waited for; matrix products, arithmetic and copies ran while one was open for 0% of the time, Pallas kernels for 15%

profile of v2, /device:TPU:0, one launch (start us, length us, event | category | flops | bytes accessed | tf_op | source)
XLA Modules:
  0.0 151.7 jit_solution(14393061798337436202)
XLA Ops:
  0.6 0.0 copy-start
  0.6 2.3 %copy-done = f32[3,3,256,512]{3,2,1,0:T(8,128)S(1)} copy-done((f32[3,3,256,512]{3,2,1,0:T(8,128)S(1)}, f32[3,3,256,512]{3,2,1,0:T(8,128)}, u32[]{:S(2)}) %copy-start) | copy-done | bytes 4718616
  3.0 2.3 %copy-done.3 = f32[3,3,256,512]{3,2,1,0:T(8,128)S(1)} copy-done((f32[3,3,256,512]{3,2,1,0:T(8,128)S(1)}, f32[3,3,256,512]{3,2,1,0:T(8,128)}, u32[]{:S(2)}) %copy-start.3) | copy-done | bytes 4718616
  5.3 1.4 copy-done.9
  6.7 0.7 copy-done.13
  7.4 0.7 pack_rows.1
  8.0 0.0 copy-start.17
  8.0 1.4 collective-permute-start
  9.5 1.3 collective-permute-start.1
  10.8 1.4 scales.1.s_lo.s_hi.scale_in
  12.2 0.0 copy-start.10
  12.3 0.1 pad_add_fusion.place_ref
  12.3 0.0 collective-permute-done.top_lo.top_hi.from_top
  12.3 2.2 %collective-permute-done.1.bot_lo.bot_hi.from_bottom = f32[48,512]{1,0:T(8,128)S(1)} collective-permute-done((f32[48,512]{1,0:T(8,128)S(1)}, f32[48,512]{1,0:T(8,128)S(1)}, u32[]{:S(2)}, u32[]{:S(2)}) %collective-permute-start.1) | collective-permute-done | bytes 98336 | tf_op jit(solution)/shard_map/ppermute | solution.py:680
  14.6 2.3 %copy-done.1 = f32[3,3,256,512]{3,2,1,0:T(8,128)S(1)} copy-done((f32[3,3,256,512]{3,2,1,0:T(8,128)S(1)}, f32[3,3,256,512]{3,2,1,0:T(8,128)}, u32[]{:S(2)}) %copy-start.1) | copy-done | bytes 4718616
  16.9 2.3 %copy-done.4 = f32[3,3,256,512]{3,2,1,0:T(8,128)S(1)} copy-done((f32[3,3,256,512]{3,2,1,0:T(8,128)S(1)}, f32[3,3,256,512]{3,2,1,0:T(8,128)}, u32[]{:S(2)}) %copy-start.4) | copy-done | bytes 4718616
  19.2 2.6 %pack_cols.1 = (f32[272,128]{1,0:T(8,128)S(1)}, f32[272,128]{1,0:T(8,128)S(1)}) custom-call(f32[3,3,256,512]{3,2,1,0:T(8,128)S(1)} %copy-done.1, f32[3,3,256,512]{3,2,1,0:T(8,128)S(1)} %copy-done.1, f32[3,3,256,512]{3,2,1,0:T(8,128)S(1)} %copy-done.4, f32[3,3,256,512]{3,2,1,0:T(8,128)S(1)} %copy-done.4, f32[3,256,512]{2,1,0:T(8,128)S(1)} %scales.1.s_lo.s_hi.scale_in, ...), custom_call_target="tpu_custom_call" | custom-call | tf_op jit(solution)/shard_map/pack_cols/pallas_call | solution.py:202
  21.9 1.3 collective-permute-start.3
  23.2 0.0 slice-start
  23.2 0.0 copy-start.5
  23.2 4.8 %collective-permute-start.2 = (f32[272,128]{1,0:T(8,128)S(1)}, f32[272,128]{1,0:T(8,128)S(1)}, u32[]{:S(2)}, u32[]{:S(2)}) collective-permute-start(f32[272,128]{1,0:T(8,128)S(1)} %get-tuple-element.19), channel_id=1, source_target_pairs={{0,1},{1,2},{2,3},{3,4},{4,5},{5,6},{6,7},{8,9},{9,10},{10,11},{11... | collective-permute-start | bytes 417800 | tf_op jit(solution)/shard_map/ppermute | solution.py:683
  28.0 2.6 %sources.1.grid_in = f32[3,5,272,128]{3,2,1,0:T(8,128)S(1)} custom-call(s32[3,32,128]{2,1,0:T(8,128)S(1)} %bitcast.26, f32[32,128]{1,0:T(8,128)S(1)} %bitcast.27, s32[2]{0:T(128)S(1)} %pad_add_fusion.place_ref), custom_call_target="tpu_custom_call" | custom-call | flops 3000000000 | bytes 3000000 | tf_op jit(solution)/shard_map/sources/pallas_call | solution.py:287
  30.6 0.0 collective-permute-done.3.from_right
  30.7 17.9 %yee_face.1 = bf16[16,256,256]{2,1,0:T(8,128)(2,1)S(1)} custom-call(f32[3,3,256,512]{3,2,1,0:T(8,128)S(1)} %bitcast.22, f32[3,3,256,512]{3,2,1,0:T(8,128)S(1)} %copy-done.5, f32[3,256,512]{2,1,0:T(8,128)S(1)} %scales.1.s_lo.s_hi.scale_in, f32[3,5,272,128]{3,2,1,0:T(8,128)S(1)} %sources.1.grid_in, f32[272,128]{1,0:T(8,128)S(1)} %collective-permute-done.2.from_left, ...), custom_call_target="tpu_custom_call" | custom-call | flops 5000000000 | bytes 40000000 | tf_op jit(solution)/shard_map/yee_face/pallas_call | solution.py:537
  48.6 1.3 copy-done.12
  50.0 1.3 copy-done.15
  51.3 8.6 %all-to-all-start = ((bf16[16,256,256]{2,1,0:T(8,128)(2,1)}), bf16[16,256,256]{2,1,0:T(8,128)(2,1)S(1)}, u32[]{:S(2)}, u32[]{:S(2)}) async-start(bf16[16,256,256]{2,1,0:T(8,128)(2,1)} %copy-done.12), calls=%async_computation | async-start | bytes 4194304 | tf_op jit(solution)/shard_map/all_to_all | solution.py:699
  59.9 0.0 copy-start.2
  59.9 2.3 %copy-done.2 = f32[3,3,256,512]{3,2,1,0:T(8,128)S(1)} copy-done((f32[3,3,256,512]{3,2,1,0:T(8,128)S(1)}, f32[3,3,256,512]{3,2,1,0:T(8,128)}, u32[]{:S(2)}) %copy-start.2) | copy-done | bytes 4718616
  62.2 2.3 %copy-done.6 = f32[3,3,256,512]{3,2,1,0:T(8,128)S(1)} copy-done((f32[3,3,256,512]{3,2,1,0:T(8,128)S(1)}, f32[3,3,256,512]{3,2,1,0:T(8,128)}, u32[]{:S(2)}) %copy-start.6) | copy-done | bytes 4718616
  64.5 1.4 copy-done.11
  65.9 1.6 %copy-done.16 = f32[3,5,272,128]{3,2,1,0:T(8,128)S(1)} copy-done((f32[3,5,272,128]{3,2,1,0:T(8,128)S(1)}, f32[3,5,272,128]{3,2,1,0:T(8,128)}, u32[]{:S(2)}) %copy-start.16) | copy-done | bytes 2088984
  67.5 19.1 %yee_fields.1 = (f32[3,3,256,512]{3,2,1,0:T(8,128)}, f32[3,3,256,512]{3,2,1,0:T(8,128)}) custom-call(f32[3,3,256,512]{3,2,1,0:T(8,128)S(1)} %copy-done.2, f32[3,3,256,512]{3,2,1,0:T(8,128)S(1)} %copy-done.6, f32[3,256,512]{2,1,0:T(8,128)S(1)} %copy-done.11, f32[3,5,272,128]{3,2,1,0:T(8,128)S(1)} %copy-done.16, ...), custom_call_target="tpu_custom_call" | custom-call | flops 5000000000 | bytes 40000000 | tf_op jit(solution)/shard_map/yee_fields/pallas_call | solution.py:537
  86.6 2.0 %all-to-all-done = bf16[16,256,256]{2,1,0:T(8,128)(2,1)S(1)} async-done(((bf16[16,256,256]{2,1,0:T(8,128)(2,1)}), bf16[16,256,256]{2,1,0:T(8,128)(2,1)S(1)}, u32[]{:S(2)}, u32[]{:S(2)}) %all-to-all-start) | async-done | bytes 2097184 | tf_op jit(solution)/shard_map/all_to_all | solution.py:699
  88.6 4.0 %copy-done.8 = bf16[1280,4096]{1,0:T(8,128)(2,1)S(1)} copy-done((bf16[1280,4096]{1,0:T(8,128)(2,1)S(1)}, bf16[1280,4096]{1,0:T(8,128)(2,1)}, u32[]{:S(2)}) %copy-start.8) | copy-done | bytes 10485784
  92.6 3.4 %rows_transform.1 = bf16[1280,256]{1,0:T(8,128)(2,1)S(1)} custom-call(bf16[4096,256]{1,0:T(8,128)(2,1)S(1)} %bitcast.23, bf16[1280,4096]{1,0:T(8,128)(2,1)S(1)} %copy-done.8), custom_call_target="tpu_custom_call" | custom-call | tf_op jit(solution)/shard_map/rows_transform/pallas_call | solution.py:558
  96.0 26.1 %all_to_all.15.rows_ref = bf16[16,80,256]{2,1,0:T(8,128)(2,1)S(1)} all-to-all(bf16[16,80,256]{2,1,0:T(8,128)(2,1)S(1)} %bitcast.24), channel_id=1, replica_groups=mesh['ga'=8,'gc'=2,'gy'=8] {'gc','gy'}, dimensions={0} | all-to-all | bytes 1310720 | tf_op jit(solution)/shard_map/all_to_all | solution.py:702
  122.1 5.8 %copy-done.7 = bf16[16,256,2048]{2,1,0:T(8,128)(2,1)S(1)} copy-done((bf16[16,256,2048]{2,1,0:T(8,128)(2,1)S(1)}, bf16[16,256,2048]{2,1,0:T(8,128)(2,1)}, u32[]{:S(2)}) %copy-start.7) | copy-done | bytes 16777240
  127.9 4.8 %columns.1 = bf16[1024,128]{1,0:T(8,128)(2,1)} custom-call(bf16[16,80,256]{2,1,0:T(8,128)(2,1)S(1)} %all_to_all.15.rows_ref, bf16[16,256,2048]{2,1,0:T(8,128)(2,1)S(1)} %copy-done.7), custom_call_target="tpu_custom_call" | custom-call | tf_op jit(solution)/shard_map/columns/pallas_call | solution.py:613
  132.6 6.7 %all-to-all-start.2 = ((bf16[128,8,128]{2,1,0:T(8,128)(2,1)}), bf16[128,8,128]{2,1,0:T(8,128)(2,1)S(1)}, u32[]{:S(2)}, u32[]{:S(2)}) async-start(bf16[128,8,128]{2,1,0:T(8,128)(2,1)} %bitcast.6), calls=%async_computation.2 | async-start | bytes 524288 | tf_op jit(solution)/shard_map/all_to_all | solution.py:704
  139.4 0.1 multiply_bitcast_fusion.3
  139.4 0.1 copy.12
  139.5 0.1 copy.13
  139.6 0.1 copy.14
  139.7 0.1 copy.15
  139.8 0.1 maximum_multiply_fusion.coef_ref
  139.9 10.1 %all-to-all-done.2 = bf16[128,8,128]{2,1,0:T(8,128)(2,1)S(1)} async-done(((bf16[128,8,128]{2,1,0:T(8,128)(2,1)}), bf16[128,8,128]{2,1,0:T(8,128)(2,1)S(1)}, u32[]{:S(2)}, u32[]{:S(2)}) %all-to-all-start.2) | async-done | bytes 262176 | tf_op jit(solution)/shard_map/all_to_all | solution.py:704
  150.0 1.7 %combine.1 = f32[16,64,128]{2,1,0:T(8,128)} custom-call(bf16[64,16,128]{2,1,0:T(8,128)(2,1)S(1)} %bitcast.25, f32[2,4]{1,0:T(2,128)S(1)} %maximum_multiply_fusion.coef_ref, s32[2]{0:T(128)S(1)} %pad_add_fusion.place_ref), custom_call_target="tpu_custom_call" | custom-call | tf_op jit(solution)/shard_map/combine/pallas_call | solution.py:664
  (25 shorter events, 0.0 us)
Async XLA Ops:
  0.6 2.3 %copy-start = (f32[3,3,256,512]{3,2,1,0:T(8,128)S(1)}, f32[3,3,256,512]{3,2,1,0:T(8,128)}, u32[]{:S(2)}) copy-start(f32[3,3,256,512]{3,2,1,0:T(8,128)} %e_in.3) | copy-start | bytes 14155780
  3.0 2.3 %copy-start.3 = (f32[3,3,256,512]{3,2,1,0:T(8,128)S(1)}, f32[3,3,256,512]{3,2,1,0:T(8,128)}, u32[]{:S(2)}) copy-start(f32[3,3,256,512]{3,2,1,0:T(8,128)} %h_in.3) | copy-start | bytes 14155780
  5.3 1.4 copy-start.9
  6.7 0.7 copy-start.13
  8.0 4.2 %copy-start.17 = (s32[4096,3]{0,1:T(4,128)S(1)}, s32[4096,3]{0,1:T(4,128)}, u32[]{:S(2)}) copy-start(s32[4096,3]{0,1:T(4,128)} %param.13) | copy-start | bytes 147460
  8.0 4.3 %collective-permute-start = (f32[48,512]{1,0:T(8,128)S(1)}, f32[48,512]{1,0:T(8,128)S(1)}, u32[]{:S(2)}, u32[]{:S(2)}) collective-permute-start(f32[48,512]{1,0:T(8,128)S(1)} %get-tuple-element.14), channel_id=1, source_target_pairs={{0,8},{8,16},{16,24},{24,32},{32,40},{40,48},{48,56},{56,64},{64,7... | collective-permute-start | bytes 294920 | tf_op jit(solution)/shard_map/ppermute | solution.py:679
  9.5 5.1 %collective-permute-start.1 = (f32[48,512]{1,0:T(8,128)S(1)}, f32[48,512]{1,0:T(8,128)S(1)}, u32[]{:S(2)}, u32[]{:S(2)}) collective-permute-start(f32[48,512]{1,0:T(8,128)S(1)} %get-tuple-element.15), channel_id=1, source_target_pairs={{8,0},{16,8},{24,16},{32,24},{40,32},{48,40},{56,48},{64,56},{72,6... | collective-permute-start | bytes 294920 | tf_op jit(solution)/shard_map/ppermute | solution.py:680
  12.2 18.5 %copy-start.10 = (f32[3,256,512]{2,1,0:T(8,128)}, f32[3,256,512]{2,1,0:T(8,128)S(1)}, u32[]{:S(2)}) copy-start(f32[3,256,512]{2,1,0:T(8,128)S(1)} %scales.1.s_lo.s_hi.scale_in) | copy-start | bytes 4718596
  14.6 2.3 %copy-start.1 = (f32[3,3,256,512]{3,2,1,0:T(8,128)S(1)}, f32[3,3,256,512]{3,2,1,0:T(8,128)}, u32[]{:S(2)}) copy-start(f32[3,3,256,512]{3,2,1,0:T(8,128)} %e_in.3) | copy-start | bytes 14155780
  16.9 2.3 %copy-start.4 = (f32[3,3,256,512]{3,2,1,0:T(8,128)S(1)}, f32[3,3,256,512]{3,2,1,0:T(8,128)}, u32[]{:S(2)}) copy-start(f32[3,3,256,512]{3,2,1,0:T(8,128)} %h_in.3) | copy-start | bytes 14155780
  19.2 8.8 %copy-start.14 = (f32[4096]{0:T(1024)S(1)}, f32[4096]{0:T(1024)}, u32[]{:S(2)}) copy-start(f32[4096]{0:T(1024)} %param.14) | copy-start | bytes 49156
  21.9 8.8 %collective-permute-start.3 = (f32[272,128]{1,0:T(8,128)S(1)}, f32[272,128]{1,0:T(8,128)S(1)}, u32[]{:S(2)}, u32[]{:S(2)}) collective-permute-start(f32[272,128]{1,0:T(8,128)S(1)} %get-tuple-element.16), channel_id=1, source_target_pairs={{1,0},{2,1},{3,2},{4,3},{5,4},{6,5},{7,6},{9,8},{10,9},{11,10},{12... | collective-permute-start | bytes 417800 | tf_op jit(solution)/shard_map/ppermute | solution.py:684
  23.2 7.5 %slice-start = ((s8[4718592]{0:T(1024)(128)(4,1)}), s8[4194304]{0:T(1024)(128)(4,1)S(1)}, s32[]{:S(2)}) async-start(s8[4718592]{0:T(1024)(128)(4,1)} %bitcast.21), calls=%async_computation.3 | async-start | bytes 8388608
  23.2 7.5 %slice-start.1 = ((s8[4718592]{0:T(1024)(128)(4,1)}), s8[524288]{0:T(1024)(128)(4,1)S(1)}, s32[]{:S(2)}) async-start(s8[4718592]{0:T(1024)(128)(4,1)} %bitcast.21), calls=%async_computation.4 | async-start | bytes 1048576
  23.2 7.5 %copy-start.5 = (f32[3,3,256,512]{3,2,1,0:T(8,128)S(1)}, f32[3,3,256,512]{3,2,1,0:T(8,128)}, u32[]{:S(2)}) copy-start(f32[3,3,256,512]{3,2,1,0:T(8,128)} %h_in.3) | copy-start | bytes 14155780
  23.2 7.4 %collective-permute-start.2 = (f32[272,128]{1,0:T(8,128)S(1)}, f32[272,128]{1,0:T(8,128)S(1)}, u32[]{:S(2)}, u32[]{:S(2)}) collective-permute-start(f32[272,128]{1,0:T(8,128)S(1)} %get-tuple-element.19), channel_id=1, source_target_pairs={{0,1},{1,2},{2,3},{3,4},{4,5},{5,6},{6,7},{8,9},{9,10},{10,11},{11... | collective-permute-start | bytes 417800 | tf_op jit(solution)/shard_map/ppermute | solution.py:683
  48.6 1.4 copy-start.12
  50.0 1.3 copy-start.15
  51.3 37.3 %all-to-all-start = ((bf16[16,256,256]{2,1,0:T(8,128)(2,1)}), bf16[16,256,256]{2,1,0:T(8,128)(2,1)S(1)}, u32[]{:S(2)}, u32[]{:S(2)}) async-start(bf16[16,256,256]{2,1,0:T(8,128)(2,1)} %copy-done.12), calls=%async_computation | async-start | bytes 4194304 | tf_op jit(solution)/shard_map/all_to_all | solution.py:699
  59.9 2.3 %copy-start.2 = (f32[3,3,256,512]{3,2,1,0:T(8,128)S(1)}, f32[3,3,256,512]{3,2,1,0:T(8,128)}, u32[]{:S(2)}) copy-start(f32[3,3,256,512]{3,2,1,0:T(8,128)} %e_in.3) | copy-start | bytes 14155780
  62.2 2.3 %copy-start.6 = (f32[3,3,256,512]{3,2,1,0:T(8,128)S(1)}, f32[3,3,256,512]{3,2,1,0:T(8,128)}, u32[]{:S(2)}) copy-start(f32[3,3,256,512]{3,2,1,0:T(8,128)} %h_in.3) | copy-start | bytes 14155780
  64.5 1.4 copy-start.11
  65.9 1.6 %copy-start.16 = (f32[3,5,272,128]{3,2,1,0:T(8,128)S(1)}, f32[3,5,272,128]{3,2,1,0:T(8,128)}, u32[]{:S(2)}) copy-start(f32[3,5,272,128]{3,2,1,0:T(8,128)} %copy-done.15) | copy-start | bytes 6266884
  88.6 4.0 %copy-start.8 = (bf16[1280,4096]{1,0:T(8,128)(2,1)S(1)}, bf16[1280,4096]{1,0:T(8,128)(2,1)}, u32[]{:S(2)}) copy-start(bf16[1280,4096]{1,0:T(8,128)(2,1)} %constant.25.clone.table_ref) | copy-start | bytes 31457284
  122.1 5.8 %copy-start.7 = (bf16[16,256,2048]{2,1,0:T(8,128)(2,1)S(1)}, bf16[16,256,2048]{2,1,0:T(8,128)(2,1)}, u32[]{:S(2)}) copy-start(bf16[16,256,2048]{2,1,0:T(8,128)(2,1)} %constant.26.clone.table_ref) | copy-start | bytes 50331652
  127.9 11.5 %copy-start.18 = (f32[2]{0:T(128)S(1)}, f32[2]{0:T(128)}, u32[]{:S(2)}) copy-start(f32[2]{0:T(128)} %param.15) | copy-start | bytes 28
  132.6 17.4 %all-to-all-start.2 = ((bf16[128,8,128]{2,1,0:T(8,128)(2,1)}), bf16[128,8,128]{2,1,0:T(8,128)(2,1)S(1)}, u32[]{:S(2)}, u32[]{:S(2)}) async-start(bf16[128,8,128]{2,1,0:T(8,128)(2,1)} %bitcast.6), calls=%async_computation.2 | async-start | bytes 524288 | tf_op jit(solution)/shard_map/all_to_all | solution.py:704

commit v3 on v2

--- a/solution.py
+++ b/solution.py
@@ -23,7 +23,7 @@
 TILES = 5
 GROUP = 4
 USED_R = 272
-CHUNKS = 4
+CHUNKS = 2
 courant = 0.5
 source_rate = 0.7
 PERIOD = 4 * N
@@ -50,6 +50,10 @@
 
 def params(mib):
     return pltpu.CompilerParams(vmem_limit_bytes=mib * MIB)
+
+
+def stay(*arrays):
+    return [pltpu.with_memory_space_constraint(array, pltpu.HBM) for array in arrays]
 
 
 def vmem():
@@ -134,7 +138,7 @@
         out_shape=[jax.ShapeDtypeStruct((48, COLS), F32)] * 2,
         compiler_params=params(8),
         name="pack_rows",
-    )(e, e, h, h, material, material, eps)
+    )(*stay(e, e, h, h, material, material), eps)
 
 
 def rim_rows(packed, index, to_top):
@@ -153,15 +157,12 @@
 
     def packed(pair_of, shape):
         lane = lax.broadcasted_iota(jnp.int32, shape, 1)
-        left = jnp.zeros(shape, F32)
-        right = jnp.zeros(shape, F32)
+        both = jnp.zeros(shape, F32)
         for index in range(7 * LZ):
-            q = 2 * index
             lo, hi = pair_of(index)
-            here = (lane == q) | (lane == q + 1)
-            left = jnp.where(here, pltpu.roll(lo, q, 1) if q else lo, left)
-            right = jnp.where(here, pltpu.roll(hi, q + 2, 1), right)
-        return left, right
+            ends = pltpu.roll(jnp.where(lane < 64, lo, hi), 4 * index + 2, 1)
+            both = jnp.where(lane // 4 == index, ends, both)
+        return jnp.where(lane % 4 >= 2, both, 0.0), jnp.where(lane % 4 < 2, both, 0.0)
 
     def strip(s, _):
         r = pl.multiple_of(s * rows, rows)
@@ -207,15 +208,13 @@
         out_shape=[jax.ShapeDtypeStruct((USED_R, 128), F32)] * 2,
         compiler_params=params(16),
         name="pack_cols",
-    )(e, e, h, h, scale, scale, from_top, from_top, from_bottom, from_bottom)
-
-
-def rim_tile(from_left, from_right, index):
-    lane = lax.broadcasted_iota(jnp.int32, from_left.shape, 1)
-    q = 2 * index
-    right = pltpu.roll(from_right, 128 - q, 1) if q else from_right
-    left = pltpu.roll(from_left, 126 - q, 1)
-    return jnp.where(lane < 2, right, jnp.where(lane >= 126, left, 0.0))
+    )(*stay(e, e, h, h), scale, scale, from_top, from_top, from_bottom, from_bottom)
+
+
+def rim_tile(both, index):
+    lane = lax.broadcasted_iota(jnp.int32, both.shape, 1)
+    moved = pltpu.roll(both, (126 - 4 * index) % 128, 1)
+    return jnp.where((lane < 2) | (lane >= 126), moved, 0.0)
 
 
 def sources_kernel(pos_ref, amp_ref, place_ref, grid_ref):
@@ -363,16 +362,13 @@
             target[tile, USED_R : USED_R + 8, :] = jnp.zeros((8, 128), F32)
 
     def rim_strip(s, _):
-        r = pl.multiple_of(s * 8, 8)
-        left = from_left[pl.ds(r, 8), :]
-        right = from_right[pl.ds(r, 8), :]
+        r = pl.multiple_of(s * 16, 16)
+        both = from_left[pl.ds(r, 16), :] + from_right[pl.ds(r, 16), :]
         for index in range(7 * LZ):
-            array_of(index // LZ, index % LZ)[own_tiles, pl.ds(r, 8), :] = rim_tile(
-                left, right, index
-            )
+            array_of(index // LZ, index % LZ)[own_tiles, pl.ds(r, 16), :] = rim_tile(both, index)
         return 0
 
-    lax.fori_loop(0, USED_R // 8, rim_strip, 0)
+    lax.fori_loop(0, USED_R // 16, rim_strip, 0, unroll=2)
 
     row_place, col_place = place_ref[0], place_ref[1]
     rim_half = jnp.full((8, 128), courant, F32)
@@ -400,52 +396,73 @@
 
     zero = [jnp.zeros((8, 128), F32)] * TILES
 
-    def update_h(r, coef):
+    every = frozenset((a, layer) for a in range(3) for layer in range(LZ))
+    if with_fields:
+        first_e = last_h = last_e = every
+    else:
+        last_e = frozenset(((0, 1), (1, 1)))
+        last_h = frozenset(((0, 0), (1, 0), (0, 1), (1, 1), (2, 1)))
+        first_e = every - {(2, 2)}
+
+    def update_h(r, coef, wanted=every):
         for layer in range(LZ):
+            if not any((a, layer) in wanted for a in range(3)):
+                continue
             ex, ey, ez = (load(e, a, layer, r) for a in range(3))
             top = layer + 1 == LZ
-            ex_up = zero if top else load(e, 0, layer + 1, r)
-            ey_up = zero if top else load(e, 1, layer + 1, r)
-            ey_x, ez_x = load(e, 1, layer, r + 1), load(e, 2, layer, r + 1)
-            ex_y, ez_y = y_next(ex), y_next(ez)
+            if (0, layer) in wanted:
+                ey_up = zero if top else load(e, 1, layer + 1, r)
+                ez_y = y_next(ez)
+            if (1, layer) in wanted:
+                ex_up = zero if top else load(e, 0, layer + 1, r)
+                ez_x = load(e, 2, layer, r + 1)
+            if (2, layer) in wanted:
+                ey_x, ex_y = load(e, 1, layer, r + 1), y_next(ex)
             for t in range(TILES):
-                curls = (
-                    ez_y[t] - ez[t] - (ey_up[t] - ey[t]),
-                    ex_up[t] - ex[t] - (ez_x[t] - ez[t]),
-                    ey_x[t] - ey[t] - (ex_y[t] - ex[t]),
-                )
-                for a in range(3):
-                    h[a, layer, t, pl.ds(r, 8), :] -= coef[t] * curls[a]
-
-    def update_e(r, moment):
+                rows = pl.ds(r, 8)
+                if (0, layer) in wanted:
+                    h[0, layer, t, rows, :] -= coef[t] * (ez_y[t] - ez[t] - (ey_up[t] - ey[t]))
+                if (1, layer) in wanted:
+                    h[1, layer, t, rows, :] -= coef[t] * (ex_up[t] - ex[t] - (ez_x[t] - ez[t]))
+                if (2, layer) in wanted:
+                    h[2, layer, t, rows, :] -= coef[t] * (ey_x[t] - ey[t] - (ex_y[t] - ex[t]))
+
+    def update_e(r, moment, wanted, tiles):
         strength = math.sin(source_rate * moment)
         for layer in range(LZ):
+            if not any((a, layer) in wanted for a in range(3)):
+                continue
             hx, hy, hz = (load(h, a, layer, r) for a in range(3))
-            hx_low = load(h, 0, layer - 1, r) if layer else zero
-            hy_low = load(h, 1, layer - 1, r) if layer else zero
-            if isinstance(r, int) and r == 0:
-                hy_x = [pltpu.roll(value, 1, 0) for value in hy]
-                hz_x = [pltpu.roll(value, 1, 0) for value in hz]
-            else:
-                hy_x, hz_x = load(h, 1, layer, r - 1), load(h, 2, layer, r - 1)
-            hx_y, hz_y = y_last(hx), y_last(hz)
-            for t in range(TILES):
+            edge = isinstance(r, int) and r == 0
+            if (0, layer) in wanted:
+                hy_low = load(h, 1, layer - 1, r) if layer else zero
+                hz_y = y_last(hz)
+            if (1, layer) in wanted:
+                hx_low = load(h, 0, layer - 1, r) if layer else zero
+                hz_x = [pltpu.roll(v, 1, 0) for v in hz] if edge else load(h, 2, layer, r - 1)
+            if (2, layer) in wanted:
+                hy_x = [pltpu.roll(v, 1, 0) for v in hy] if edge else load(h, 1, layer, r - 1)
+                hx_y = y_last(hx)
+            for t in range(tiles):
                 rows = pl.ds(r, 8)
                 rate = scale[layer, t, rows, :]
-                e[0, layer, t, rows, :] += rate * (hz[t] - hz_y[t] - (hy[t] - hy_low[t]))
-                e[1, layer, t, rows, :] += rate * (hx[t] - hx_low[t] - (hz[t] - hz_x[t]))
-                e[2, layer, t, rows, :] = (
-                    e[2, layer, t, rows, :]
-                    + rate * (hy[t] - hy_x[t] - (hx[t] - hx_y[t]))
-                    + strength * grid[layer, t, rows, :]
-                )
+                if (0, layer) in wanted:
+                    e[0, layer, t, rows, :] += rate * (hz[t] - hz_y[t] - (hy[t] - hy_low[t]))
+                if (1, layer) in wanted:
+                    e[1, layer, t, rows, :] += rate * (hx[t] - hx_low[t] - (hz[t] - hz_x[t]))
+                if (2, layer) in wanted:
+                    e[2, layer, t, rows, :] = (
+                        e[2, layer, t, rows, :]
+                        + rate * (hy[t] - hy_x[t] - (hx[t] - hx_y[t]))
+                        + strength * grid[layer, t, rows, :]
+                    )
 
     face_of = ((h, 1, -1.0), (h, 0, 1.0), (e, 1, 1.0), (e, 0, -1.0))
 
     def first_step(s, _):
         r = pl.multiple_of(s * 8, 8)
         update_h(r, half)
-        update_e(r, 1.0)
+        update_e(r, 1.0, first_e, TILES)
         if with_face:
             for k, (ref, a, _sign) in enumerate(face_of):
                 for tile in range(own_tiles):
@@ -458,8 +475,8 @@
         own = pl.multiple_of(s * 16, 16)
         for part in range(2):
             r = pl.multiple_of(own + OFF + 8 * part, 8)
-            update_h(r, half)
-            update_e(r, 2.0)
+            update_h(r, half, last_h)
+            update_e(r, 2.0, last_e, own_tiles)
         if with_face:
             now_rows = pl.ds(pl.multiple_of(own + OFF, 8), 16)
             for k, (ref, a, sign) in enumerate(face_of):
@@ -477,23 +494,23 @@
         copy.wait()
     grid_copy.wait()
     update_h(0, half_top)
-    update_e(0, 1.0)
+    update_e(0, 1.0, first_e, TILES)
     for chunk in range(CHUNKS):
         begin = 1 + chunk * strips
         if chunk + 1 < CHUNKS:
-            lax.fori_loop(begin, begin + strips - 1, first_step, 0)
+            lax.fori_loop(begin, begin + strips - 1, first_step, 0, unroll=2)
             for copy in arrivals[chunk + 1]:
                 copy.wait()
             first_step(jnp.int32(begin + strips - 1), 0)
         else:
-            lax.fori_loop(begin, begin + strips, first_step, 0)
+            lax.fori_loop(begin, begin + strips, first_step, 0, unroll=2)
     update_h(ROWS + OFF, half_bottom)
-    update_e(ROWS + OFF, 1.0)
-
-    update_h(0, half_top)
+    update_e(ROWS + OFF, 1.0, first_e, TILES)
+
+    update_h(0, half_top, last_h)
     sent = []
     for chunk in range(CHUNKS):
-        lax.fori_loop(chunk * (span // 16), (chunk + 1) * (span // 16), second_step, 0)
+        lax.fori_loop(chunk * (span // 16), (chunk + 1) * (span // 16), second_step, 0, unroll=2)
         if with_fields:
             source_rows = pl.ds(OFF + chunk * span, span)
             target_rows = pl.ds(chunk * span, span)
@@ -545,7 +562,7 @@
             flops=5_000_000_000, bytes_accessed=40_000_000, transcendentals=0
         ),
         name="yee_fields" if with_fields else "yee_face",
-    )(e, h, scale, grid, *rims, place)
+    )(*stay(e, h), scale, grid, *rims, place)
 
 
 def rows_kernel(field_ref, table_ref, out_ref):
@@ -566,7 +583,7 @@
         out_shape=jax.ShapeDtypeStruct((1280, 256), BF16),
         compiler_params=params(16),
         name="rows_transform",
-    )(field, table)
+    )(field, *stay(table))
 
 
 def columns_kernel(rows_ref, table_ref, out_ref, total, spread):
@@ -622,7 +639,7 @@
         scratch_shapes=[pltpu.VMEM((80, 2 * NA), F32), pltpu.VMEM((1024, 128), F32)],
         compiler_params=params(24),
         name="columns",
-    )(rows, table)
+    )(rows, *stay(table))
 
 
 def combine_kernel(parts_ref, coef_ref, place_ref, out_ref):

time: 152 us -> 132 us (0.87)
  local copies, waits for them, and re-layouts: 31.9 us -> 6.79 us
  waiting for transfers between devices: 14.3 us -> 23.9 us
  Pallas kernels: 54.1 us -> 49.6 us
    unnamed x43 -> x21, local copies, waits for them, and re-layouts: 31.5 us -> 6.42 us
    pallas_call x2, Pallas kernels: 37 us -> 23.8 us  [yee(): pl.pallas_call(functools.partial(yee_kernel, with_fields, with_face), in_...]
    all_to_all x1, waiting for transfers between devices: 1.96 us -> 11.5 us  [on_device(): face = lax.all_to_all(face, GX, 0, 0, tiled=True)]
    pallas_call x1, Pallas kernels: 4.77 us -> 8.85 us  [columns(): pl.pallas_call(columns_kernel, grid=(16 // GROUP,), in_specs=[pl.BlockSpe...]
    pallas_call x1, Pallas kernels: 3.39 us -> 6.24 us  [rows_transform(): pl.pallas_call(rows_kernel, grid=(1280 // step,), in_specs=[pl.BlockSpec(...]
  transfers between devices with their start and end apart: 6 -> 6, of which waited for: 3 -> 3; matrix products, arithmetic and copies ran while one was open for 0% -> 0% of each run, Pallas kernels for 15% -> 14%
where the time goes in v3:
time: 132 us; the launch traced here: 131 us
  Pallas kernels  49.6 us (38%)
  blocking collectives  26.1 us (20%)
  waiting for transfers between devices  23.9 us (18%)
  starting transfers between devices  23.8 us (18%)
  local copies, waits for them, and re-layouts  6.79 us (5%)
    all_to_all x1, blocking collectives, on_device(): lax.all_to_all(rows.reshape(16, 80, 256), ('gc', 'gy'), 0, 0, tiled=True)  26.1 us
    pallas_call x2, Pallas kernels, yee(): pl.pallas_call(functools.partial(yee_kernel, with_fields, with_face), in_...  23.8 us
    all_to_all x1, waiting for transfers between devices, on_device(): face = lax.all_to_all(face, GX, 0, 0, tiled=True)  11.5 us
    all_to_all x1, waiting for transfers between devices, on_device(): lax.all_to_all(far.reshape(128, 8, 128), GX + ('gy',), 0, 0, tiled=True)  10.1 us
    pallas_call x1, Pallas kernels, columns(): pl.pallas_call(columns_kernel, grid=(16 // GROUP,), in_specs=[pl.BlockSpe...  8.85 us
    all_to_all x1, starting transfers between devices, on_device(): face = lax.all_to_all(face, GX, 0, 0, tiled=True)  8.54 us
    all_to_all x1, starting transfers between devices, on_device(): lax.all_to_all(far.reshape(128, 8, 128), GX + ('gy',), 0, 0, tiled=True)  6.72 us
    unnamed x21, local copies, waits for them, and re-layouts  6.42 us
  transfers between devices with their start and end apart: 6, of which 3 were waited for; matrix products, arithmetic and copies ran while one was open for 0% of the time, Pallas kernels for 14%

profile of v3, /device:TPU:0, one launch (start us, length us, event | category | flops | bytes accessed | tf_op | source)
XLA Modules:
  0.0 131.3 jit_solution(10519176264917931229)
XLA Ops:
  0.6 0.0 copy-start
  0.6 0.0 copy-start.4
  0.7 0.8 copy-done.4
  1.4 1.3 pack_rows.1
  2.7 0.0 copy-start.8
  2.7 1.4 %collective-permute-start = (f32[48,512]{1,0:T(8,128)S(1)}, f32[48,512]{1,0:T(8,128)S(1)}, u32[]{:S(2)}, u32[]{:S(2)}) collective-permute-start(f32[48,512]{1,0:T(8,128)S(1)} %get-tuple-element.14), channel_id=1, source_target_pairs={{0,8},{8,16},{16,24},{24,32},{32,40},{40,48},{48,56},{56,64},{64,7... | collective-permute-start | bytes 294920 | tf_op jit(solution)/shard_map/ppermute | solution.py:696
  4.1 1.3 collective-permute-start.1
  5.4 0.0 copy-done
  5.4 1.4 %scales.1.s_lo.s_hi.scale_in = f32[3,256,512]{2,1,0:T(8,128)S(1)} custom-call(s32[3,256,512]{2,1,0:T(8,128)S(1)} %copy-done, f32[8]{0:T(128)S(1)} %copy-done.4), custom_call_target="tpu_custom_call" | custom-call | flops 1500000000 | bytes 3000000 | tf_op jit(solution)/shard_map/scales/pallas_call | solution.py:89
  6.9 0.0 copy-start.1
  6.9 0.0 copy-done.8
  6.9 0.1 pad_add_fusion.place_ref
  7.0 0.0 copy-start.5
  7.0 0.0 collective-permute-done.top_lo.top_hi.from_top
  7.0 2.2 %collective-permute-done.1.bot_lo.bot_hi.from_bottom = f32[48,512]{1,0:T(8,128)S(1)} collective-permute-done((f32[48,512]{1,0:T(8,128)S(1)}, f32[48,512]{1,0:T(8,128)S(1)}, u32[]{:S(2)}, u32[]{:S(2)}) %collective-permute-start.1) | collective-permute-done | bytes 98336 | tf_op jit(solution)/shard_map/ppermute | solution.py:697
  9.2 3.8 %pack_cols.1 = (f32[272,128]{1,0:T(8,128)S(1)}, f32[272,128]{1,0:T(8,128)S(1)}) custom-call(f32[3,3,256,512]{3,2,1,0:T(8,128)} %e_in.3, f32[3,3,256,512]{3,2,1,0:T(8,128)} %e_in.3, f32[3,3,256,512]{3,2,1,0:T(8,128)} %h_in.3, f32[3,3,256,512]{3,2,1,0:T(8,128)} %h_in.3, f32[3,256,512]{2,1,0:T(8,128)S(1)} %scales.1.s_lo.s_hi.scale_in, ...), custom_call_target="tpu_custom_call" | custom-call | tf_op jit(solution)/shard_map/pack_cols/pallas_call | solution.py:203
  13.0 1.3 collective-permute-start.3
  14.3 4.6 %collective-permute-start.2 = (f32[272,128]{1,0:T(8,128)S(1)}, f32[272,128]{1,0:T(8,128)S(1)}, u32[]{:S(2)}, u32[]{:S(2)}) collective-permute-start(f32[272,128]{1,0:T(8,128)S(1)} %get-tuple-element.19), channel_id=1, source_target_pairs={{0,1},{1,2},{2,3},{3,4},{4,5},{5,6},{6,7},{8,9},{9,10},{10,11},{11... | collective-permute-start | bytes 417800 | tf_op jit(solution)/shard_map/ppermute | solution.py:700
  18.8 0.0 copy-done.5
  18.9 2.6 %sources.1.grid_in = f32[3,5,272,128]{3,2,1,0:T(8,128)S(1)} custom-call(s32[3,32,128]{2,1,0:T(8,128)S(1)} %bitcast.24, f32[32,128]{1,0:T(8,128)S(1)} %bitcast.25, s32[2]{0:T(128)S(1)} %pad_add_fusion.place_ref), custom_call_target="tpu_custom_call" | custom-call | flops 3000000000 | bytes 3000000 | tf_op jit(solution)/shard_map/sources/pallas_call | solution.py:286
  21.5 0.0 collective-permute-done.3.from_right
  21.5 0.0 collective-permute-done.2.from_left
  21.5 0.0 copy-done.1
  21.5 9.6 %yee_face.1 = bf16[16,256,256]{2,1,0:T(8,128)(2,1)S(1)} custom-call(f32[3,3,256,512]{3,2,1,0:T(8,128)} %e_in.3, f32[3,3,256,512]{3,2,1,0:T(8,128)} %h_in.3, f32[3,256,512]{2,1,0:T(8,128)S(1)} %scales.1.s_lo.s_hi.scale_in, f32[3,5,272,128]{3,2,1,0:T(8,128)S(1)} %sources.1.grid_in, f32[272,128]{1,0:T(8,128)S(1)} %collective-permute-done.2.from_left, ...), custom_call_target="tpu_custom_call" | custom-call | flops 5000000000 | bytes 40000000 | tf_op jit(solution)/shard_map/yee_face/pallas_call | solution.py:554
  31.1 0.0 copy-start.3
  31.1 1.3 %copy-done.3 = bf16[16,256,256]{2,1,0:T(8,128)(2,1)} copy-done((bf16[16,256,256]{2,1,0:T(8,128)(2,1)}, bf16[16,256,256]{2,1,0:T(8,128)(2,1)S(1)}, u32[]{:S(2)}) %copy-start.3) | copy-done | bytes 2097176
  32.4 0.0 copy-start.6
  32.4 1.3 copy-done.6
  33.7 8.5 %all-to-all-start = ((bf16[16,256,256]{2,1,0:T(8,128)(2,1)}), bf16[16,256,256]{2,1,0:T(8,128)(2,1)S(1)}, u32[]{:S(2)}, u32[]{:S(2)}) async-start(bf16[16,256,256]{2,1,0:T(8,128)(2,1)} %copy-done.3), calls=%async_computation | async-start | bytes 4194304 | tf_op jit(solution)/shard_map/all_to_all | solution.py:716
  42.3 0.0 copy-start.2
  42.3 1.4 %copy-done.2 = f32[3,256,512]{2,1,0:T(8,128)S(1)} copy-done((f32[3,256,512]{2,1,0:T(8,128)S(1)}, f32[3,256,512]{2,1,0:T(8,128)}, u32[]{:S(2)}) %copy-start.2) | copy-done | bytes 1572888
  43.7 0.0 copy-start.7
  43.7 1.6 %copy-done.7 = f32[3,5,272,128]{3,2,1,0:T(8,128)S(1)} copy-done((f32[3,5,272,128]{3,2,1,0:T(8,128)S(1)}, f32[3,5,272,128]{3,2,1,0:T(8,128)}, u32[]{:S(2)}) %copy-start.7) | copy-done | bytes 2088984
  45.3 14.2 %yee_fields.1 = (f32[3,3,256,512]{3,2,1,0:T(8,128)}, f32[3,3,256,512]{3,2,1,0:T(8,128)}) custom-call(f32[3,3,256,512]{3,2,1,0:T(8,128)} %e_in.3, f32[3,3,256,512]{3,2,1,0:T(8,128)} %h_in.3, f32[3,256,512]{2,1,0:T(8,128)S(1)} %copy-done.2, f32[3,5,272,128]{3,2,1,0:T(8,128)S(1)} %copy-done.7, f32[272,128]{1,0:T(8,128)S(1)} %collective-permute-done.2.from_left, ...), custom_call_target="tpu_custom_call" | custom-call | flops 5000000000 | bytes 40000000 | tf_op jit(solution)/shard_map/yee_fields/pallas_call | solution.py:554
  59.5 11.5 %all-to-all-done = bf16[16,256,256]{2,1,0:T(8,128)(2,1)S(1)} async-done(((bf16[16,256,256]{2,1,0:T(8,128)(2,1)}), bf16[16,256,256]{2,1,0:T(8,128)(2,1)S(1)}, u32[]{:S(2)}, u32[]{:S(2)}) %all-to-all-start) | async-done | bytes 2097184 | tf_op jit(solution)/shard_map/all_to_all | solution.py:716
  71.1 6.2 %rows_transform.1 = bf16[1280,256]{1,0:T(8,128)(2,1)S(1)} custom-call(bf16[4096,256]{1,0:T(8,128)(2,1)S(1)} %bitcast.21, bf16[1280,4096]{1,0:T(8,128)(2,1)} %constant.25.clone.table_ref), custom_call_target="tpu_custom_call" | custom-call | tf_op jit(solution)/shard_map/rows_transform/pallas_call | solution.py:575
  77.3 26.1 %all_to_all.15.rows_ref = bf16[16,80,256]{2,1,0:T(8,128)(2,1)S(1)} all-to-all(bf16[16,80,256]{2,1,0:T(8,128)(2,1)S(1)} %bitcast.22), channel_id=1, replica_groups=mesh['ga'=8,'gc'=2,'gy'=8] {'gc','gy'}, dimensions={0} | all-to-all | bytes 1310720 | tf_op jit(solution)/shard_map/all_to_all | solution.py:719
  103.4 8.8 %columns.1 = bf16[1024,128]{1,0:T(8,128)(2,1)} custom-call(bf16[16,80,256]{2,1,0:T(8,128)(2,1)S(1)} %all_to_all.15.rows_ref, bf16[16,256,2048]{2,1,0:T(8,128)(2,1)} %constant.26.clone.table_ref), custom_call_target="tpu_custom_call" | custom-call | tf_op jit(solution)/shard_map/columns/pallas_call | solution.py:630
  112.3 6.7 %all-to-all-start.2 = ((bf16[128,8,128]{2,1,0:T(8,128)(2,1)}), bf16[128,8,128]{2,1,0:T(8,128)(2,1)S(1)}, u32[]{:S(2)}, u32[]{:S(2)}) async-start(bf16[128,8,128]{2,1,0:T(8,128)(2,1)} %bitcast.6), calls=%async_computation.2 | async-start | bytes 524288 | tf_op jit(solution)/shard_map/all_to_all | solution.py:721
  119.0 0.0 copy-done.9
  119.0 0.1 multiply_bitcast_fusion.3
  119.1 0.1 copy.12
  119.2 0.1 copy.13
  119.2 0.1 copy.14
  119.3 0.1 copy.15
  119.4 0.1 maximum_multiply_fusion.coef_ref
  119.5 10.1 %all-to-all-done.2 = bf16[128,8,128]{2,1,0:T(8,128)(2,1)S(1)} async-done(((bf16[128,8,128]{2,1,0:T(8,128)(2,1)}), bf16[128,8,128]{2,1,0:T(8,128)(2,1)S(1)}, u32[]{:S(2)}, u32[]{:S(2)}) %all-to-all-start.2) | async-done | bytes 262176 | tf_op jit(solution)/shard_map/all_to_all | solution.py:721
  129.7 1.7 %combine.1 = f32[16,64,128]{2,1,0:T(8,128)} custom-call(bf16[64,16,128]{2,1,0:T(8,128)(2,1)S(1)} %bitcast.23, f32[2,4]{1,0:T(2,128)S(1)} %maximum_multiply_fusion.coef_ref, s32[2]{0:T(128)S(1)} %pad_add_fusion.place_ref), custom_call_target="tpu_custom_call" | custom-call | tf_op jit(solution)/shard_map/combine/pallas_call | solution.py:681
  (2 shorter events, 0.0 us)
Async XLA Ops:
  0.6 4.8 %copy-start = (s32[3,256,512]{2,1,0:T(8,128)S(1)}, s32[3,256,512]{2,1,0:T(8,128)}, u32[]{:S(2)}) copy-start(s32[3,256,512]{2,1,0:T(8,128)} %m_hi.1) | copy-start | bytes 4718596
  0.6 0.8 copy-start.4
  2.7 4.2 %copy-start.8 = (s32[4096,3]{0,1:T(4,128)S(1)}, s32[4096,3]{0,1:T(4,128)}, u32[]{:S(2)}) copy-start(s32[4096,3]{0,1:T(4,128)} %param.13) | copy-start | bytes 147460
  2.7 4.3 %collective-permute-start = (f32[48,512]{1,0:T(8,128)S(1)}, f32[48,512]{1,0:T(8,128)S(1)}, u32[]{:S(2)}, u32[]{:S(2)}) collective-permute-start(f32[48,512]{1,0:T(8,128)S(1)} %get-tuple-element.14), channel_id=1, source_target_pairs={{0,8},{8,16},{16,24},{24,32},{32,40},{40,48},{48,56},{56,64},{64,7... | collective-permute-start | bytes 294920 | tf_op jit(solution)/shard_map/ppermute | solution.py:696
  4.1 5.1 %collective-permute-start.1 = (f32[48,512]{1,0:T(8,128)S(1)}, f32[48,512]{1,0:T(8,128)S(1)}, u32[]{:S(2)}, u32[]{:S(2)}) collective-permute-start(f32[48,512]{1,0:T(8,128)S(1)} %get-tuple-element.15), channel_id=1, source_target_pairs={{8,0},{16,8},{24,16},{32,24},{40,32},{48,40},{56,48},{64,56},{72,6... | collective-permute-start | bytes 294920 | tf_op jit(solution)/shard_map/ppermute | solution.py:697
  6.9 14.6 %copy-start.1 = (f32[3,256,512]{2,1,0:T(8,128)}, f32[3,256,512]{2,1,0:T(8,128)S(1)}, u32[]{:S(2)}) copy-start(f32[3,256,512]{2,1,0:T(8,128)S(1)} %scales.1.s_lo.s_hi.scale_in) | copy-start | bytes 4718596
  7.0 11.9 %copy-start.5 = (f32[4096]{0:T(1024)S(1)}, f32[4096]{0:T(1024)}, u32[]{:S(2)}) copy-start(f32[4096]{0:T(1024)} %param.14) | copy-start | bytes 49156
  13.0 8.5 %collective-permute-start.3 = (f32[272,128]{1,0:T(8,128)S(1)}, f32[272,128]{1,0:T(8,128)S(1)}, u32[]{:S(2)}, u32[]{:S(2)}) collective-permute-start(f32[272,128]{1,0:T(8,128)S(1)} %get-tuple-element.16), channel_id=1, source_target_pairs={{1,0},{2,1},{3,2},{4,3},{5,4},{6,5},{7,6},{9,8},{10,9},{11,10},{12... | collective-permute-start | bytes 417800 | tf_op jit(solution)/shard_map/ppermute | solution.py:701
  14.3 7.2 %collective-permute-start.2 = (f32[272,128]{1,0:T(8,128)S(1)}, f32[272,128]{1,0:T(8,128)S(1)}, u32[]{:S(2)}, u32[]{:S(2)}) collective-permute-start(f32[272,128]{1,0:T(8,128)S(1)} %get-tuple-element.19), channel_id=1, source_target_pairs={{0,1},{1,2},{2,3},{3,4},{4,5},{5,6},{6,7},{8,9},{9,10},{10,11},{11... | collective-permute-start | bytes 417800 | tf_op jit(solution)/shard_map/ppermute | solution.py:700
  31.1 1.3 %copy-start.3 = (bf16[16,256,256]{2,1,0:T(8,128)(2,1)}, bf16[16,256,256]{2,1,0:T(8,128)(2,1)S(1)}, u32[]{:S(2)}) copy-start(bf16[16,256,256]{2,1,0:T(8,128)(2,1)S(1)} %yee_face.1) | copy-start | bytes 6291460
  32.4 1.3 copy-start.6
  33.7 37.3 %all-to-all-start = ((bf16[16,256,256]{2,1,0:T(8,128)(2,1)}), bf16[16,256,256]{2,1,0:T(8,128)(2,1)S(1)}, u32[]{:S(2)}, u32[]{:S(2)}) async-start(bf16[16,256,256]{2,1,0:T(8,128)(2,1)} %copy-done.3), calls=%async_computation | async-start | bytes 4194304 | tf_op jit(solution)/shard_map/all_to_all | solution.py:716
  42.3 1.4 %copy-start.2 = (f32[3,256,512]{2,1,0:T(8,128)S(1)}, f32[3,256,512]{2,1,0:T(8,128)}, u32[]{:S(2)}) copy-start(f32[3,256,512]{2,1,0:T(8,128)} %copy-done.1) | copy-start | bytes 4718596
  43.7 1.6 %copy-start.7 = (f32[3,5,272,128]{3,2,1,0:T(8,128)S(1)}, f32[3,5,272,128]{3,2,1,0:T(8,128)}, u32[]{:S(2)}) copy-start(f32[3,5,272,128]{3,2,1,0:T(8,128)} %copy-done.6) | copy-start | bytes 6266884
  103.4 15.6 %copy-start.9 = (f32[2]{0:T(128)S(1)}, f32[2]{0:T(128)}, u32[]{:S(2)}) copy-start(f32[2]{0:T(128)} %param.15) | copy-start | bytes 28
  112.3 17.4 %all-to-all-start.2 = ((bf16[128,8,128]{2,1,0:T(8,128)(2,1)}), bf16[128,8,128]{2,1,0:T(8,128)(2,1)S(1)}, u32[]{:S(2)}, u32[]{:S(2)}) async-start(bf16[128,8,128]{2,1,0:T(8,128)(2,1)} %bitcast.6), calls=%async_computation.2 | async-start | bytes 524288 | tf_op jit(solution)/shard_map/all_to_all | solution.py:721

commit v4 on v3

--- a/solution.py
+++ b/solution.py
@@ -21,7 +21,6 @@
 EXT_R = 280
 EXT_C = 640
 TILES = 5
-GROUP = 4
 USED_R = 272
 CHUNKS = 2
 courant = 0.5
@@ -90,7 +89,7 @@
         scale_kernel,
         in_specs=[vmem(), smem()],
         out_specs=vmem(),
-        out_shape=jax.ShapeDtypeStruct((LZ, ROWS, COLS), F32),
+        out_shape=pltpu.HBM((LZ, ROWS, COLS), F32),
         compiler_params=params(8),
         cost_estimate=pl.CostEstimate(
             flops=1_500_000_000, bytes_accessed=3_000_000, transcendentals=0
@@ -208,7 +207,7 @@
         out_shape=[jax.ShapeDtypeStruct((USED_R, 128), F32)] * 2,
         compiler_params=params(16),
         name="pack_cols",
-    )(*stay(e, e, h, h), scale, scale, from_top, from_top, from_bottom, from_bottom)
+    )(*stay(e, e, h, h, scale, scale), from_top, from_top, from_bottom, from_bottom)
 
 
 def rim_tile(both, index):
@@ -287,7 +286,7 @@
         sources_kernel,
         in_specs=[vmem(), vmem(), smem()],
         out_specs=vmem(),
-        out_shape=jax.ShapeDtypeStruct((LZ, TILES, USED_R, 128), F32),
+        out_shape=pltpu.HBM((LZ, TILES, USED_R, 128), F32),
         compiler_params=params(12),
         cost_estimate=pl.CostEstimate(
             flops=3_000_000_000, bytes_accessed=3_000_000, transcendentals=0
@@ -312,10 +311,10 @@
 ):
     refs = list(refs)
     e_out, h_out = (refs.pop(0), refs.pop(0)) if with_fields else (None, None)
-    face_out = refs.pop(0) if with_face else None
+    face_target = refs.pop(0) if with_face else None
     e, h, scale, grid = refs[:4]
     refs = refs[4:]
-    first = refs.pop(0) if with_face else None
+    first, face_out = (refs.pop(0), refs.pop(0)) if with_face else (None, None)
     in_sem, grid_sem, out_sem = refs
     span = ROWS // CHUNKS
     own_tiles = COLS // 128
@@ -511,6 +510,13 @@
     sent = []
     for chunk in range(CHUNKS):
         lax.fori_loop(chunk * (span // 16), (chunk + 1) * (span // 16), second_step, 0, unroll=2)
+        if with_face:
+            rows = pl.ds(chunk * span, span)
+            copy = pltpu.make_async_copy(
+                face_out.at[:, rows, :], face_target.at[:, rows, :], out_sem.at[len(sent)]
+            )
+            copy.start()
+            sent.append(copy)
         if with_fields:
             source_rows = pl.ds(OFF + chunk * span, span)
             target_rows = pl.ds(chunk * span, span)
@@ -543,13 +549,14 @@
         out_shape += [field, field]
         out_specs += [anywhere, anywhere]
     if with_face:
-        out_shape.append(jax.ShapeDtypeStruct((16, ROWS, 256), BF16))
-        out_specs.append(vmem())
+        out_shape.append(pltpu.HBM((16, ROWS, 256), BF16))
+        out_specs.append(anywhere)
         scratch.append(pltpu.VMEM((4, COLS // 128, ROWS, 128), F32))
+        scratch.append(pltpu.VMEM((16, ROWS, 256), BF16))
     scratch += [
         pltpu.SemaphoreType.DMA((CHUNKS, 3 * COLS // 128)),
         pltpu.SemaphoreType.DMA,
-        pltpu.SemaphoreType.DMA((CHUNKS * 2 * COLS // 128,)),
+        pltpu.SemaphoreType.DMA((CHUNKS * (2 * COLS // 128 + 1),)),
     ]
     return pl.pallas_call(
         functools.partial(yee_kernel, with_fields, with_face),
@@ -562,84 +569,108 @@
             flops=5_000_000_000, bytes_accessed=40_000_000, transcendentals=0
         ),
         name="yee_fields" if with_fields else "yee_face",
-    )(*stay(e, h), scale, grid, *rims, place)
+    )(*stay(e, h, scale, grid), *rims, place)
+
+
+def fetch_kernel(x_in, y_in, x_out, y_out, sem):
+    copies = [
+        pltpu.make_async_copy(x_in, x_out, sem.at[0]),
+        pltpu.make_async_copy(y_in, y_out, sem.at[1]),
+    ]
+    for copy in copies:
+        copy.start()
+    for copy in copies:
+        copy.wait()
+
+
+def fetch(x_table, y_table):
+    anywhere = pl.BlockSpec(memory_space=pl.ANY)
+    return pl.pallas_call(
+        fetch_kernel,
+        in_specs=[anywhere, anywhere],
+        out_specs=[vmem(), vmem()],
+        out_shape=[
+            pltpu.VMEM(x_table.shape, x_table.dtype),
+            pltpu.VMEM(y_table.shape, y_table.dtype),
+        ],
+        scratch_shapes=[pltpu.SemaphoreType.DMA((2,))],
+        compiler_params=params(4),
+        cost_estimate=pl.CostEstimate(
+            flops=1_000_000, bytes_accessed=54_000_000, transcendentals=0
+        ),
+        name="fetch",
+    )(*stay(x_table, y_table))
+
+
+def held(array):
+    return pltpu.with_memory_space_constraint(array, pltpu.VMEM)
 
 
 def rows_kernel(field_ref, table_ref, out_ref):
-    total = jnp.dot(table_ref[...], field_ref[...], preferred_element_type=F32)
-    out_ref[...] = total.astype(BF16)
+    def part(s, _):
+        span = pl.ds(pl.multiple_of(s * 320, 320), 320)
+        total = jnp.dot(table_ref[span, :], field_ref[...], preferred_element_type=F32)
+        out_ref[span, :] = total.astype(BF16)
+        return 0
+
+    lax.fori_loop(0, 4, part, 0)
 
 
 def rows_transform(field, table):
-    step = 320
     return pl.pallas_call(
         rows_kernel,
-        grid=(1280 // step,),
-        in_specs=[
-            pl.BlockSpec((N, 256), lambda t: (0, 0)),
-            pl.BlockSpec((step, N), lambda t: (t, 0)),
-        ],
-        out_specs=pl.BlockSpec((step, 256), lambda t: (t, 0)),
+        in_specs=[vmem(), vmem()],
+        out_specs=vmem(),
         out_shape=jax.ShapeDtypeStruct((1280, 256), BF16),
-        compiler_params=params(16),
+        compiler_params=params(8),
         name="rows_transform",
-    )(field, *stay(table))
+    )(field, held(table))
 
 
 def columns_kernel(rows_ref, table_ref, out_ref, total, spread):
-    step = pl.program_id(0)
-    part = jnp.dot(rows_ref[0], table_ref[0], preferred_element_type=F32)
-    for g in range(1, GROUP):
-        part += jnp.dot(rows_ref[g], table_ref[g], preferred_element_type=F32)
-
-    @pl.when(step == 0)
-    def _():
-        total[...] = part
-
-    @pl.when(step > 0)
-    def _():
-        total[...] += part
-
-    @pl.when(step == 16 // GROUP - 1)
-    def _():
-        sub = lax.broadcasted_iota(jnp.int32, (8, NA), 0)
-
-        def flip(value):
-            value = pltpu.roll(value, 4, 0)
-            value = jnp.where(sub % 4 < 2, pltpu.roll(value, 6, 0), pltpu.roll(value, 2, 0))
-            return jnp.where(sub % 2 == 0, pltpu.roll(value, 7, 0), pltpu.roll(value, 1, 0))
-
-        for q in range(4):
-            for plus in (True, False):
-                base = 16 * (q if plus else 4 - q)
-                cos_re, cos_im = total[base : base + 8, 0:NA], total[base : base + 8, NA : 2 * NA]
-                sin_re = total[base + 8 : base + 16, 0:NA]
-                sin_im = total[base + 8 : base + 16, NA : 2 * NA]
-                if plus:
-                    parts = (cos_re + sin_im, cos_im - sin_re)
-                else:
-                    parts = (flip(cos_re - sin_im), flip(cos_im + sin_re))
-                for ri, value in enumerate(parts):
-                    for j in range(8):
-                        start = ((8 if plus else 0) * 8 + j) * 8 + 2 * q + ri
-                        spread[pl.ds(start, 8, stride=64), :] = value[:, 128 * j : 128 * j + 128]
-        out_ref[...] = spread[...].astype(BF16)
+    def width(s, _):
+        cols = pl.ds(pl.multiple_of(s * 512, 512), 512)
+        part = jnp.dot(rows_ref[0], table_ref[0, :, cols], preferred_element_type=F32)
+        for g in range(1, 16):
+            part += jnp.dot(rows_ref[g], table_ref[g, :, cols], preferred_element_type=F32)
+        total[:, cols] = part
+        return 0
+
+    lax.fori_loop(0, 4, width, 0)
+    sub = lax.broadcasted_iota(jnp.int32, (8, NA), 0)
+
+    def flip(value):
+        value = pltpu.roll(value, 4, 0)
+        value = jnp.where(sub % 4 < 2, pltpu.roll(value, 6, 0), pltpu.roll(value, 2, 0))
+        return jnp.where(sub % 2 == 0, pltpu.roll(value, 7, 0), pltpu.roll(value, 1, 0))
+
+    for q in range(4):
+        for plus in (True, False):
+            base = 16 * (q if plus else 4 - q)
+            cos_re, cos_im = total[base : base + 8, 0:NA], total[base : base + 8, NA : 2 * NA]
+            sin_re = total[base + 8 : base + 16, 0:NA]
+            sin_im = total[base + 8 : base + 16, NA : 2 * NA]
+            if plus:
+                parts = (cos_re + sin_im, cos_im - sin_re)
+            else:
+                parts = (flip(cos_re - sin_im), flip(cos_im + sin_re))
+            for ri, value in enumerate(parts):
+                for j in range(8):
+                    start = ((8 if plus else 0) * 8 + j) * 8 + 2 * q + ri
+                    spread[pl.ds(start, 8, stride=64), :] = value[:, 128 * j : 128 * j + 128]
+    out_ref[...] = spread[...].astype(BF16)
 
 
 def columns(rows, table):
     return pl.pallas_call(
         columns_kernel,
-        grid=(16 // GROUP,),
-        in_specs=[
-            pl.BlockSpec((GROUP, 80, 256), lambda t: (t, 0, 0)),
-            pl.BlockSpec((GROUP, 256, 2 * NA), lambda t: (t, 0, 0)),
-        ],
-        out_specs=pl.BlockSpec((1024, 128), lambda t: (0, 0)),
-        out_shape=jax.ShapeDtypeStruct((1024, 128), BF16),
+        in_specs=[vmem(), vmem()],
+        out_specs=vmem(),
+        out_shape=pltpu.HBM((1024, 128), BF16),
         scratch_shapes=[pltpu.VMEM((80, 2 * NA), F32), pltpu.VMEM((1024, 128), F32)],
-        compiler_params=params(24),
+        compiler_params=params(8),
         name="columns",
-    )(rows, *stay(table))
+    )(rows, held(table))
 
 
 def combine_kernel(parts_ref, coef_ref, place_ref, out_ref):
@@ -714,7 +745,11 @@
     ) * (1.0 / N)
 
     face = lax.all_to_all(face, GX, 0, 0, tiled=True)
-    face, e_out, h_out = lax.optimization_barrier((face, e_out, h_out))
+    x_table, y_table, e_out = lax.optimization_barrier((x_table, y_table, e_out))
+    x_table, y_table = fetch(x_table, y_table)
+    face, e_out, h_out, x_table, y_table = lax.optimization_barrier(
+        (face, e_out, h_out, x_table, y_table)
+    )
     rows = rows_transform(face.reshape(N, 256), x_table)
     rows = lax.all_to_all(rows.reshape(16, 80, 256), ("gc", "gy"), 0, 0, tiled=True)
     far = columns(rows, y_table)

time: 132 us -> 143 us (1.083)
  local copies, waits for them, and re-layouts: 6.79 us -> 20.6 us
  waiting for transfers between devices: 23.9 us -> 11.3 us
  Pallas kernels: 49.6 us -> 60.3 us
    unnamed x21 -> x19, local copies, waits for them, and re-layouts: 6.42 us -> 20.3 us
    all_to_all x1, waiting for transfers between devices: 11.5 us -> 0.01 us  [on_device(): face = lax.all_to_all(face, GX, 0, 0, tiled=True)]
    pallas_call x2, Pallas kernels: 23.8 us -> 30.1 us  [yee(): pl.pallas_call(functools.partial(yee_kernel, with_fields, with_face), in_...]
    pallas_call x2 -> x3, Pallas kernels: 15.1 us -> 16.8 us  [the longest x1 8.77 us: fetch(): pl.pallas_call(fetch_kernel, in_specs=[anywhere, anywhere], out_specs=[vm...]
  transfers between devices with their start and end apart: 6 -> 6, of which waited for: 3 -> 2; matrix products, arithmetic and copies ran while one was open for 0% -> 0% of each run, Pallas kernels for 14% -> 23%
where the time goes in v4:
time: 143 us; the launch traced here: 142 us
  Pallas kernels  60.3 us (42%)
  blocking collectives  25.3 us (18%)
  starting transfers between devices  23.7 us (17%)
  local copies, waits for them, and re-layouts  20.6 us (14%)
  waiting for transfers between devices  11.3 us (8%)
    pallas_call x2, Pallas kernels, yee(): pl.pallas_call(functools.partial(yee_kernel, with_fields, with_face), in_...  30.1 us
    all_to_all x1, blocking collectives, on_device(): lax.all_to_all(rows.reshape(16, 80, 256), ('gc', 'gy'), 0, 0, tiled=True)  25.3 us
    unnamed x19, local copies, waits for them, and re-layouts  20.3 us
    all_to_all x1, waiting for transfers between devices, on_device(): lax.all_to_all(far.reshape(128, 8, 128), GX + ('gy',), 0, 0, tiled=True)  10.1 us
    pallas_call x1, Pallas kernels, fetch(): pl.pallas_call(fetch_kernel, in_specs=[anywhere, anywhere], out_specs=[vm...  8.77 us
    all_to_all x1, starting transfers between devices, on_device(): face = lax.all_to_all(face, GX, 0, 0, tiled=True)  8.56 us
    all_to_all x1, starting transfers between devices, on_device(): lax.all_to_all(far.reshape(128, 8, 128), GX + ('gy',), 0, 0, tiled=True)  6.54 us
    ppermute x1, starting transfers between devices, on_device(): from_left = lax.ppermute(right, 'gy', [(k, k + 1) for k in range(7)])  4.55 us
  transfers between devices with their start and end apart: 6, of which 2 were waited for; matrix products, arithmetic and copies ran while one was open for 0% of the time, Pallas kernels for 23%

profile of v4, /device:TPU:0, one launch (start us, length us, event | category | flops | bytes accessed | tf_op | source)
XLA Modules:
  0.0 142.2 jit_solution(6955301525301917286)
XLA Ops:
  0.6 0.0 copy-start.4
  0.6 0.0 copy-start.5
  0.7 0.8 copy-done.5
  1.4 1.3 pack_rows.1
  2.7 0.0 copy-start.7
  2.7 1.4 %collective-permute-start = (f32[48,512]{1,0:T(8,128)S(1)}, f32[48,512]{1,0:T(8,128)S(1)}, u32[]{:S(2)}, u32[]{:S(2)}) collective-permute-start(f32[48,512]{1,0:T(8,128)S(1)} %get-tuple-element.21), channel_id=1, source_target_pairs={{0,8},{8,16},{16,24},{24,32},{32,40},{40,48},{48,56},{56,64},{64,7... | collective-permute-start | bytes 294920 | tf_op jit(solution)/shard_map/ppermute | solution.py:727
  4.1 1.3 collective-permute-start.1
  5.4 0.0 copy-done.4
  5.4 2.6 %scales.1.s_lo.s_hi.scale_in = f32[3,256,512]{2,1,0:T(8,128)} custom-call(s32[3,256,512]{2,1,0:T(8,128)S(1)} %copy-done.4, f32[8]{0:T(128)S(1)} %copy-done.5), custom_call_target="tpu_custom_call" | custom-call | flops 1500000000 | bytes 3000000 | tf_op jit(solution)/shard_map/scales/pallas_call | solution.py:88
  8.0 0.0 copy-done.7
  8.0 0.1 pad_add_fusion.place_ref
  8.1 0.0 copy-start.6
  8.1 0.0 collective-permute-done.top_lo.top_hi.from_top
  8.1 1.1 collective-permute-done.1.bot_lo.bot_hi.from_bottom
  9.2 4.0 %pack_cols.1 = (f32[272,128]{1,0:T(8,128)S(1)}, f32[272,128]{1,0:T(8,128)S(1)}) custom-call(f32[3,3,256,512]{3,2,1,0:T(8,128)} %e_in.3, f32[3,3,256,512]{3,2,1,0:T(8,128)} %e_in.3, f32[3,3,256,512]{3,2,1,0:T(8,128)} %h_in.3, f32[3,3,256,512]{3,2,1,0:T(8,128)} %h_in.3, f32[3,256,512]{2,1,0:T(8,128)} %scales.1.s_lo.s_hi.scale_in, ...), custom_call_target="tpu_custom_call" | custom-call | tf_op jit(solution)/shard_map/pack_cols/pallas_call | solution.py:202
  13.2 1.3 collective-permute-start.3
  14.5 4.6 %collective-permute-start.2 = (f32[272,128]{1,0:T(8,128)S(1)}, f32[272,128]{1,0:T(8,128)S(1)}, u32[]{:S(2)}, u32[]{:S(2)}) collective-permute-start(f32[272,128]{1,0:T(8,128)S(1)} %get-tuple-element.26), channel_id=1, source_target_pairs={{0,1},{1,2},{2,3},{3,4},{4,5},{5,6},{6,7},{8,9},{9,10},{10,11},{11... | collective-permute-start | bytes 417800 | tf_op jit(solution)/shard_map/ppermute | solution.py:731
  19.1 0.0 copy-done.6
  19.1 3.9 %sources.1.grid_in = f32[3,5,272,128]{3,2,1,0:T(8,128)} custom-call(s32[3,32,128]{2,1,0:T(8,128)S(1)} %bitcast.24, f32[32,128]{1,0:T(8,128)S(1)} %bitcast.25, s32[2]{0:T(128)S(1)} %pad_add_fusion.place_ref), custom_call_target="tpu_custom_call" | custom-call | flops 3000000000 | bytes 3000000 | tf_op jit(solution)/shard_map/sources/pallas_call | solution.py:285
  23.0 0.0 collective-permute-done.2.from_left
  23.0 0.0 collective-permute-done.3.from_right
  23.0 13.2 %yee_face.1 = bf16[16,256,256]{2,1,0:T(8,128)(2,1)} custom-call(f32[3,3,256,512]{3,2,1,0:T(8,128)} %e_in.3, f32[3,3,256,512]{3,2,1,0:T(8,128)} %h_in.3, f32[3,256,512]{2,1,0:T(8,128)} %scales.1.s_lo.s_hi.scale_in, f32[3,5,272,128]{3,2,1,0:T(8,128)} %sources.1.grid_in, f32[272,128]{1,0:T(8,128)S(1)} %collective-permute-done.2.from_left, ...), custom_call_target="tpu_custom_call" | custom-call | flops 5000000000 | bytes 40000000 | tf_op jit(solution)/shard_map/yee_face/pallas_call | solution.py:561
  36.3 8.6 %all-to-all-start = ((bf16[16,256,256]{2,1,0:T(8,128)(2,1)}), bf16[16,256,256]{2,1,0:T(8,128)(2,1)S(1)}, u32[]{:S(2)}, u32[]{:S(2)}) async-start(bf16[16,256,256]{2,1,0:T(8,128)(2,1)} %yee_face.1), calls=%async_computation | async-start | bytes 4194304 | tf_op jit(solution)/shard_map/all_to_all | solution.py:747
  44.8 16.8 %yee_fields.1 = (f32[3,3,256,512]{3,2,1,0:T(8,128)}, f32[3,3,256,512]{3,2,1,0:T(8,128)}) custom-call(f32[3,3,256,512]{3,2,1,0:T(8,128)} %e_in.3, f32[3,3,256,512]{3,2,1,0:T(8,128)} %h_in.3, f32[3,256,512]{2,1,0:T(8,128)} %scales.1.s_lo.s_hi.scale_in, f32[3,5,272,128]{3,2,1,0:T(8,128)} %sources.1.grid_in, f32[272,128]{1,0:T(8,128)S(1)} %collective-permute-done.2.from_left, ...), custom_call_target="tpu_custom_call" | custom-call | flops 5000000000 | bytes 40000000 | tf_op jit(solution)/shard_map/yee_fields/pallas_call | solution.py:561
  61.7 8.8 %fetch.1 = (bf16[1280,4096]{1,0:T(8,128)(2,1)S(1)}, bf16[16,256,2048]{2,1,0:T(8,128)(2,1)S(1)}) custom-call(bf16[1280,4096]{1,0:T(8,128)(2,1)} %constant.25.clone.x_in, bf16[16,256,2048]{2,1,0:T(8,128)(2,1)} %constant.26.clone.y_in), custom_call_target="tpu_custom_call" | custom-call | flops 1000000 | bytes 54000000 | tf_op jit(solution)/shard_map/fetch/pallas_call | solution.py:588
  70.5 0.0 copy-start
  70.5 5.7 %copy-done = bf16[16,256,2048]{2,1,0:T(8,128)(2,1)} copy-done((bf16[16,256,2048]{2,1,0:T(8,128)(2,1)}, bf16[16,256,2048]{2,1,0:T(8,128)(2,1)S(1)}, u32[]{:S(2)}) %copy-start) | copy-done | bytes 16777240
  76.2 0.0 copy-start.2
  76.2 4.0 %copy-done.2 = bf16[1280,4096]{1,0:T(8,128)(2,1)} copy-done((bf16[1280,4096]{1,0:T(8,128)(2,1)}, bf16[1280,4096]{1,0:T(8,128)(2,1)S(1)}, u32[]{:S(2)}) %copy-start.2) | copy-done | bytes 10485784
  80.2 0.0 all-to-all-done
  80.2 0.0 copy-start.3
  80.2 4.0 %copy-done.3 = bf16[1280,4096]{1,0:T(8,128)(2,1)S(1)} copy-done((bf16[1280,4096]{1,0:T(8,128)(2,1)S(1)}, bf16[1280,4096]{1,0:T(8,128)(2,1)}, u32[]{:S(2)}) %copy-start.3) | copy-done | bytes 10485784
  84.2 3.5 %rows_transform.1 = bf16[1280,256]{1,0:T(8,128)(2,1)S(1)} custom-call(bf16[4096,256]{1,0:T(8,128)(2,1)S(1)} %bitcast.21, bf16[1280,4096]{1,0:T(8,128)(2,1)S(1)} %copy-done.3), custom_call_target="tpu_custom_call" | custom-call | tf_op jit(solution)/shard_map/rows_transform/pallas_call | solution.py:620
  87.7 25.3 %all_to_all.15.rows_ref = bf16[16,80,256]{2,1,0:T(8,128)(2,1)S(1)} all-to-all(bf16[16,80,256]{2,1,0:T(8,128)(2,1)S(1)} %bitcast.22), channel_id=1, replica_groups=mesh['ga'=8,'gc'=2,'gy'=8] {'gc','gy'}, dimensions={0} | all-to-all | bytes 1310720 | tf_op jit(solution)/shard_map/all_to_all | solution.py:754
  113.0 0.0 copy-start.1
  113.0 5.8 %copy-done.1 = bf16[16,256,2048]{2,1,0:T(8,128)(2,1)S(1)} copy-done((bf16[16,256,2048]{2,1,0:T(8,128)(2,1)S(1)}, bf16[16,256,2048]{2,1,0:T(8,128)(2,1)}, u32[]{:S(2)}) %copy-start.1) | copy-done | bytes 16777240
  118.7 0.0 copy-start.8
  118.7 4.5 %columns.1 = bf16[1024,128]{1,0:T(8,128)(2,1)} custom-call(bf16[16,80,256]{2,1,0:T(8,128)(2,1)S(1)} %all_to_all.15.rows_ref, bf16[16,256,2048]{2,1,0:T(8,128)(2,1)S(1)} %copy-done.1), custom_call_target="tpu_custom_call" | custom-call | tf_op jit(solution)/shard_map/columns/pallas_call | solution.py:665
  123.3 6.5 %all-to-all-start.2 = ((bf16[128,8,128]{2,1,0:T(8,128)(2,1)}), bf16[128,8,128]{2,1,0:T(8,128)(2,1)S(1)}, u32[]{:S(2)}, u32[]{:S(2)}) async-start(bf16[128,8,128]{2,1,0:T(8,128)(2,1)} %bitcast.26), calls=%async_computation.2 | async-start | bytes 524288 | tf_op jit(solution)/shard_map/all_to_all | solution.py:756
  129.8 0.0 copy-done.8
  129.9 0.1 multiply_bitcast_fusion.3
  129.9 0.1 copy.15
  130.0 0.1 copy.14
  130.1 0.1 copy.13
  130.2 0.1 copy.12
  130.3 0.1 maximum_multiply_fusion.coef_ref
  130.4 10.1 %all-to-all-done.2 = bf16[128,8,128]{2,1,0:T(8,128)(2,1)S(1)} async-done(((bf16[128,8,128]{2,1,0:T(8,128)(2,1)}), bf16[128,8,128]{2,1,0:T(8,128)(2,1)S(1)}, u32[]{:S(2)}, u32[]{:S(2)}) %all-to-all-start.2) | async-done | bytes 262176 | tf_op jit(solution)/shard_map/all_to_all | solution.py:756
  140.5 1.7 %combine.1 = f32[16,64,128]{2,1,0:T(8,128)} custom-call(bf16[64,16,128]{2,1,0:T(8,128)(2,1)S(1)} %bitcast.23, f32[2,4]{1,0:T(2,128)S(1)} %maximum_multiply_fusion.coef_ref, s32[2]{0:T(128)S(1)} %pad_add_fusion.place_ref), custom_call_target="tpu_custom_call" | custom-call | tf_op jit(solution)/shard_map/combine/pallas_call | solution.py:712
  (1 shorter events, 0.0 us)
Async XLA Ops:
  0.6 4.8 %copy-start.4 = (s32[3,256,512]{2,1,0:T(8,128)S(1)}, s32[3,256,512]{2,1,0:T(8,128)}, u32[]{:S(2)}) copy-start(s32[3,256,512]{2,1,0:T(8,128)} %m_hi.1) | copy-start | bytes 4718596
  0.6 0.8 copy-start.5
  2.7 5.3 %copy-start.7 = (s32[4096,3]{0,1:T(4,128)S(1)}, s32[4096,3]{0,1:T(4,128)}, u32[]{:S(2)}) copy-start(s32[4096,3]{0,1:T(4,128)} %param.13) | copy-start | bytes 147460
  2.7 5.4 %collective-permute-start = (f32[48,512]{1,0:T(8,128)S(1)}, f32[48,512]{1,0:T(8,128)S(1)}, u32[]{:S(2)}, u32[]{:S(2)}) collective-permute-start(f32[48,512]{1,0:T(8,128)S(1)} %get-tuple-element.21), channel_id=1, source_target_pairs={{0,8},{8,16},{16,24},{24,32},{32,40},{40,48},{48,56},{56,64},{64,7... | collective-permute-start | bytes 294920 | tf_op jit(solution)/shard_map/ppermute | solution.py:727
  4.1 5.1 %collective-permute-start.1 = (f32[48,512]{1,0:T(8,128)S(1)}, f32[48,512]{1,0:T(8,128)S(1)}, u32[]{:S(2)}, u32[]{:S(2)}) collective-permute-start(f32[48,512]{1,0:T(8,128)S(1)} %get-tuple-element.22), channel_id=1, source_target_pairs={{8,0},{16,8},{24,16},{32,24},{40,32},{48,40},{56,48},{64,56},{72,6... | collective-permute-start | bytes 294920 | tf_op jit(solution)/shard_map/ppermute | solution.py:728
  8.1 11.0 %copy-start.6 = (f32[4096]{0:T(1024)S(1)}, f32[4096]{0:T(1024)}, u32[]{:S(2)}) copy-start(f32[4096]{0:T(1024)} %param.14) | copy-start | bytes 49156
  13.2 9.8 %collective-permute-start.3 = (f32[272,128]{1,0:T(8,128)S(1)}, f32[272,128]{1,0:T(8,128)S(1)}, u32[]{:S(2)}, u32[]{:S(2)}) collective-permute-start(f32[272,128]{1,0:T(8,128)S(1)} %get-tuple-element.23), channel_id=1, source_target_pairs={{1,0},{2,1},{3,2},{4,3},{5,4},{6,5},{7,6},{9,8},{10,9},{11,10},{12... | collective-permute-start | bytes 417800 | tf_op jit(solution)/shard_map/ppermute | solution.py:732
  14.5 8.5 %collective-permute-start.2 = (f32[272,128]{1,0:T(8,128)S(1)}, f32[272,128]{1,0:T(8,128)S(1)}, u32[]{:S(2)}, u32[]{:S(2)}) collective-permute-start(f32[272,128]{1,0:T(8,128)S(1)} %get-tuple-element.26), channel_id=1, source_target_pairs={{0,1},{1,2},{2,3},{3,4},{4,5},{5,6},{6,7},{8,9},{9,10},{10,11},{11... | collective-permute-start | bytes 417800 | tf_op jit(solution)/shard_map/ppermute | solution.py:731
  36.3 43.9 %all-to-all-start = ((bf16[16,256,256]{2,1,0:T(8,128)(2,1)}), bf16[16,256,256]{2,1,0:T(8,128)(2,1)S(1)}, u32[]{:S(2)}, u32[]{:S(2)}) async-start(bf16[16,256,256]{2,1,0:T(8,128)(2,1)} %yee_face.1), calls=%async_computation | async-start | bytes 4194304 | tf_op jit(solution)/shard_map/all_to_all | solution.py:747
  70.5 5.7 %copy-start = (bf16[16,256,2048]{2,1,0:T(8,128)(2,1)}, bf16[16,256,2048]{2,1,0:T(8,128)(2,1)S(1)}, u32[]{:S(2)}) copy-start(bf16[16,256,2048]{2,1,0:T(8,128)(2,1)S(1)} %get-tuple-element.38.table_ref) | copy-start | bytes 50331652
  76.2 4.0 %copy-start.2 = (bf16[1280,4096]{1,0:T(8,128)(2,1)}, bf16[1280,4096]{1,0:T(8,128)(2,1)S(1)}, u32[]{:S(2)}) copy-start(bf16[1280,4096]{1,0:T(8,128)(2,1)S(1)} %get-tuple-element.37.table_ref) | copy-start | bytes 31457284
  80.2 4.0 %copy-start.3 = (bf16[1280,4096]{1,0:T(8,128)(2,1)S(1)}, bf16[1280,4096]{1,0:T(8,128)(2,1)}, u32[]{:S(2)}) copy-start(bf16[1280,4096]{1,0:T(8,128)(2,1)} %copy-done.2) | copy-start | bytes 31457284
  113.0 5.8 %copy-start.1 = (bf16[16,256,2048]{2,1,0:T(8,128)(2,1)S(1)}, bf16[16,256,2048]{2,1,0:T(8,128)(2,1)}, u32[]{:S(2)}) copy-start(bf16[16,256,2048]{2,1,0:T(8,128)(2,1)} %copy-done) | copy-start | bytes 50331652
  118.7 11.1 %copy-start.8 = (f32[2]{0:T(128)S(1)}, f32[2]{0:T(128)}, u32[]{:S(2)}) copy-start(f32[2]{0:T(128)} %param.15) | copy-start | bytes 28
  123.3 17.2 %all-to-all-start.2 = ((bf16[128,8,128]{2,1,0:T(8,128)(2,1)}), bf16[128,8,128]{2,1,0:T(8,128)(2,1)S(1)}, u32[]{:S(2)}, u32[]{:S(2)}) async-start(bf16[128,8,128]{2,1,0:T(8,128)(2,1)} %bitcast.26), calls=%async_computation.2 | async-start | bytes 524288 | tf_op jit(solution)/shard_map/all_to_all | solution.py:756

commit v5 on v4

--- a/solution.py
+++ b/solution.py
@@ -22,6 +22,9 @@
 EXT_C = 640
 TILES = 5
 USED_R = 272
+FOLD = 136
+ROW_STEP = 320
+COL_STEP = 256
 CHUNKS = 2
 courant = 0.5
 source_rate = 0.7
@@ -89,7 +92,7 @@
         scale_kernel,
         in_specs=[vmem(), smem()],
         out_specs=vmem(),
-        out_shape=pltpu.HBM((LZ, ROWS, COLS), F32),
+        out_shape=jax.ShapeDtypeStruct((LZ, ROWS, COLS), F32),
         compiler_params=params(8),
         cost_estimate=pl.CostEstimate(
             flops=1_500_000_000, bytes_accessed=3_000_000, transcendentals=0
@@ -150,7 +153,8 @@
 
 
 def pack_cols_kernel(
-    e_lo, e_hi, h_lo, h_hi, s_lo, s_hi, top_lo, top_hi, bot_lo, bot_hi, left_ref, right_ref
+    e_lo, e_hi, h_lo, h_hi, s_lo, s_hi, top_lo, top_hi, bot_lo, bot_hi, left_ref, right_ref,
+    all_rows,
 ):
     rows = 32
 
@@ -161,7 +165,7 @@
             lo, hi = pair_of(index)
             ends = pltpu.roll(jnp.where(lane < 64, lo, hi), 4 * index + 2, 1)
             both = jnp.where(lane // 4 == index, ends, both)
-        return jnp.where(lane % 4 >= 2, both, 0.0), jnp.where(lane % 4 < 2, both, 0.0)
+        return both
 
     def strip(s, _):
         r = pl.multiple_of(s * rows, rows)
@@ -175,19 +179,18 @@
                 return h_lo[a - 3, layer, span, :], h_hi[a - 3, layer, span, :]
             return s_lo[layer, span, :], s_hi[layer, span, :]
 
-        left, right = packed(pair_of, (rows, 128))
-        target = pl.ds(pl.multiple_of(r + OFF, 8), rows)
-        left_ref[target, :] = left
-        right_ref[target, :] = right
+        all_rows[pl.ds(pl.multiple_of(r + OFF, 8), rows), :] = packed(pair_of, (rows, 128))
         return 0
 
     lax.fori_loop(0, ROWS // rows, strip, 0)
     for to_top, lo, hi, r in ((True, top_lo, top_hi, 0), (False, bot_lo, bot_hi, ROWS + OFF)):
-        left, right = packed(
+        all_rows[r : r + 8, :] = packed(
             lambda index: (rim_rows(lo, index, to_top), rim_rows(hi, index, to_top)), (8, 128)
         )
-        left_ref[r : r + 8, :] = left
-        right_ref[r : r + 8, :] = right
+    high = lax.broadcasted_iota(jnp.int32, (FOLD, 128), 1) % 4 >= 2
+    near, far = all_rows[0:FOLD, :], all_rows[FOLD:USED_R, :]
+    left_ref[...] = jnp.where(high, near, pltpu.roll(far, 126, 1))
+    right_ref[...] = jnp.where(high, pltpu.roll(far, 2, 1), near)
 
 
 def pack_cols(e, h, scale, from_top, from_bottom):
@@ -198,16 +201,17 @@
     hi3 = pl.BlockSpec((LZ, ROWS, 128), lambda r: (0, 0, end))
     lo2 = pl.BlockSpec((48, 128), lambda r: (0, 0))
     hi2 = pl.BlockSpec((48, 128), lambda r: (0, end))
-    out = pl.BlockSpec((USED_R, 128), lambda r: (0, 0))
+    out = pl.BlockSpec((FOLD, 128), lambda r: (0, 0))
     return pl.pallas_call(
         pack_cols_kernel,
         grid=(1,),
         in_specs=[lo4, hi4, lo4, hi4, lo3, hi3, lo2, hi2, lo2, hi2],
         out_specs=[out, out],
-        out_shape=[jax.ShapeDtypeStruct((USED_R, 128), F32)] * 2,
+        out_shape=[jax.ShapeDtypeStruct((FOLD, 128), F32)] * 2,
+        scratch_shapes=[pltpu.VMEM((USED_R, 128), F32)],
         compiler_params=params(16),
         name="pack_cols",
-    )(*stay(e, e, h, h, scale, scale), from_top, from_top, from_bottom, from_bottom)
+    )(*stay(e, e, h, h), scale, scale, from_top, from_top, from_bottom, from_bottom)
 
 
 def rim_tile(both, index):
@@ -216,7 +220,7 @@
     return jnp.where((lane < 2) | (lane >= 126), moved, 0.0)
 
 
-def sources_kernel(pos_ref, amp_ref, place_ref, grid_ref):
+def sources_kernel(pos_ref, amp_ref, place_ref, grid_ref, kept_ref, sem):
     groups = NSRC // 128
     row = pos_ref[1] - place_ref[0] * ROWS + OFF
     col = pos_ref[2] - place_ref[1] * COLS
@@ -279,14 +283,21 @@
         return 0
 
     lax.fori_loop(0, (count + 127) // 128, one_pass, 0)
+    copy = pltpu.make_async_copy(grid_ref, kept_ref, sem)
+    copy.start()
+    copy.wait()
 
 
 def sources(pos, amp, place):
     return pl.pallas_call(
         sources_kernel,
         in_specs=[vmem(), vmem(), smem()],
-        out_specs=vmem(),
-        out_shape=pltpu.HBM((LZ, TILES, USED_R, 128), F32),
+        out_specs=[vmem(), pl.BlockSpec(memory_space=pl.ANY)],
+        out_shape=[
+            jax.ShapeDtypeStruct((LZ, TILES, USED_R, 128), F32),
+            pltpu.HBM((LZ, TILES, USED_R, 128), F32),
+        ],
+        scratch_shapes=[pltpu.SemaphoreType.DMA],
         compiler_params=params(12),
         cost_estimate=pl.CostEstimate(
             flops=3_000_000_000, bytes_accessed=3_000_000, transcendentals=0
@@ -319,6 +330,8 @@
     span = ROWS // CHUNKS
     own_tiles = COLS // 128
 
+    grid_copy = pltpu.make_async_copy(grid_in, grid, grid_sem)
+    grid_copy.start()
     arrivals = []
     for chunk in range(CHUNKS):
         here = []
@@ -336,9 +349,6 @@
                 copy.start()
                 here.append(copy)
         arrivals.append(here)
-    grid_copy = pltpu.make_async_copy(grid_in, grid, grid_sem)
-    grid_copy.start()
-
     sub = lax.broadcasted_iota(jnp.int32, (8, 128), 0)
     lane = lax.broadcasted_iota(jnp.int32, (8, 128), 1)
 
@@ -361,13 +371,18 @@
             target[tile, USED_R : USED_R + 8, :] = jnp.zeros((8, 128), F32)
 
     def rim_strip(s, _):
-        r = pl.multiple_of(s * 16, 16)
-        both = from_left[pl.ds(r, 16), :] + from_right[pl.ds(r, 16), :]
+        r = pl.multiple_of(s * 8, 8)
+        left, right = from_left[pl.ds(r, 8), :], from_right[pl.ds(r, 8), :]
+        high = lane % 4 >= 2
+        near = jnp.where(high, right, left)
+        far = jnp.where(high, pltpu.roll(right, 2, 1), pltpu.roll(left, 126, 1))
         for index in range(7 * LZ):
-            array_of(index // LZ, index % LZ)[own_tiles, pl.ds(r, 16), :] = rim_tile(both, index)
-        return 0
-
-    lax.fori_loop(0, USED_R // 16, rim_strip, 0, unroll=2)
+            target = array_of(index // LZ, index % LZ)
+            target[own_tiles, pl.ds(r, 8), :] = rim_tile(near, index)
+            target[own_tiles, pl.ds(pl.multiple_of(r + FOLD, 8), 8), :] = rim_tile(far, index)
+        return 0
+
+    lax.fori_loop(0, FOLD // 8, rim_strip, 0, unroll=2)
 
     row_place, col_place = place_ref[0], place_ref[1]
     rim_half = jnp.full((8, 128), courant, F32)
@@ -569,74 +584,59 @@
             flops=5_000_000_000, bytes_accessed=40_000_000, transcendentals=0
         ),
         name="yee_fields" if with_fields else "yee_face",
-    )(*stay(e, h, scale, grid), *rims, place)
-
-
-def fetch_kernel(x_in, y_in, x_out, y_out, sem):
-    copies = [
-        pltpu.make_async_copy(x_in, x_out, sem.at[0]),
-        pltpu.make_async_copy(y_in, y_out, sem.at[1]),
-    ]
-    for copy in copies:
-        copy.start()
-    for copy in copies:
+    )(*stay(e, h), scale, grid, *rims, place)
+
+
+def rows_kernel(field_ref, table_in, out_ref, table, sem):
+    def copy_of(s):
+        span = pl.ds(pl.multiple_of(s * ROW_STEP, ROW_STEP), ROW_STEP)
+        return span, pltpu.make_async_copy(table_in.at[span], table.at[span], sem.at[s])
+
+    for s in range(1280 // ROW_STEP):
+        copy_of(s)[1].start()
+
+    def part(s, _):
+        span, copy = copy_of(s)
         copy.wait()
-
-
-def fetch(x_table, y_table):
-    anywhere = pl.BlockSpec(memory_space=pl.ANY)
-    return pl.pallas_call(
-        fetch_kernel,
-        in_specs=[anywhere, anywhere],
-        out_specs=[vmem(), vmem()],
-        out_shape=[
-            pltpu.VMEM(x_table.shape, x_table.dtype),
-            pltpu.VMEM(y_table.shape, y_table.dtype),
-        ],
-        scratch_shapes=[pltpu.SemaphoreType.DMA((2,))],
-        compiler_params=params(4),
-        cost_estimate=pl.CostEstimate(
-            flops=1_000_000, bytes_accessed=54_000_000, transcendentals=0
-        ),
-        name="fetch",
-    )(*stay(x_table, y_table))
-
-
-def held(array):
-    return pltpu.with_memory_space_constraint(array, pltpu.VMEM)
-
-
-def rows_kernel(field_ref, table_ref, out_ref):
-    def part(s, _):
-        span = pl.ds(pl.multiple_of(s * 320, 320), 320)
-        total = jnp.dot(table_ref[span, :], field_ref[...], preferred_element_type=F32)
+        total = jnp.dot(table[span, :], field_ref[...], preferred_element_type=F32)
         out_ref[span, :] = total.astype(BF16)
         return 0
 
-    lax.fori_loop(0, 4, part, 0)
+    lax.fori_loop(0, 1280 // ROW_STEP, part, 0)
 
 
 def rows_transform(field, table):
     return pl.pallas_call(
         rows_kernel,
-        in_specs=[vmem(), vmem()],
+        in_specs=[vmem(), pl.BlockSpec(memory_space=pl.ANY)],
         out_specs=vmem(),
         out_shape=jax.ShapeDtypeStruct((1280, 256), BF16),
-        compiler_params=params(8),
+        scratch_shapes=[pltpu.VMEM((1280, N), BF16), pltpu.SemaphoreType.DMA((1280 // ROW_STEP,))],
+        compiler_params=params(18),
         name="rows_transform",
-    )(field, held(table))
-
-
-def columns_kernel(rows_ref, table_ref, out_ref, total, spread):
+    )(field, *stay(table))
+
+
+def columns_kernel(rows_ref, table_in, out_ref, table, total, spread, sem):
+    def copy_of(s):
+        cols = pl.ds(pl.multiple_of(s * COL_STEP, COL_STEP), COL_STEP)
+        return cols, pltpu.make_async_copy(
+            table_in.at[:, :, cols], table.at[:, :, cols], sem.at[s]
+        )
+
+    for s in range(2 * NA // COL_STEP):
+        copy_of(s)[1].start()
+
     def width(s, _):
-        cols = pl.ds(pl.multiple_of(s * 512, 512), 512)
-        part = jnp.dot(rows_ref[0], table_ref[0, :, cols], preferred_element_type=F32)
+        cols, copy = copy_of(s)
+        copy.wait()
+        part = jnp.dot(rows_ref[0], table[0, :, cols], preferred_element_type=F32)
         for g in range(1, 16):
-            part += jnp.dot(rows_ref[g], table_ref[g, :, cols], preferred_element_type=F32)
+            part += jnp.dot(rows_ref[g], table[g, :, cols], preferred_element_type=F32)
         total[:, cols] = part
         return 0
 
-    lax.fori_loop(0, 4, width, 0)
+    lax.fori_loop(0, 2 * NA // COL_STEP, width, 0)
     sub = lax.broadcasted_iota(jnp.int32, (8, NA), 0)
 
     def flip(value):
@@ -664,13 +664,18 @@
 def columns(rows, table):
     return pl.pallas_call(
         columns_kernel,
-        in_specs=[vmem(), vmem()],
+        in_specs=[vmem(), pl.BlockSpec(memory_space=pl.ANY)],
         out_specs=vmem(),
         out_shape=pltpu.HBM((1024, 128), BF16),
-        scratch_shapes=[pltpu.VMEM((80, 2 * NA), F32), pltpu.VMEM((1024, 128), F32)],
-        compiler_params=params(8),
+        scratch_shapes=[
+            pltpu.VMEM((16, 256, 2 * NA), BF16),
+            pltpu.VMEM((80, 2 * NA), F32),
+            pltpu.VMEM((1024, 128), F32),
+            pltpu.SemaphoreType.DMA((2 * NA // COL_STEP,)),
+        ],
+        compiler_params=params(24),
         name="columns",
-    )(rows, held(table))
+    )(rows, *stay(table))
 
 
 def combine_kernel(parts_ref, coef_ref, place_ref, out_ref):
@@ -733,10 +738,10 @@
     pos = src_pos.T.reshape(3, NSRC // 128, 128)
     amp = src_amp.reshape(NSRC // 128, 128)
     pos, amp, left = lax.optimization_barrier((pos, amp, left))
-    grid = sources(pos, amp, place)
+    grid, kept_grid = sources(pos, amp, place)
     rims = (from_left, from_right, from_top, from_bottom)
     (face,) = yee(False, True, e, h, scale, grid, rims, place)
-    e_out, h_out = yee(True, False, e, h, scale, grid, rims, place)
+    e_out, h_out = yee(True, False, e, h, scale, *stay(kept_grid), rims, place)
 
     half = jnp.cos(freqs * 0.5), jnp.sin(freqs * 0.5)
     turn = jnp.cos(freqs * 1.5), jnp.sin(freqs * 1.5)
@@ -745,11 +750,7 @@
     ) * (1.0 / N)
 
     face = lax.all_to_all(face, GX, 0, 0, tiled=True)
-    x_table, y_table, e_out = lax.optimization_barrier((x_table, y_table, e_out))
-    x_table, y_table = fetch(x_table, y_table)
-    face, e_out, h_out, x_table, y_table = lax.optimization_barrier(
-        (face, e_out, h_out, x_table, y_table)
-    )
+    face, e_out, h_out = lax.optimization_barrier((face, e_out, h_out))
     rows = rows_transform(face.reshape(N, 256), x_table)
     rows = lax.all_to_all(rows.reshape(16, 80, 256), ("gc", "gy"), 0, 0, tiled=True)
     far = columns(rows, y_table)

time: 143 us -> 127 us (0.89)
  local copies, waits for them, and re-layouts: 20.6 us -> 2.57 us
  waiting for transfers between devices: 11.3 us -> 24.9 us
  Pallas kernels: 60.3 us -> 50.8 us
  blocking collectives: 25.3 us -> 23.3 us
    unnamed x19 -> x15, local copies, waits for them, and re-layouts: 20.3 us -> 2.2 us
    all_to_all x1, waiting for transfers between devices: 0.01 us -> 12.5 us  [on_device(): face = lax.all_to_all(face, GX, 0, 0, tiled=True)]
    pallas_call x2, Pallas kernels: 30.1 us -> 25.9 us  [yee(): pl.pallas_call(functools.partial(yee_kernel, with_fields, with_face), in_...]
    pallas_call x3 -> x2, Pallas kernels: 16.8 us -> 12.8 us  [the longest x1 7.68 us: columns(): pl.pallas_call(columns_kernel, in_specs=[vmem(), pl.BlockSpec(memory_spac...]
    all_to_all x1, blocking collectives: 25.3 us -> 23.3 us  [on_device(): lax.all_to_all(rows.reshape(16, 80, 256), ('gc', 'gy'), 0, 0, tiled=True)]
  transfers between devices with their start and end apart: 6 -> 6, of which waited for: 2 -> 3; matrix products, arithmetic and copies ran while one was open for 0% -> 0% of each run, Pallas kernels for 23% -> 16%
where the time goes in v5:
time: 127 us; the launch traced here: 126 us
  Pallas kernels  50.8 us (40%)
  waiting for transfers between devices  24.9 us (20%)
  starting transfers between devices  23.8 us (19%)
  blocking collectives  23.3 us (18%)
  local copies, waits for them, and re-layouts  2.57 us (2%)
    pallas_call x2, Pallas kernels, yee(): pl.pallas_call(functools.partial(yee_kernel, with_fields, with_face), in_...  25.9 us
    all_to_all x1, blocking collectives, on_device(): lax.all_to_all(rows.reshape(16, 80, 256), ('gc', 'gy'), 0, 0, tiled=True)  23.3 us
    all_to_all x1, waiting for transfers between devices, on_device(): face = lax.all_to_all(face, GX, 0, 0, tiled=True)  12.5 us
    all_to_all x1, waiting for transfers between devices, on_device(): lax.all_to_all(far.reshape(128, 8, 128), GX + ('gy',), 0, 0, tiled=True)  10.1 us
    all_to_all x1, starting transfers between devices, on_device(): face = lax.all_to_all(face, GX, 0, 0, tiled=True)  8.56 us
    pallas_call x1, Pallas kernels, columns(): pl.pallas_call(columns_kernel, in_specs=[vmem(), pl.BlockSpec(memory_spac...  7.68 us
    all_to_all x1, starting transfers between devices, on_device(): lax.all_to_all(far.reshape(128, 8, 128), GX + ('gy',), 0, 0, tiled=True)  6.73 us
    pallas_call x1, Pallas kernels, rows_transform(): pl.pallas_call(rows_kernel, in_specs=[vmem(), pl.BlockSpec(memory_space=p...  5.16 us
  transfers between devices with their start and end apart: 6, of which 3 were waited for; matrix products, arithmetic and copies ran while one was open for 0% of the time, Pallas kernels for 16%

profile of v5, /device:TPU:0, one launch (start us, length us, event | category | flops | bytes accessed | tf_op | source)
XLA Modules:
  0.0 126.5 jit_solution(3659197373376641328)
XLA Ops:
  0.6 0.0 copy-start
  0.6 0.0 copy-start.3
  0.7 0.8 copy-done.3
  1.4 1.3 pack_rows.1
  2.7 0.0 copy-start.5
  2.7 1.4 %collective-permute-start = (f32[48,512]{1,0:T(8,128)S(1)}, f32[48,512]{1,0:T(8,128)S(1)}, u32[]{:S(2)}, u32[]{:S(2)}) collective-permute-start(f32[48,512]{1,0:T(8,128)S(1)} %get-tuple-element.16), channel_id=1, source_target_pairs={{0,8},{8,16},{16,24},{24,32},{32,40},{40,48},{48,56},{56,64},{64,7... | collective-permute-start | bytes 294920 | tf_op jit(solution)/shard_map/ppermute | solution.py:732
  4.1 1.3 %collective-permute-start.1 = (f32[48,512]{1,0:T(8,128)S(1)}, f32[48,512]{1,0:T(8,128)S(1)}, u32[]{:S(2)}, u32[]{:S(2)}) collective-permute-start(f32[48,512]{1,0:T(8,128)S(1)} %get-tuple-element.17), channel_id=1, source_target_pairs={{8,0},{16,8},{24,16},{32,24},{40,32},{48,40},{56,48},{64,56},{72,6... | collective-permute-start | bytes 294920 | tf_op jit(solution)/shard_map/ppermute | solution.py:733
  5.4 0.0 copy-done
  5.4 1.4 %scales.1.s_lo.s_hi.scale_in = f32[3,256,512]{2,1,0:T(8,128)S(1)} custom-call(s32[3,256,512]{2,1,0:T(8,128)S(1)} %copy-done, f32[8]{0:T(128)S(1)} %copy-done.3), custom_call_target="tpu_custom_call" | custom-call | flops 1500000000 | bytes 3000000 | tf_op jit(solution)/shard_map/scales/pallas_call | solution.py:91
  6.9 0.0 copy-start.1
  6.9 0.0 copy-done.5
  6.9 0.1 pad_add_fusion.place_ref
  7.0 0.0 copy-start.4
  7.0 0.0 collective-permute-done.top_lo.top_hi.from_top
  7.0 2.2 %collective-permute-done.1.bot_lo.bot_hi.from_bottom = f32[48,512]{1,0:T(8,128)S(1)} collective-permute-done((f32[48,512]{1,0:T(8,128)S(1)}, f32[48,512]{1,0:T(8,128)S(1)}, u32[]{:S(2)}, u32[]{:S(2)}) %collective-permute-start.1) | collective-permute-done | bytes 98336 | tf_op jit(solution)/shard_map/ppermute | solution.py:733
  9.2 3.8 %pack_cols.1 = (f32[136,128]{1,0:T(8,128)S(1)}, f32[136,128]{1,0:T(8,128)S(1)}) custom-call(f32[3,3,256,512]{3,2,1,0:T(8,128)} %e_in.3, f32[3,3,256,512]{3,2,1,0:T(8,128)} %e_in.3, f32[3,3,256,512]{3,2,1,0:T(8,128)} %h_in.3, f32[3,3,256,512]{3,2,1,0:T(8,128)} %h_in.3, f32[3,256,512]{2,1,0:T(8,128)S(1)} %scales.1.s_lo.s_hi.scale_in, ...), custom_call_target="tpu_custom_call" | custom-call | tf_op jit(solution)/shard_map/pack_cols/pallas_call | solution.py:205
  13.0 1.3 %collective-permute-start.3 = (f32[136,128]{1,0:T(8,128)S(1)}, f32[136,128]{1,0:T(8,128)S(1)}, u32[]{:S(2)}, u32[]{:S(2)}) collective-permute-start(f32[136,128]{1,0:T(8,128)S(1)} %get-tuple-element.18), channel_id=1, source_target_pairs={{1,0},{2,1},{3,2},{4,3},{5,4},{6,5},{7,6},{9,8},{10,9},{11,10},{12... | collective-permute-start | bytes 208904 | tf_op jit(solution)/shard_map/ppermute | solution.py:737
  14.3 4.5 %collective-permute-start.2 = (f32[136,128]{1,0:T(8,128)S(1)}, f32[136,128]{1,0:T(8,128)S(1)}, u32[]{:S(2)}, u32[]{:S(2)}) collective-permute-start(f32[136,128]{1,0:T(8,128)S(1)} %get-tuple-element.22), channel_id=1, source_target_pairs={{0,1},{1,2},{2,3},{3,4},{4,5},{5,6},{6,7},{8,9},{9,10},{10,11},{11... | collective-permute-start | bytes 208904 | tf_op jit(solution)/shard_map/ppermute | solution.py:736
  18.9 0.0 copy-done.4
  18.9 3.9 %sources.1 = (f32[3,5,272,128]{3,2,1,0:T(8,128)S(1)}, f32[3,5,272,128]{3,2,1,0:T(8,128)}) custom-call(s32[3,32,128]{2,1,0:T(8,128)S(1)} %bitcast.24, f32[32,128]{1,0:T(8,128)S(1)} %bitcast.25, s32[2]{0:T(128)S(1)} %pad_add_fusion.place_ref), custom_call_target="tpu_custom_call" | custom-call | flops 3000000000 | bytes 3000000 | tf_op jit(solution)/shard_map/sources/pallas_call | solution.py:292
  22.8 0.0 collective-permute-done.3.from_right
  22.8 0.0 collective-permute-done.2.from_left
  22.8 0.0 copy-done.1
  22.8 11.1 %yee_face.1 = bf16[16,256,256]{2,1,0:T(8,128)(2,1)} custom-call(f32[3,3,256,512]{3,2,1,0:T(8,128)} %e_in.3, f32[3,3,256,512]{3,2,1,0:T(8,128)} %h_in.3, f32[3,256,512]{2,1,0:T(8,128)S(1)} %scales.1.s_lo.s_hi.scale_in, f32[3,5,272,128]{3,2,1,0:T(8,128)S(1)} %get-tuple-element.21.grid_in, f32[136,128]{1,0:T(8,128)S(1)} %collective-permute-done.2.from_left, ...), custom_call_target="tpu_custom_call" | custom-call | flops 5000000000 | bytes 40000000 | tf_op jit(solution)/shard_map/yee_face/pallas_call | solution.py:576
  33.9 8.6 %all-to-all-start = ((bf16[16,256,256]{2,1,0:T(8,128)(2,1)}), bf16[16,256,256]{2,1,0:T(8,128)(2,1)S(1)}, u32[]{:S(2)}, u32[]{:S(2)}) async-start(bf16[16,256,256]{2,1,0:T(8,128)(2,1)} %yee_face.1), calls=%async_computation | async-start | bytes 4194304 | tf_op jit(solution)/shard_map/all_to_all | solution.py:752
  42.5 0.0 copy-start.2
  42.5 1.4 %copy-done.2 = f32[3,256,512]{2,1,0:T(8,128)S(1)} copy-done((f32[3,256,512]{2,1,0:T(8,128)S(1)}, f32[3,256,512]{2,1,0:T(8,128)}, u32[]{:S(2)}) %copy-start.2) | copy-done | bytes 1572888
  43.9 14.9 %yee_fields.1 = (f32[3,3,256,512]{3,2,1,0:T(8,128)}, f32[3,3,256,512]{3,2,1,0:T(8,128)}) custom-call(f32[3,3,256,512]{3,2,1,0:T(8,128)} %e_in.3, f32[3,3,256,512]{3,2,1,0:T(8,128)} %h_in.3, f32[3,256,512]{2,1,0:T(8,128)S(1)} %copy-done.2, f32[3,5,272,128]{3,2,1,0:T(8,128)} %get-tuple-element.23.grid_in, f32[136,128]{1,0:T(8,128)S(1)} %collective-permute-done.2.from_left, ...), custom_call_target="tpu_custom_call" | custom-call | flops 5000000000 | bytes 40000000 | tf_op jit(solution)/shard_map/yee_fields/pallas_call | solution.py:576
  58.8 12.5 %all-to-all-done = bf16[16,256,256]{2,1,0:T(8,128)(2,1)S(1)} async-done(((bf16[16,256,256]{2,1,0:T(8,128)(2,1)}), bf16[16,256,256]{2,1,0:T(8,128)(2,1)S(1)}, u32[]{:S(2)}, u32[]{:S(2)}) %all-to-all-start) | async-done | bytes 2097184 | tf_op jit(solution)/shard_map/all_to_all | solution.py:752
  71.3 5.2 %rows_transform.1 = bf16[1280,256]{1,0:T(8,128)(2,1)S(1)} custom-call(bf16[4096,256]{1,0:T(8,128)(2,1)S(1)} %bitcast.21, bf16[1280,4096]{1,0:T(8,128)(2,1)} %constant.25.clone.table_in), custom_call_target="tpu_custom_call" | custom-call | tf_op jit(solution)/shard_map/rows_transform/pallas_call | solution.py:609
  76.4 23.3 %all_to_all.15.rows_ref = bf16[16,80,256]{2,1,0:T(8,128)(2,1)S(1)} all-to-all(bf16[16,80,256]{2,1,0:T(8,128)(2,1)S(1)} %bitcast.22), channel_id=1, replica_groups=mesh['ga'=8,'gc'=2,'gy'=8] {'gc','gy'}, dimensions={0} | all-to-all | bytes 1310720 | tf_op jit(solution)/shard_map/all_to_all | solution.py:755
  99.7 0.0 copy-start.6
  99.7 7.7 %columns.1 = bf16[1024,128]{1,0:T(8,128)(2,1)} custom-call(bf16[16,80,256]{2,1,0:T(8,128)(2,1)S(1)} %all_to_all.15.rows_ref, bf16[16,256,2048]{2,1,0:T(8,128)(2,1)} %constant.26.clone.table_in), custom_call_target="tpu_custom_call" | custom-call | tf_op jit(solution)/shard_map/columns/pallas_call | solution.py:665
  107.4 6.7 %all-to-all-start.2 = ((bf16[128,8,128]{2,1,0:T(8,128)(2,1)}), bf16[128,8,128]{2,1,0:T(8,128)(2,1)S(1)}, u32[]{:S(2)}, u32[]{:S(2)}) async-start(bf16[128,8,128]{2,1,0:T(8,128)(2,1)} %bitcast.26), calls=%async_computation.2 | async-start | bytes 524288 | tf_op jit(solution)/shard_map/all_to_all | solution.py:757
  114.1 0.0 copy-done.6
  114.1 0.1 multiply_bitcast_fusion.3
  114.2 0.1 copy.12
  114.3 0.1 copy.13
  114.4 0.1 copy.14
  114.5 0.1 copy.15
  114.6 0.1 maximum_multiply_fusion.coef_ref
  114.7 10.1 %all-to-all-done.2 = bf16[128,8,128]{2,1,0:T(8,128)(2,1)S(1)} async-done(((bf16[128,8,128]{2,1,0:T(8,128)(2,1)}), bf16[128,8,128]{2,1,0:T(8,128)(2,1)S(1)}, u32[]{:S(2)}, u32[]{:S(2)}) %all-to-all-start.2) | async-done | bytes 262176 | tf_op jit(solution)/shard_map/all_to_all | solution.py:757
  124.8 1.7 %combine.1 = f32[16,64,128]{2,1,0:T(8,128)} custom-call(bf16[64,16,128]{2,1,0:T(8,128)(2,1)S(1)} %bitcast.23, f32[2,4]{1,0:T(2,128)S(1)} %maximum_multiply_fusion.coef_ref, s32[2]{0:T(128)S(1)} %pad_add_fusion.place_ref), custom_call_target="tpu_custom_call" | custom-call | tf_op jit(solution)/shard_map/combine/pallas_call | solution.py:717
  (1 shorter events, 0.0 us)
Async XLA Ops:
  0.6 4.8 %copy-start = (s32[3,256,512]{2,1,0:T(8,128)S(1)}, s32[3,256,512]{2,1,0:T(8,128)}, u32[]{:S(2)}) copy-start(s32[3,256,512]{2,1,0:T(8,128)} %m_hi.1) | copy-start | bytes 4718596
  0.6 0.8 copy-start.3
  2.7 4.2 %copy-start.5 = (s32[4096,3]{0,1:T(4,128)S(1)}, s32[4096,3]{0,1:T(4,128)}, u32[]{:S(2)}) copy-start(s32[4096,3]{0,1:T(4,128)} %param.13) | copy-start | bytes 147460
  2.7 4.3 %collective-permute-start = (f32[48,512]{1,0:T(8,128)S(1)}, f32[48,512]{1,0:T(8,128)S(1)}, u32[]{:S(2)}, u32[]{:S(2)}) collective-permute-start(f32[48,512]{1,0:T(8,128)S(1)} %get-tuple-element.16), channel_id=1, source_target_pairs={{0,8},{8,16},{16,24},{24,32},{32,40},{40,48},{48,56},{56,64},{64,7... | collective-permute-start | bytes 294920 | tf_op jit(solution)/shard_map/ppermute | solution.py:732
  4.1 5.1 %collective-permute-start.1 = (f32[48,512]{1,0:T(8,128)S(1)}, f32[48,512]{1,0:T(8,128)S(1)}, u32[]{:S(2)}, u32[]{:S(2)}) collective-permute-start(f32[48,512]{1,0:T(8,128)S(1)} %get-tuple-element.17), channel_id=1, source_target_pairs={{8,0},{16,8},{24,16},{32,24},{40,32},{48,40},{56,48},{64,56},{72,6... | collective-permute-start | bytes 294920 | tf_op jit(solution)/shard_map/ppermute | solution.py:733
  6.9 16.0 %copy-start.1 = (f32[3,256,512]{2,1,0:T(8,128)}, f32[3,256,512]{2,1,0:T(8,128)S(1)}, u32[]{:S(2)}) copy-start(f32[3,256,512]{2,1,0:T(8,128)S(1)} %scales.1.s_lo.s_hi.scale_in) | copy-start | bytes 4718596
  7.0 11.9 %copy-start.4 = (f32[4096]{0:T(1024)S(1)}, f32[4096]{0:T(1024)}, u32[]{:S(2)}) copy-start(f32[4096]{0:T(1024)} %param.14) | copy-start | bytes 49156
  13.0 9.8 %collective-permute-start.3 = (f32[136,128]{1,0:T(8,128)S(1)}, f32[136,128]{1,0:T(8,128)S(1)}, u32[]{:S(2)}, u32[]{:S(2)}) collective-permute-start(f32[136,128]{1,0:T(8,128)S(1)} %get-tuple-element.18), channel_id=1, source_target_pairs={{1,0},{2,1},{3,2},{4,3},{5,4},{6,5},{7,6},{9,8},{10,9},{11,10},{12... | collective-permute-start | bytes 208904 | tf_op jit(solution)/shard_map/ppermute | solution.py:737
  14.3 8.5 %collective-permute-start.2 = (f32[136,128]{1,0:T(8,128)S(1)}, f32[136,128]{1,0:T(8,128)S(1)}, u32[]{:S(2)}, u32[]{:S(2)}) collective-permute-start(f32[136,128]{1,0:T(8,128)S(1)} %get-tuple-element.22), channel_id=1, source_target_pairs={{0,1},{1,2},{2,3},{3,4},{4,5},{5,6},{6,7},{8,9},{9,10},{10,11},{11... | collective-permute-start | bytes 208904 | tf_op jit(solution)/shard_map/ppermute | solution.py:736
  33.9 37.3 %all-to-all-start = ((bf16[16,256,256]{2,1,0:T(8,128)(2,1)}), bf16[16,256,256]{2,1,0:T(8,128)(2,1)S(1)}, u32[]{:S(2)}, u32[]{:S(2)}) async-start(bf16[16,256,256]{2,1,0:T(8,128)(2,1)} %yee_face.1), calls=%async_computation | async-start | bytes 4194304 | tf_op jit(solution)/shard_map/all_to_all | solution.py:752
  42.5 1.4 %copy-start.2 = (f32[3,256,512]{2,1,0:T(8,128)S(1)}, f32[3,256,512]{2,1,0:T(8,128)}, u32[]{:S(2)}) copy-start(f32[3,256,512]{2,1,0:T(8,128)} %copy-done.1) | copy-start | bytes 4718596
  99.7 14.4 %copy-start.6 = (f32[2]{0:T(128)S(1)}, f32[2]{0:T(128)}, u32[]{:S(2)}) copy-start(f32[2]{0:T(128)} %param.15) | copy-start | bytes 28
  107.4 17.4 %all-to-all-start.2 = ((bf16[128,8,128]{2,1,0:T(8,128)(2,1)}), bf16[128,8,128]{2,1,0:T(8,128)(2,1)S(1)}, u32[]{:S(2)}, u32[]{:S(2)}) async-start(bf16[128,8,128]{2,1,0:T(8,128)(2,1)} %bitcast.26), calls=%async_computation.2 | async-start | bytes 524288 | tf_op jit(solution)/shard_map/all_to_all | solution.py:757

commit v6 on v5

--- a/solution.py
+++ b/solution.py
@@ -24,7 +24,6 @@
 USED_R = 272
 FOLD = 136
 ROW_STEP = 320
-COL_STEP = 256
 CHUNKS = 2
 courant = 0.5
 source_rate = 0.7
@@ -44,10 +43,15 @@
     phase = np.remainder(w * cell, PERIOD) * (2.0 * math.pi / PERIOD)
     x_table = np.stack([np.cos(phase), np.sin(phase)], 2).reshape(16 * 80, N)
     v = np.arange(NA, dtype=np.int64) + NA // 4
-    phase = np.remainder(cell[:, None] * v[None, :], PERIOD) * (2.0 * math.pi / PERIOD)
-    y_table = np.concatenate([np.cos(phase), -np.sin(phase)], 1)
-    y_table = y_table.reshape(8, 2, 256, 2 * NA).transpose(1, 0, 2, 3).reshape(16, 256, 2 * NA)
-    return x_table.astype(ml_dtypes.bfloat16), y_table.astype(ml_dtypes.bfloat16)
+    inner = np.remainder(cell[:256, None] * v[None, :], PERIOD) * (2.0 * math.pi / PERIOD)
+    y_table = np.stack([np.cos(inner), -np.sin(inner)], 1)
+    y_table = y_table.reshape(256, 2, 8, 128).transpose(2, 0, 1, 3).reshape(8, 256, 256)
+    block = (2 * np.arange(8)[None, :] + np.arange(2)[:, None]).reshape(16)
+    outer = np.remainder(256 * block[:, None] * v[None, :], PERIOD) * (2.0 * math.pi / PERIOD)
+    y_phase = np.stack([np.cos(outer), -np.sin(outer)], 1)
+    y_phase = y_phase.reshape(32, 8, 128).transpose(1, 0, 2)
+    half_width = ml_dtypes.bfloat16
+    return x_table.astype(half_width), y_table.astype(half_width), y_phase.astype(np.float32)
 
 
 def params(mib):
@@ -152,20 +156,20 @@
     return jnp.where(sub >= 6 if to_top else sub < 2, value, 0.0)
 
 
+def packed_ends(pair_of, shape):
+    lane = lax.broadcasted_iota(jnp.int32, shape, 1)
+    both = jnp.zeros(shape, F32)
+    for index in range(7 * LZ):
+        lo, hi = pair_of(index)
+        ends = pltpu.roll(jnp.where(lane < 64, lo, hi), 4 * index + 2, 1)
+        both = jnp.where(lane // 4 == index, ends, both)
+    return both
+
+
 def pack_cols_kernel(
-    e_lo, e_hi, h_lo, h_hi, s_lo, s_hi, top_lo, top_hi, bot_lo, bot_hi, left_ref, right_ref,
-    all_rows,
+    e_lo, e_hi, h_lo, h_hi, s_lo, s_hi, own_ref
 ):
     rows = 32
-
-    def packed(pair_of, shape):
-        lane = lax.broadcasted_iota(jnp.int32, shape, 1)
-        both = jnp.zeros(shape, F32)
-        for index in range(7 * LZ):
-            lo, hi = pair_of(index)
-            ends = pltpu.roll(jnp.where(lane < 64, lo, hi), 4 * index + 2, 1)
-            both = jnp.where(lane // 4 == index, ends, both)
-        return both
 
     def strip(s, _):
         r = pl.multiple_of(s * rows, rows)
@@ -179,39 +183,58 @@
                 return h_lo[a - 3, layer, span, :], h_hi[a - 3, layer, span, :]
             return s_lo[layer, span, :], s_hi[layer, span, :]
 
-        all_rows[pl.ds(pl.multiple_of(r + OFF, 8), rows), :] = packed(pair_of, (rows, 128))
+        own_ref[span, :] = packed_ends(pair_of, (rows, 128))
         return 0
 
     lax.fori_loop(0, ROWS // rows, strip, 0)
-    for to_top, lo, hi, r in ((True, top_lo, top_hi, 0), (False, bot_lo, bot_hi, ROWS + OFF)):
-        all_rows[r : r + 8, :] = packed(
-            lambda index: (rim_rows(lo, index, to_top), rim_rows(hi, index, to_top)), (8, 128)
-        )
-    high = lax.broadcasted_iota(jnp.int32, (FOLD, 128), 1) % 4 >= 2
-    near, far = all_rows[0:FOLD, :], all_rows[FOLD:USED_R, :]
-    left_ref[...] = jnp.where(high, near, pltpu.roll(far, 126, 1))
-    right_ref[...] = jnp.where(high, pltpu.roll(far, 2, 1), near)
-
-
-def pack_cols(e, h, scale, from_top, from_bottom):
+
+
+def pack_cols(e, h, scale):
     end = COLS // 128 - 1
     lo4 = pl.BlockSpec((3, LZ, ROWS, 128), lambda r: (0, 0, 0, 0))
     hi4 = pl.BlockSpec((3, LZ, ROWS, 128), lambda r: (0, 0, 0, end))
     lo3 = pl.BlockSpec((LZ, ROWS, 128), lambda r: (0, 0, 0))
     hi3 = pl.BlockSpec((LZ, ROWS, 128), lambda r: (0, 0, end))
-    lo2 = pl.BlockSpec((48, 128), lambda r: (0, 0))
-    hi2 = pl.BlockSpec((48, 128), lambda r: (0, end))
-    out = pl.BlockSpec((FOLD, 128), lambda r: (0, 0))
     return pl.pallas_call(
         pack_cols_kernel,
         grid=(1,),
-        in_specs=[lo4, hi4, lo4, hi4, lo3, hi3, lo2, hi2, lo2, hi2],
-        out_specs=[out, out],
+        in_specs=[lo4, hi4, lo4, hi4, lo3, hi3],
+        out_specs=pl.BlockSpec((ROWS, 128), lambda r: (0, 0)),
+        out_shape=jax.ShapeDtypeStruct((ROWS, 128), F32),
+        compiler_params=params(16),
+        cost_estimate=pl.CostEstimate(
+            flops=2_000_000_000, bytes_accessed=6_000_000, transcendentals=0
+        ),
+        name="pack_cols",
+    )(*stay(e, e, h, h), scale, scale)
+
+
+def fold_cols_kernel(own_ref, top_ref, bottom_ref, left_ref, right_ref, all_rows):
+    end = COLS - 128
+    all_rows[OFF : OFF + ROWS, :] = own_ref[...]
+    for to_top, packed, r in ((True, top_ref, 0), (False, bottom_ref, ROWS + OFF)):
+
+        def pair_of(index):
+            rows = rim_rows(packed, index, to_top)
+            return rows[:, 0:128], rows[:, end:COLS]
+
+        all_rows[r : r + 8, :] = packed_ends(pair_of, (8, 128))
+    high = lax.broadcasted_iota(jnp.int32, (FOLD, 128), 1) % 4 >= 2
+    near, far = all_rows[0:FOLD, :], all_rows[FOLD:USED_R, :]
+    left_ref[...] = jnp.where(high, near, pltpu.roll(far, 126, 1))
+    right_ref[...] = jnp.where(high, pltpu.roll(far, 2, 1), near)
+
+
+def fold_cols(own, from_top, from_bottom):
+    return pl.pallas_call(
+        fold_cols_kernel,
+        in_specs=[vmem()] * 3,
+        out_specs=[vmem()] * 2,
         out_shape=[jax.ShapeDtypeStruct((FOLD, 128), F32)] * 2,
         scratch_shapes=[pltpu.VMEM((USED_R, 128), F32)],
-        compiler_params=params(16),
-        name="pack_cols",
-    )(*stay(e, e, h, h), scale, scale, from_top, from_top, from_bottom, from_bottom)
+        compiler_params=params(4),
+        name="fold_cols",
+    )(own, from_top, from_bottom)
 
 
 def rim_tile(both, index):
@@ -617,26 +640,23 @@
     )(field, *stay(table))
 
 
-def columns_kernel(rows_ref, table_in, out_ref, table, total, spread, sem):
-    def copy_of(s):
-        cols = pl.ds(pl.multiple_of(s * COL_STEP, COL_STEP), COL_STEP)
-        return cols, pltpu.make_async_copy(
-            table_in.at[:, :, cols], table.at[:, :, cols], sem.at[s]
-        )
-
-    for s in range(2 * NA // COL_STEP):
-        copy_of(s)[1].start()
-
-    def width(s, _):
-        cols, copy = copy_of(s)
-        copy.wait()
-        part = jnp.dot(rows_ref[0], table[0, :, cols], preferred_element_type=F32)
-        for g in range(1, 16):
-            part += jnp.dot(rows_ref[g], table[g, :, cols], preferred_element_type=F32)
-        total[:, cols] = part
+def columns_kernel(rows_ref, table_ref, phase_ref, out_ref, product, total, spread):
+    def width(c, _):
+        product[...] = jnp.dot(rows_ref[...], table_ref[c], preferred_element_type=F32)
+        sum_re = jnp.zeros((80, 128), F32)
+        sum_im = jnp.zeros((80, 128), F32)
+        for b in range(16):
+            part_re = product[80 * b : 80 * b + 80, 0:128]
+            part_im = product[80 * b : 80 * b + 80, 128:256]
+            turn_re = phase_ref[c, 2 * b : 2 * b + 1, :]
+            turn_im = phase_ref[c, 2 * b + 1 : 2 * b + 2, :]
+            sum_re += turn_re * part_re - turn_im * part_im
+            sum_im += turn_re * part_im + turn_im * part_re
+        total[:, pl.ds(pl.multiple_of(128 * c, 128), 128)] = sum_re
+        total[:, pl.ds(pl.multiple_of(NA + 128 * c, 128), 128)] = sum_im
         return 0
 
-    lax.fori_loop(0, 2 * NA // COL_STEP, width, 0)
+    lax.fori_loop(0, 8, width, 0, unroll=2)
     sub = lax.broadcasted_iota(jnp.int32, (8, NA), 0)
 
     def flip(value):
@@ -661,21 +681,20 @@
     out_ref[...] = spread[...].astype(BF16)
 
 
-def columns(rows, table):
+def columns(rows, table, phase):
     return pl.pallas_call(
         columns_kernel,
-        in_specs=[vmem(), pl.BlockSpec(memory_space=pl.ANY)],
+        in_specs=[vmem(), vmem(), vmem()],
         out_specs=vmem(),
         out_shape=pltpu.HBM((1024, 128), BF16),
         scratch_shapes=[
-            pltpu.VMEM((16, 256, 2 * NA), BF16),
+            pltpu.VMEM((1280, 256), F32),
             pltpu.VMEM((80, 2 * NA), F32),
             pltpu.VMEM((1024, 128), F32),
-            pltpu.SemaphoreType.DMA((2 * NA // COL_STEP,)),
         ],
-        compiler_params=params(24),
+        compiler_params=params(12),
         name="columns",
-    )(rows, *stay(table))
+    )(rows, table, phase)
 
 
 def combine_kernel(parts_ref, coef_ref, place_ref, out_ref):
@@ -724,7 +743,7 @@
     )(parts, coef, place)
 
 
-def on_device(x_table, y_table, e, h, material, eps, src_pos, src_amp, freqs):
+def on_device(x_table, y_table, y_phase, e, h, material, eps, src_pos, src_amp, freqs):
     row_place = lax.axis_index(GX)
     col_place = lax.axis_index("gy")
     place = jnp.stack([row_place, col_place]).astype(jnp.int32)
@@ -732,7 +751,8 @@
     from_top = lax.ppermute(down, GX, [(k, k + 1) for k in range(15)])
     from_bottom = lax.ppermute(up, GX, [(k + 1, k) for k in range(15)])
     scale = scales(material, eps)
-    left, right = pack_cols(e, h, scale, from_top, from_bottom)
+    own = pack_cols(e, h, scale)
+    left, right = fold_cols(own, from_top, from_bottom)
     from_left = lax.ppermute(right, "gy", [(k, k + 1) for k in range(7)])
     from_right = lax.ppermute(left, "gy", [(k + 1, k) for k in range(7)])
     pos = src_pos.T.reshape(3, NSRC // 128, 128)
@@ -753,7 +773,7 @@
     face, e_out, h_out = lax.optimization_barrier((face, e_out, h_out))
     rows = rows_transform(face.reshape(N, 256), x_table)
     rows = lax.all_to_all(rows.reshape(16, 80, 256), ("gc", "gy"), 0, 0, tiled=True)
-    far = columns(rows, y_table)
+    far = columns(rows.reshape(1280, 256), y_table, y_phase)
     far = lax.all_to_all(far.reshape(128, 8, 128), GX + ("gy",), 0, 0, tiled=True)
     far = combine(far.reshape(64, 16, 128), coef, place)
     return e_out, h_out, far.reshape(64, 8, 2, 128)
@@ -762,7 +782,7 @@
 def solution(mesh):
     fine = Mesh(mesh.devices.reshape(8, 2, 8), ("ga", "gc", "gy"))
     field = P(None, None, GX, "gy")
-    placed = (P(), P(), field, field, P(None, GX, "gy"), P(), P(), P(), P())
+    placed = (P(), P(), P(), field, field, P(None, GX, "gy"), P(), P(), P(), P())
     mapped = jax.shard_map(
         on_device,
         mesh=fine,
@@ -770,11 +790,11 @@
         out_specs=(field, field, P(GX, None, None, "gy")),
         check_vma=False,
     )
-    x_table, y_table = tables()
+    constants = tables()
 
     def program(e_field, h_field, material, eps_table, src_pos, src_amp, freqs):
         return mapped(
-            x_table, y_table, e_field, h_field, material, eps_table, src_pos, src_amp, freqs
+            *constants, e_field, h_field, material, eps_table, src_pos, src_amp, freqs
         )
 
     return program

time: 127 us -> 122 us (0.961)
  Pallas kernels: 50.8 us -> 47 us
  waiting for transfers between devices: 24.9 us -> 22.6 us
    pallas_call x1 -> x2, Pallas kernels: 7.68 us -> 3.36 us  [the longest x1 3.2 us: columns(): pl.pallas_call(columns_kernel, in_specs=[vmem(), vmem(), vmem()], out_spe...]
    ppermute x1, waiting for transfers between devices: 2.22 us -> 0.01 us  [on_device(): from_bottom = lax.ppermute(up, GX, [(k + 1, k) for k in range(15)])]
  transfers between devices with their start and end apart: 6 -> 6, of which waited for: 3 -> 2; matrix products, arithmetic and copies ran while one was open for 0% -> 0% of each run, Pallas kernels for 16% -> 20%
where the time goes in v6:
time: 122 us; the launch traced here: 121 us
  Pallas kernels  47 us (39%)
  blocking collectives  24.4 us (20%)
  starting transfers between devices  23.7 us (19%)
  waiting for transfers between devices  22.6 us (19%)
  local copies, waits for them, and re-layouts  2.58 us (2%)
    pallas_call x2, Pallas kernels, yee(): pl.pallas_call(functools.partial(yee_kernel, with_fields, with_face), in_...  25.9 us
    all_to_all x1, blocking collectives, on_device(): lax.all_to_all(rows.reshape(16, 80, 256), ('gc', 'gy'), 0, 0, tiled=True)  24.4 us
    all_to_all x1, waiting for transfers between devices, on_device(): face = lax.all_to_all(face, GX, 0, 0, tiled=True)  12.5 us
    all_to_all x1, waiting for transfers between devices, on_device(): lax.all_to_all(far.reshape(128, 8, 128), GX + ('gy',), 0, 0, tiled=True)  10.1 us
    all_to_all x1, starting transfers between devices, on_device(): face = lax.all_to_all(face, GX, 0, 0, tiled=True)  8.14 us
    all_to_all x1, starting transfers between devices, on_device(): lax.all_to_all(far.reshape(128, 8, 128), GX + ('gy',), 0, 0, tiled=True)  6.73 us
    pallas_call x1, Pallas kernels, rows_transform(): pl.pallas_call(rows_kernel, in_specs=[vmem(), pl.BlockSpec(memory_space=p...  5.25 us
    ppermute x1, starting transfers between devices, on_device(): from_left = lax.ppermute(right, 'gy', [(k, k + 1) for k in range(7)])  4.99 us
  transfers between devices with their start and end apart: 6, of which 2 were waited for; matrix products, arithmetic and copies ran while one was open for 0% of the time, Pallas kernels for 20%

profile of v6, /device:TPU:0, one launch (start us, length us, event | category | flops | bytes accessed | tf_op | source)
XLA Modules:
  0.0 121.4 jit_solution(2918688336202895429)
XLA Ops:
  0.6 0.0 copy-start
  0.6 0.0 copy-start.5
  0.7 0.8 copy-done.5
  1.4 1.3 %pack_rows.1 = (f32[48,512]{1,0:T(8,128)S(1)}, f32[48,512]{1,0:T(8,128)S(1)}) custom-call(f32[3,3,256,512]{3,2,1,0:T(8,128)} %e_in.3, f32[3,3,256,512]{3,2,1,0:T(8,128)} %e_in.3, f32[3,3,256,512]{3,2,1,0:T(8,128)} %h_in.3, f32[3,3,256,512]{3,2,1,0:T(8,128)} %h_in.3, s32[3,256,512]{2,1,0:T(8,128)} %m_hi.1, s32[3,256,512]{2,1,0:T(8,128)} %m_hi.1, f32[8]{0:T(128)S(1)} %copy-done.5), custom_call_target="tpu_custom_call" | custom-call | tf_op jit(solution)/shard_map/pack_rows/pallas_call | solution.py:139
  2.7 1.3 %collective-permute-start = (f32[48,512]{1,0:T(8,128)S(1)}, f32[48,512]{1,0:T(8,128)S(1)}, u32[]{:S(2)}, u32[]{:S(2)}) collective-permute-start(f32[48,512]{1,0:T(8,128)S(1)} %get-tuple-element.16), channel_id=1, source_target_pairs={{0,8},{8,16},{16,24},{24,32},{32,40},{40,48},{48,56},{56,64},{64,7... | collective-permute-start | bytes 294920 | tf_op jit(solution)/shard_map/ppermute | solution.py:751
  4.0 1.3 %collective-permute-start.1 = (f32[48,512]{1,0:T(8,128)S(1)}, f32[48,512]{1,0:T(8,128)S(1)}, u32[]{:S(2)}, u32[]{:S(2)}) collective-permute-start(f32[48,512]{1,0:T(8,128)S(1)} %get-tuple-element.17), channel_id=1, source_target_pairs={{8,0},{16,8},{24,16},{32,24},{40,32},{48,40},{56,48},{64,56},{72,6... | collective-permute-start | bytes 294920 | tf_op jit(solution)/shard_map/ppermute | solution.py:752
  5.3 0.0 copy-done
  5.3 1.4 %scales.1.s_lo.s_hi.scale_in = f32[3,256,512]{2,1,0:T(8,128)S(1)} custom-call(s32[3,256,512]{2,1,0:T(8,128)S(1)} %copy-done, f32[8]{0:T(128)S(1)} %copy-done.5), custom_call_target="tpu_custom_call" | custom-call | flops 1500000000 | bytes 3000000 | tf_op jit(solution)/shard_map/scales/pallas_call | solution.py:95
  6.7 0.0 copy-start.1
  6.7 0.0 copy-start.7
  6.7 0.0 copy-start.6
  6.8 4.2 %pack_cols.1.own_ref = f32[256,128]{1,0:T(8,128)S(1)} custom-call(f32[3,3,256,512]{3,2,1,0:T(8,128)} %e_in.3, f32[3,3,256,512]{3,2,1,0:T(8,128)} %e_in.3, f32[3,3,256,512]{3,2,1,0:T(8,128)} %h_in.3, f32[3,3,256,512]{3,2,1,0:T(8,128)} %h_in.3, f32[3,256,512]{2,1,0:T(8,128)S(1)} %scales.1.s_lo.s_hi.scale_in, f32[3,256,512]{2,1,0:T(8,128)S(1)} %scales.1.s_lo.s_hi.scale_in), custom_call_target="tpu_custom_call" | custom-call | flops 2000000000 | bytes 6000000 | tf_op jit(solution)/shard_map/pack_cols/pallas_call | solution.py:198
  11.0 0.0 copy-done.7
  11.0 0.1 pad_add_fusion.place_ref
  11.1 0.0 collective-permute-done.top_ref.from_top
  11.1 0.0 collective-permute-done.1.bottom_ref.from_bottom
  11.1 0.2 fold_cols.1
  11.3 1.3 %collective-permute-start.3 = (f32[136,128]{1,0:T(8,128)S(1)}, f32[136,128]{1,0:T(8,128)S(1)}, u32[]{:S(2)}, u32[]{:S(2)}) collective-permute-start(f32[136,128]{1,0:T(8,128)S(1)} %get-tuple-element.18), channel_id=1, source_target_pairs={{1,0},{2,1},{3,2},{4,3},{5,4},{6,5},{7,6},{9,8},{10,9},{11,10},{12... | collective-permute-start | bytes 208904 | tf_op jit(solution)/shard_map/ppermute | solution.py:757
  12.6 5.0 %collective-permute-start.2 = (f32[136,128]{1,0:T(8,128)S(1)}, f32[136,128]{1,0:T(8,128)S(1)}, u32[]{:S(2)}, u32[]{:S(2)}) collective-permute-start(f32[136,128]{1,0:T(8,128)S(1)} %get-tuple-element.22), channel_id=1, source_target_pairs={{0,1},{1,2},{2,3},{3,4},{4,5},{5,6},{6,7},{8,9},{9,10},{10,11},{11... | collective-permute-start | bytes 208904 | tf_op jit(solution)/shard_map/ppermute | solution.py:756
  17.6 0.0 copy-done.6
  17.6 3.9 %sources.1 = (f32[3,5,272,128]{3,2,1,0:T(8,128)S(1)}, f32[3,5,272,128]{3,2,1,0:T(8,128)}) custom-call(s32[3,32,128]{2,1,0:T(8,128)S(1)} %bitcast.26, f32[32,128]{1,0:T(8,128)S(1)} %bitcast.27, s32[2]{0:T(128)S(1)} %pad_add_fusion.place_ref), custom_call_target="tpu_custom_call" | custom-call | flops 3000000000 | bytes 3000000 | tf_op jit(solution)/shard_map/sources/pallas_call | solution.py:315
  21.5 0.0 collective-permute-done.3.from_right
  21.5 0.0 collective-permute-done.2.from_left
  21.5 0.0 copy-done.1
  21.5 11.1 %yee_face.1 = bf16[16,256,256]{2,1,0:T(8,128)(2,1)} custom-call(f32[3,3,256,512]{3,2,1,0:T(8,128)} %e_in.3, f32[3,3,256,512]{3,2,1,0:T(8,128)} %h_in.3, f32[3,256,512]{2,1,0:T(8,128)S(1)} %scales.1.s_lo.s_hi.scale_in, f32[3,5,272,128]{3,2,1,0:T(8,128)S(1)} %get-tuple-element.21.grid_in, f32[136,128]{1,0:T(8,128)S(1)} %collective-permute-done.2.from_left, ...), custom_call_target="tpu_custom_call" | custom-call | flops 5000000000 | bytes 40000000 | tf_op jit(solution)/shard_map/yee_face/pallas_call | solution.py:599
  32.6 8.1 %all-to-all-start = ((bf16[16,256,256]{2,1,0:T(8,128)(2,1)}), bf16[16,256,256]{2,1,0:T(8,128)(2,1)S(1)}, u32[]{:S(2)}, u32[]{:S(2)}) async-start(bf16[16,256,256]{2,1,0:T(8,128)(2,1)} %yee_face.1), calls=%async_computation | async-start | bytes 4194304 | tf_op jit(solution)/shard_map/all_to_all | solution.py:772
  40.7 0.0 copy-start.2
  40.8 1.4 %copy-done.2 = f32[3,256,512]{2,1,0:T(8,128)S(1)} copy-done((f32[3,256,512]{2,1,0:T(8,128)S(1)}, f32[3,256,512]{2,1,0:T(8,128)}, u32[]{:S(2)}) %copy-start.2) | copy-done | bytes 1572888
  42.1 14.9 %yee_fields.1 = (f32[3,3,256,512]{3,2,1,0:T(8,128)}, f32[3,3,256,512]{3,2,1,0:T(8,128)}) custom-call(f32[3,3,256,512]{3,2,1,0:T(8,128)} %e_in.3, f32[3,3,256,512]{3,2,1,0:T(8,128)} %h_in.3, f32[3,256,512]{2,1,0:T(8,128)S(1)} %copy-done.2, f32[3,5,272,128]{3,2,1,0:T(8,128)} %get-tuple-element.23.grid_in, f32[136,128]{1,0:T(8,128)S(1)} %collective-permute-done.2.from_left, ...), custom_call_target="tpu_custom_call" | custom-call | flops 5000000000 | bytes 40000000 | tf_op jit(solution)/shard_map/yee_fields/pallas_call | solution.py:599
  57.0 12.5 %all-to-all-done = bf16[16,256,256]{2,1,0:T(8,128)(2,1)S(1)} async-done(((bf16[16,256,256]{2,1,0:T(8,128)(2,1)}), bf16[16,256,256]{2,1,0:T(8,128)(2,1)S(1)}, u32[]{:S(2)}, u32[]{:S(2)}) %all-to-all-start) | async-done | bytes 2097184 | tf_op jit(solution)/shard_map/all_to_all | solution.py:772
  69.5 0.0 copy-start.3
  69.5 0.0 copy-start.4
  69.5 5.3 %rows_transform.1 = bf16[1280,256]{1,0:T(8,128)(2,1)S(1)} custom-call(bf16[4096,256]{1,0:T(8,128)(2,1)S(1)} %bitcast.22, bf16[1280,4096]{1,0:T(8,128)(2,1)} %constant.27.clone.table_in), custom_call_target="tpu_custom_call" | custom-call | tf_op jit(solution)/shard_map/rows_transform/pallas_call | solution.py:632
  74.8 0.0 copy-start.8
  74.8 24.4 %all_to_all.15 = bf16[16,80,256]{2,1,0:T(8,128)(2,1)S(1)} all-to-all(bf16[16,80,256]{2,1,0:T(8,128)(2,1)S(1)} %bitcast.23), channel_id=1, replica_groups=mesh['ga'=8,'gc'=2,'gy'=8] {'gc','gy'}, dimensions={0} | all-to-all | bytes 1310720 | tf_op jit(solution)/shard_map/all_to_all | solution.py:775
  99.1 0.0 copy-done.3
  99.1 0.0 copy-done.4
  99.2 3.2 %columns.1 = bf16[1024,128]{1,0:T(8,128)(2,1)} custom-call(bf16[1280,256]{1,0:T(8,128)(2,1)S(1)} %bitcast.24, bf16[8,256,256]{2,1,0:T(8,128)(2,1)S(1)} %copy-done.3, f32[8,32,128]{2,1,0:T(8,128)S(1)} %copy-done.4), custom_call_target="tpu_custom_call" | custom-call | tf_op jit(solution)/shard_map/columns/pallas_call | solution.py:685
  102.3 6.7 %all-to-all-start.2 = ((bf16[128,8,128]{2,1,0:T(8,128)(2,1)}), bf16[128,8,128]{2,1,0:T(8,128)(2,1)S(1)}, u32[]{:S(2)}, u32[]{:S(2)}) async-start(bf16[128,8,128]{2,1,0:T(8,128)(2,1)} %bitcast.28), calls=%async_computation.2 | async-start | bytes 524288 | tf_op jit(solution)/shard_map/all_to_all | solution.py:777
  109.1 0.0 copy-done.8
  109.1 0.1 multiply_bitcast_fusion.3
  109.1 0.1 copy.13
  109.2 0.1 copy.14
  109.3 0.1 copy.15
  109.4 0.1 copy.16
  109.5 0.1 maximum_multiply_fusion.coef_ref
  109.6 10.1 %all-to-all-done.2 = bf16[128,8,128]{2,1,0:T(8,128)(2,1)S(1)} async-done(((bf16[128,8,128]{2,1,0:T(8,128)(2,1)}), bf16[128,8,128]{2,1,0:T(8,128)(2,1)S(1)}, u32[]{:S(2)}, u32[]{:S(2)}) %all-to-all-start.2) | async-done | bytes 262176 | tf_op jit(solution)/shard_map/all_to_all | solution.py:777
  119.7 1.7 %combine.1 = f32[16,64,128]{2,1,0:T(8,128)} custom-call(bf16[64,16,128]{2,1,0:T(8,128)(2,1)S(1)} %bitcast.25, f32[2,4]{1,0:T(2,128)S(1)} %maximum_multiply_fusion.coef_ref, s32[2]{0:T(128)S(1)} %pad_add_fusion.place_ref), custom_call_target="tpu_custom_call" | custom-call | tf_op jit(solution)/shard_map/combine/pallas_call | solution.py:736
  (1 shorter events, 0.0 us)
Async XLA Ops:
  0.6 4.7 %copy-start = (s32[3,256,512]{2,1,0:T(8,128)S(1)}, s32[3,256,512]{2,1,0:T(8,128)}, u32[]{:S(2)}) copy-start(s32[3,256,512]{2,1,0:T(8,128)} %m_hi.1) | copy-start | bytes 4718596
  0.6 0.8 copy-start.5
  2.7 8.4 %collective-permute-start = (f32[48,512]{1,0:T(8,128)S(1)}, f32[48,512]{1,0:T(8,128)S(1)}, u32[]{:S(2)}, u32[]{:S(2)}) collective-permute-start(f32[48,512]{1,0:T(8,128)S(1)} %get-tuple-element.16), channel_id=1, source_target_pairs={{0,8},{8,16},{16,24},{24,32},{32,40},{40,48},{48,56},{56,64},{64,7... | collective-permute-start | bytes 294920 | tf_op jit(solution)/shard_map/ppermute | solution.py:751
  4.0 7.1 %collective-permute-start.1 = (f32[48,512]{1,0:T(8,128)S(1)}, f32[48,512]{1,0:T(8,128)S(1)}, u32[]{:S(2)}, u32[]{:S(2)}) collective-permute-start(f32[48,512]{1,0:T(8,128)S(1)} %get-tuple-element.17), channel_id=1, source_target_pairs={{8,0},{16,8},{24,16},{32,24},{40,32},{48,40},{56,48},{64,56},{72,6... | collective-permute-start | bytes 294920 | tf_op jit(solution)/shard_map/ppermute | solution.py:752
  6.7 14.8 %copy-start.1 = (f32[3,256,512]{2,1,0:T(8,128)}, f32[3,256,512]{2,1,0:T(8,128)S(1)}, u32[]{:S(2)}) copy-start(f32[3,256,512]{2,1,0:T(8,128)S(1)} %scales.1.s_lo.s_hi.scale_in) | copy-start | bytes 4718596
  6.7 4.3 %copy-start.7 = (s32[4096,3]{0,1:T(4,128)S(1)}, s32[4096,3]{0,1:T(4,128)}, u32[]{:S(2)}) copy-start(s32[4096,3]{0,1:T(4,128)} %param.14) | copy-start | bytes 147460
  6.7 10.8 %copy-start.6 = (f32[4096]{0:T(1024)S(1)}, f32[4096]{0:T(1024)}, u32[]{:S(2)}) copy-start(f32[4096]{0:T(1024)} %param.15) | copy-start | bytes 49156
  11.3 10.2 %collective-permute-start.3 = (f32[136,128]{1,0:T(8,128)S(1)}, f32[136,128]{1,0:T(8,128)S(1)}, u32[]{:S(2)}, u32[]{:S(2)}) collective-permute-start(f32[136,128]{1,0:T(8,128)S(1)} %get-tuple-element.18), channel_id=1, source_target_pairs={{1,0},{2,1},{3,2},{4,3},{5,4},{6,5},{7,6},{9,8},{10,9},{11,10},{12... | collective-permute-start | bytes 208904 | tf_op jit(solution)/shard_map/ppermute | solution.py:757
  12.6 8.9 %collective-permute-start.2 = (f32[136,128]{1,0:T(8,128)S(1)}, f32[136,128]{1,0:T(8,128)S(1)}, u32[]{:S(2)}, u32[]{:S(2)}) collective-permute-start(f32[136,128]{1,0:T(8,128)S(1)} %get-tuple-element.22), channel_id=1, source_target_pairs={{0,1},{1,2},{2,3},{3,4},{4,5},{5,6},{6,7},{8,9},{9,10},{10,11},{11... | collective-permute-start | bytes 208904 | tf_op jit(solution)/shard_map/ppermute | solution.py:756
  32.6 36.9 %all-to-all-start = ((bf16[16,256,256]{2,1,0:T(8,128)(2,1)}), bf16[16,256,256]{2,1,0:T(8,128)(2,1)S(1)}, u32[]{:S(2)}, u32[]{:S(2)}) async-start(bf16[16,256,256]{2,1,0:T(8,128)(2,1)} %yee_face.1), calls=%async_computation | async-start | bytes 4194304 | tf_op jit(solution)/shard_map/all_to_all | solution.py:772
  40.7 1.4 %copy-start.2 = (f32[3,256,512]{2,1,0:T(8,128)S(1)}, f32[3,256,512]{2,1,0:T(8,128)}, u32[]{:S(2)}) copy-start(f32[3,256,512]{2,1,0:T(8,128)} %copy-done.1) | copy-start | bytes 4718596
  69.5 29.6 %copy-start.3 = (bf16[8,256,256]{2,1,0:T(8,128)(2,1)S(1)}, bf16[8,256,256]{2,1,0:T(8,128)(2,1)}, u32[]{:S(2)}) copy-start(bf16[8,256,256]{2,1,0:T(8,128)(2,1)} %constant.28.clone.table_ref) | copy-start | bytes 3145732
  69.5 29.6 %copy-start.4 = (f32[8,32,128]{2,1,0:T(8,128)S(1)}, f32[8,32,128]{2,1,0:T(8,128)}, u32[]{:S(2)}) copy-start(f32[8,32,128]{2,1,0:T(8,128)} %constant.29.clone.phase_ref) | copy-start | bytes 393220
  74.8 34.3 %copy-start.8 = (f32[2]{0:T(128)S(1)}, f32[2]{0:T(128)}, u32[]{:S(2)}) copy-start(f32[2]{0:T(128)} %param.16) | copy-start | bytes 28
  102.3 17.4 %all-to-all-start.2 = ((bf16[128,8,128]{2,1,0:T(8,128)(2,1)}), bf16[128,8,128]{2,1,0:T(8,128)(2,1)S(1)}, u32[]{:S(2)}, u32[]{:S(2)}) async-start(bf16[128,8,128]{2,1,0:T(8,128)(2,1)} %bitcast.28), calls=%async_computation.2 | async-start | bytes 524288 | tf_op jit(solution)/shard_map/all_to_all | solution.py:777

commit v7 on v6

--- a/solution.py
+++ b/solution.py
@@ -144,7 +144,7 @@
         out_shape=[jax.ShapeDtypeStruct((48, COLS), F32)] * 2,
         compiler_params=params(8),
         name="pack_rows",
-    )(*stay(e, e, h, h, material, material), eps)
+    )(*stay(e, e, h, h, material, material, eps))
 
 
 def rim_rows(packed, index, to_top):

time: 122 us -> 121 us (level)
  no operation moved by 1% of the time
where the time goes in v7:
time: 121 us
  Pallas kernels  47.1 us (39%)
  blocking collectives  24.4 us (20%)
  starting transfers between devices  23.7 us (20%)
  waiting for transfers between devices  22.6 us (19%)
  local copies, waits for them, and re-layouts  1.82 us (2%)
    pallas_call x2, Pallas kernels, yee(): pl.pallas_call(functools.partial(yee_kernel, with_fields, with_face), in_...  25.9 us
    all_to_all x1, blocking collectives, on_device(): lax.all_to_all(rows.reshape(16, 80, 256), ('gc', 'gy'), 0, 0, tiled=True)  24.4 us
    all_to_all x1, waiting for transfers between devices, on_device(): face = lax.all_to_all(face, GX, 0, 0, tiled=True)  12.5 us
    all_to_all x1, waiting for transfers between devices, on_device(): lax.all_to_all(far.reshape(128, 8, 128), GX + ('gy',), 0, 0, tiled=True)  10.1 us
    all_to_all x1, starting transfers between devices, on_device(): face = lax.all_to_all(face, GX, 0, 0, tiled=True)  8.14 us
    all_to_all x1, starting transfers between devices, on_device(): lax.all_to_all(far.reshape(128, 8, 128), GX + ('gy',), 0, 0, tiled=True)  6.73 us
    pallas_call x1, Pallas kernels, rows_transform(): pl.pallas_call(rows_kernel, in_specs=[vmem(), pl.BlockSpec(memory_space=p...  5.25 us
    ppermute x1, starting transfers between devices, on_device(): from_left = lax.ppermute(right, 'gy', [(k, k + 1) for k in range(7)])  4.99 us
  transfers between devices with their start and end apart: 6, of which 2 were waited for; matrix products, arithmetic and copies ran while one was open for 0% of the time, Pallas kernels for 20%

profile of v7, /device:TPU:0, one launch (start us, length us, event | category | flops | bytes accessed | tf_op | source)
XLA Modules:
  0.0 120.8 jit_solution(14592131826595958239)
XLA Ops:
  0.6 0.0 copy-start
  0.6 0.0 copy-start.5
  0.7 1.4 %pack_rows.1 = (f32[48,512]{1,0:T(8,128)S(1)}, f32[48,512]{1,0:T(8,128)S(1)}) custom-call(f32[3,3,256,512]{3,2,1,0:T(8,128)} %e_in.3, f32[3,3,256,512]{3,2,1,0:T(8,128)} %e_in.3, f32[3,3,256,512]{3,2,1,0:T(8,128)} %h_in.3, f32[3,3,256,512]{3,2,1,0:T(8,128)} %h_in.3, s32[3,256,512]{2,1,0:T(8,128)} %m_hi.1, s32[3,256,512]{2,1,0:T(8,128)} %m_hi.1, f32[8]{0:T(128)} %eps_ref.3), custom_call_target="tpu_custom_call" | custom-call | tf_op jit(solution)/shard_map/pack_rows/pallas_call | solution.py:139
  2.0 1.3 %collective-permute-start = (f32[48,512]{1,0:T(8,128)S(1)}, f32[48,512]{1,0:T(8,128)S(1)}, u32[]{:S(2)}, u32[]{:S(2)}) collective-permute-start(f32[48,512]{1,0:T(8,128)S(1)} %get-tuple-element.16), channel_id=1, source_target_pairs={{0,8},{8,16},{16,24},{24,32},{32,40},{40,48},{48,56},{56,64},{64,7... | collective-permute-start | bytes 294920 | tf_op jit(solution)/shard_map/ppermute | solution.py:751
  3.3 1.3 %collective-permute-start.1 = (f32[48,512]{1,0:T(8,128)S(1)}, f32[48,512]{1,0:T(8,128)S(1)}, u32[]{:S(2)}, u32[]{:S(2)}) collective-permute-start(f32[48,512]{1,0:T(8,128)S(1)} %get-tuple-element.17), channel_id=1, source_target_pairs={{8,0},{16,8},{24,16},{32,24},{40,32},{48,40},{56,48},{64,56},{72,6... | collective-permute-start | bytes 294920 | tf_op jit(solution)/shard_map/ppermute | solution.py:752
  4.6 0.0 copy-done
  4.6 0.0 copy-done.5
  4.7 1.4 %scales.1.s_lo.s_hi.scale_in = f32[3,256,512]{2,1,0:T(8,128)S(1)} custom-call(s32[3,256,512]{2,1,0:T(8,128)S(1)} %copy-done, f32[8]{0:T(128)S(1)} %copy-done.5), custom_call_target="tpu_custom_call" | custom-call | flops 1500000000 | bytes 3000000 | tf_op jit(solution)/shard_map/scales/pallas_call | solution.py:95
  6.1 0.0 copy-start.1
  6.1 0.0 copy-start.7
  6.1 0.0 copy-start.6
  6.1 4.2 %pack_cols.1.own_ref = f32[256,128]{1,0:T(8,128)S(1)} custom-call(f32[3,3,256,512]{3,2,1,0:T(8,128)} %e_in.3, f32[3,3,256,512]{3,2,1,0:T(8,128)} %e_in.3, f32[3,3,256,512]{3,2,1,0:T(8,128)} %h_in.3, f32[3,3,256,512]{3,2,1,0:T(8,128)} %h_in.3, f32[3,256,512]{2,1,0:T(8,128)S(1)} %scales.1.s_lo.s_hi.scale_in, f32[3,256,512]{2,1,0:T(8,128)S(1)} %scales.1.s_lo.s_hi.scale_in), custom_call_target="tpu_custom_call" | custom-call | flops 2000000000 | bytes 6000000 | tf_op jit(solution)/shard_map/pack_cols/pallas_call | solution.py:198
  10.4 0.0 copy-done.7
  10.4 0.1 pad_add_fusion.place_ref
  10.5 0.0 collective-permute-done.top_ref.from_top
  10.5 0.0 collective-permute-done.1.bottom_ref.from_bottom
  10.5 0.2 fold_cols.1
  10.6 1.3 %collective-permute-start.3 = (f32[136,128]{1,0:T(8,128)S(1)}, f32[136,128]{1,0:T(8,128)S(1)}, u32[]{:S(2)}, u32[]{:S(2)}) collective-permute-start(f32[136,128]{1,0:T(8,128)S(1)} %get-tuple-element.18), channel_id=1, source_target_pairs={{1,0},{2,1},{3,2},{4,3},{5,4},{6,5},{7,6},{9,8},{10,9},{11,10},{12... | collective-permute-start | bytes 208904 | tf_op jit(solution)/shard_map/ppermute | solution.py:757
  11.9 5.0 %collective-permute-start.2 = (f32[136,128]{1,0:T(8,128)S(1)}, f32[136,128]{1,0:T(8,128)S(1)}, u32[]{:S(2)}, u32[]{:S(2)}) collective-permute-start(f32[136,128]{1,0:T(8,128)S(1)} %get-tuple-element.22), channel_id=1, source_target_pairs={{0,1},{1,2},{2,3},{3,4},{4,5},{5,6},{6,7},{8,9},{9,10},{10,11},{11... | collective-permute-start | bytes 208904 | tf_op jit(solution)/shard_map/ppermute | solution.py:756
  16.9 0.0 copy-done.6
  16.9 3.9 %sources.1 = (f32[3,5,272,128]{3,2,1,0:T(8,128)S(1)}, f32[3,5,272,128]{3,2,1,0:T(8,128)}) custom-call(s32[3,32,128]{2,1,0:T(8,128)S(1)} %bitcast.26, f32[32,128]{1,0:T(8,128)S(1)} %bitcast.27, s32[2]{0:T(128)S(1)} %pad_add_fusion.place_ref), custom_call_target="tpu_custom_call" | custom-call | flops 3000000000 | bytes 3000000 | tf_op jit(solution)/shard_map/sources/pallas_call | solution.py:315
  20.9 0.0 collective-permute-done.3.from_right
  20.9 0.0 collective-permute-done.2.from_left
  20.9 0.0 copy-done.1
  20.9 11.1 %yee_face.1 = bf16[16,256,256]{2,1,0:T(8,128)(2,1)} custom-call(f32[3,3,256,512]{3,2,1,0:T(8,128)} %e_in.3, f32[3,3,256,512]{3,2,1,0:T(8,128)} %h_in.3, f32[3,256,512]{2,1,0:T(8,128)S(1)} %scales.1.s_lo.s_hi.scale_in, f32[3,5,272,128]{3,2,1,0:T(8,128)S(1)} %get-tuple-element.21.grid_in, f32[136,128]{1,0:T(8,128)S(1)} %collective-permute-done.2.from_left, ...), custom_call_target="tpu_custom_call" | custom-call | flops 5000000000 | bytes 40000000 | tf_op jit(solution)/shard_map/yee_face/pallas_call | solution.py:599
  32.0 8.1 %all-to-all-start = ((bf16[16,256,256]{2,1,0:T(8,128)(2,1)}), bf16[16,256,256]{2,1,0:T(8,128)(2,1)S(1)}, u32[]{:S(2)}, u32[]{:S(2)}) async-start(bf16[16,256,256]{2,1,0:T(8,128)(2,1)} %yee_face.1), calls=%async_computation | async-start | bytes 4194304 | tf_op jit(solution)/shard_map/all_to_all | solution.py:772
  40.1 0.0 copy-start.2
  40.1 1.4 %copy-done.2 = f32[3,256,512]{2,1,0:T(8,128)S(1)} copy-done((f32[3,256,512]{2,1,0:T(8,128)S(1)}, f32[3,256,512]{2,1,0:T(8,128)}, u32[]{:S(2)}) %copy-start.2) | copy-done | bytes 1572888
  41.5 14.9 %yee_fields.1 = (f32[3,3,256,512]{3,2,1,0:T(8,128)}, f32[3,3,256,512]{3,2,1,0:T(8,128)}) custom-call(f32[3,3,256,512]{3,2,1,0:T(8,128)} %e_in.3, f32[3,3,256,512]{3,2,1,0:T(8,128)} %h_in.3, f32[3,256,512]{2,1,0:T(8,128)S(1)} %copy-done.2, f32[3,5,272,128]{3,2,1,0:T(8,128)} %get-tuple-element.23.grid_in, f32[136,128]{1,0:T(8,128)S(1)} %collective-permute-done.2.from_left, ...), custom_call_target="tpu_custom_call" | custom-call | flops 5000000000 | bytes 40000000 | tf_op jit(solution)/shard_map/yee_fields/pallas_call | solution.py:599
  56.4 12.5 %all-to-all-done = bf16[16,256,256]{2,1,0:T(8,128)(2,1)S(1)} async-done(((bf16[16,256,256]{2,1,0:T(8,128)(2,1)}), bf16[16,256,256]{2,1,0:T(8,128)(2,1)S(1)}, u32[]{:S(2)}, u32[]{:S(2)}) %all-to-all-start) | async-done | bytes 2097184 | tf_op jit(solution)/shard_map/all_to_all | solution.py:772
  68.9 0.0 copy-start.3
  68.9 0.0 copy-start.4
  68.9 5.3 %rows_transform.1 = bf16[1280,256]{1,0:T(8,128)(2,1)S(1)} custom-call(bf16[4096,256]{1,0:T(8,128)(2,1)S(1)} %bitcast.22, bf16[1280,4096]{1,0:T(8,128)(2,1)} %constant.27.clone.table_in), custom_call_target="tpu_custom_call" | custom-call | tf_op jit(solution)/shard_map/rows_transform/pallas_call | solution.py:632
  74.1 0.0 copy-start.8
  74.1 24.4 %all_to_all.15 = bf16[16,80,256]{2,1,0:T(8,128)(2,1)S(1)} all-to-all(bf16[16,80,256]{2,1,0:T(8,128)(2,1)S(1)} %bitcast.23), channel_id=1, replica_groups=mesh['ga'=8,'gc'=2,'gy'=8] {'gc','gy'}, dimensions={0} | all-to-all | bytes 1310720 | tf_op jit(solution)/shard_map/all_to_all | solution.py:775
  98.5 0.0 copy-done.3
  98.5 0.0 copy-done.4
  98.5 3.2 %columns.1 = bf16[1024,128]{1,0:T(8,128)(2,1)} custom-call(bf16[1280,256]{1,0:T(8,128)(2,1)S(1)} %bitcast.24, bf16[8,256,256]{2,1,0:T(8,128)(2,1)S(1)} %copy-done.3, f32[8,32,128]{2,1,0:T(8,128)S(1)} %copy-done.4), custom_call_target="tpu_custom_call" | custom-call | tf_op jit(solution)/shard_map/columns/pallas_call | solution.py:685
  101.7 6.7 %all-to-all-start.2 = ((bf16[128,8,128]{2,1,0:T(8,128)(2,1)}), bf16[128,8,128]{2,1,0:T(8,128)(2,1)S(1)}, u32[]{:S(2)}, u32[]{:S(2)}) async-start(bf16[128,8,128]{2,1,0:T(8,128)(2,1)} %bitcast.28), calls=%async_computation.2 | async-start | bytes 524288 | tf_op jit(solution)/shard_map/all_to_all | solution.py:777
  108.4 0.0 copy-done.8
  108.5 0.1 multiply_bitcast_fusion.3
  108.5 0.1 copy.13
  108.6 0.1 copy.14
  108.7 0.1 copy.15
  108.8 0.1 copy.16
  108.9 0.1 maximum_multiply_fusion.coef_ref
  109.0 10.1 %all-to-all-done.2 = bf16[128,8,128]{2,1,0:T(8,128)(2,1)S(1)} async-done(((bf16[128,8,128]{2,1,0:T(8,128)(2,1)}), bf16[128,8,128]{2,1,0:T(8,128)(2,1)S(1)}, u32[]{:S(2)}, u32[]{:S(2)}) %all-to-all-start.2) | async-done | bytes 262176 | tf_op jit(solution)/shard_map/all_to_all | solution.py:777
  119.1 1.7 %combine.1 = f32[16,64,128]{2,1,0:T(8,128)} custom-call(bf16[64,16,128]{2,1,0:T(8,128)(2,1)S(1)} %bitcast.25, f32[2,4]{1,0:T(2,128)S(1)} %maximum_multiply_fusion.coef_ref, s32[2]{0:T(128)S(1)} %pad_add_fusion.place_ref), custom_call_target="tpu_custom_call" | custom-call | tf_op jit(solution)/shard_map/combine/pallas_call | solution.py:736
  (1 shorter events, 0.0 us)
Async XLA Ops:
  0.6 4.0 %copy-start = (s32[3,256,512]{2,1,0:T(8,128)S(1)}, s32[3,256,512]{2,1,0:T(8,128)}, u32[]{:S(2)}) copy-start(s32[3,256,512]{2,1,0:T(8,128)} %m_hi.1) | copy-start | bytes 4718596
  0.6 4.0 %copy-start.5 = (f32[8]{0:T(128)S(1)}, f32[8]{0:T(128)}, u32[]{:S(2)}) copy-start(f32[8]{0:T(128)} %eps_ref.3) | copy-start | bytes 100
  2.0 8.4 %collective-permute-start = (f32[48,512]{1,0:T(8,128)S(1)}, f32[48,512]{1,0:T(8,128)S(1)}, u32[]{:S(2)}, u32[]{:S(2)}) collective-permute-start(f32[48,512]{1,0:T(8,128)S(1)} %get-tuple-element.16), channel_id=1, source_target_pairs={{0,8},{8,16},{16,24},{24,32},{32,40},{40,48},{48,56},{56,64},{64,7... | collective-permute-start | bytes 294920 | tf_op jit(solution)/shard_map/ppermute | solution.py:751
  3.3 7.1 %collective-permute-start.1 = (f32[48,512]{1,0:T(8,128)S(1)}, f32[48,512]{1,0:T(8,128)S(1)}, u32[]{:S(2)}, u32[]{:S(2)}) collective-permute-start(f32[48,512]{1,0:T(8,128)S(1)} %get-tuple-element.17), channel_id=1, source_target_pairs={{8,0},{16,8},{24,16},{32,24},{40,32},{48,40},{56,48},{64,56},{72,6... | collective-permute-start | bytes 294920 | tf_op jit(solution)/shard_map/ppermute | solution.py:752
  6.1 14.8 %copy-start.1 = (f32[3,256,512]{2,1,0:T(8,128)}, f32[3,256,512]{2,1,0:T(8,128)S(1)}, u32[]{:S(2)}) copy-start(f32[3,256,512]{2,1,0:T(8,128)S(1)} %scales.1.s_lo.s_hi.scale_in) | copy-start | bytes 4718596
  6.1 4.3 %copy-start.7 = (s32[4096,3]{0,1:T(4,128)S(1)}, s32[4096,3]{0,1:T(4,128)}, u32[]{:S(2)}) copy-start(s32[4096,3]{0,1:T(4,128)} %param.14) | copy-start | bytes 147460
  6.1 10.8 %copy-start.6 = (f32[4096]{0:T(1024)S(1)}, f32[4096]{0:T(1024)}, u32[]{:S(2)}) copy-start(f32[4096]{0:T(1024)} %param.15) | copy-start | bytes 49156
  10.6 10.2 %collective-permute-start.3 = (f32[136,128]{1,0:T(8,128)S(1)}, f32[136,128]{1,0:T(8,128)S(1)}, u32[]{:S(2)}, u32[]{:S(2)}) collective-permute-start(f32[136,128]{1,0:T(8,128)S(1)} %get-tuple-element.18), channel_id=1, source_target_pairs={{1,0},{2,1},{3,2},{4,3},{5,4},{6,5},{7,6},{9,8},{10,9},{11,10},{12... | collective-permute-start | bytes 208904 | tf_op jit(solution)/shard_map/ppermute | solution.py:757
  11.9 8.9 %collective-permute-start.2 = (f32[136,128]{1,0:T(8,128)S(1)}, f32[136,128]{1,0:T(8,128)S(1)}, u32[]{:S(2)}, u32[]{:S(2)}) collective-permute-start(f32[136,128]{1,0:T(8,128)S(1)} %get-tuple-element.22), channel_id=1, source_target_pairs={{0,1},{1,2},{2,3},{3,4},{4,5},{5,6},{6,7},{8,9},{9,10},{10,11},{11... | collective-permute-start | bytes 208904 | tf_op jit(solution)/shard_map/ppermute | solution.py:756
  32.0 36.9 %all-to-all-start = ((bf16[16,256,256]{2,1,0:T(8,128)(2,1)}), bf16[16,256,256]{2,1,0:T(8,128)(2,1)S(1)}, u32[]{:S(2)}, u32[]{:S(2)}) async-start(bf16[16,256,256]{2,1,0:T(8,128)(2,1)} %yee_face.1), calls=%async_computation | async-start | bytes 4194304 | tf_op jit(solution)/shard_map/all_to_all | solution.py:772
  40.1 1.4 %copy-start.2 = (f32[3,256,512]{2,1,0:T(8,128)S(1)}, f32[3,256,512]{2,1,0:T(8,128)}, u32[]{:S(2)}) copy-start(f32[3,256,512]{2,1,0:T(8,128)} %copy-done.1) | copy-start | bytes 4718596
  68.9 29.6 %copy-start.3 = (bf16[8,256,256]{2,1,0:T(8,128)(2,1)S(1)}, bf16[8,256,256]{2,1,0:T(8,128)(2,1)}, u32[]{:S(2)}) copy-start(bf16[8,256,256]{2,1,0:T(8,128)(2,1)} %constant.28.clone.table_ref) | copy-start | bytes 3145732
  68.9 29.6 %copy-start.4 = (f32[8,32,128]{2,1,0:T(8,128)S(1)}, f32[8,32,128]{2,1,0:T(8,128)}, u32[]{:S(2)}) copy-start(f32[8,32,128]{2,1,0:T(8,128)} %constant.29.clone.phase_ref) | copy-start | bytes 393220
  74.1 34.3 %copy-start.8 = (f32[2]{0:T(128)S(1)}, f32[2]{0:T(128)}, u32[]{:S(2)}) copy-start(f32[2]{0:T(128)} %param.16) | copy-start | bytes 28
  101.7 17.4 %all-to-all-start.2 = ((bf16[128,8,128]{2,1,0:T(8,128)(2,1)}), bf16[128,8,128]{2,1,0:T(8,128)(2,1)S(1)}, u32[]{:S(2)}, u32[]{:S(2)}) async-start(bf16[128,8,128]{2,1,0:T(8,128)(2,1)} %bitcast.28), calls=%async_computation.2 | async-start | bytes 524288 | tf_op jit(solution)/shard_map/all_to_all | solution.py:777
